TPU v7x, 32 devices: a whole 2x2x4 slice. The times are simulated.
32 devices in a mesh: dp: 16 (over z, y, core), tensor: 2 (over x).
Axes of the slice: x: 2, y: 2, z: 4, core: 2. Of those that a mesh axis runs over, the one named last changes fastest.
Arguments:
- tokens: bfloat16 [1, 16384, 1024], P(None, 'dp', 'tensor'), may hold values from -6 to 6
- cotangent: bfloat16 [1, 16384, 1024], P(None, 'dp', 'tensor'), may hold values from -6 to 6
- segments: int32 [1, 16384], P(None, 'dp'), may hold values from 0 to 7, as said below
- owners: int32 [6], replicated, may hold values from 0 to 3, as said below
- attn_master: float32 [2, 4096, 1024], P(None, 'dp', 'tensor')
- attn_first: float32 [2, 4096, 1024], P(None, 'dp', 'tensor')
- attn_second: float32 [2, 4096, 1024], P(None, 'dp', 'tensor'), as said below
- mlp_master: float32 [1, 4096, 4096], P(None, 'dp', 'tensor')
- mlp_first: float32 [1, 4096, 4096], P(None, 'dp', 'tensor')
- mlp_second: float32 [1, 4096, 4096], P(None, 'dp', 'tensor'), as said below
- ssm_params: float32 [3, 1024, 16], P(None, 'tensor'), as said below
- ssm_first: float32 [3, 1024, 16], P(None, 'tensor')
- ssm_second: float32 [3, 1024, 16], P(None, 'tensor'), as said below
- norm_gains: float32 [2, 1024], P(None, 'tensor'), may hold values from 0.5 to 1.5
- gains_first: float32 [2, 1024], P(None, 'tensor')
- gains_second: float32 [2, 1024], P(None, 'tensor'), as said below
Outputs:
- block_out: bfloat16 [1, 16384, 1024], P(None, 'dp', 'tensor')
- grad_tokens: float32 [1, 16384, 1024], P(None, 'dp', 'tensor')
- attn_grad: float32 [2, 4096, 1024], P(None, 'dp', 'tensor')
- attn_first_new: float32 [2, 4096, 1024], P(None, 'dp', 'tensor')
- attn_second_new: float32 [2, 4096, 1024], P(None, 'dp', 'tensor')
- attn_new: float32 [2, 4096, 1024], P(None, 'dp', 'tensor')
- attn_new_low: bfloat16 [2, 4096, 1024], P(None, 'dp', 'tensor')
- mlp_grad: float32 [1, 4096, 4096], P(None, 'dp', 'tensor')
- mlp_first_new: float32 [1, 4096, 4096], P(None, 'dp', 'tensor')
- mlp_second_new: float32 [1, 4096, 4096], P(None, 'dp', 'tensor')
- mlp_new: float32 [1, 4096, 4096], P(None, 'dp', 'tensor')
- mlp_new_low: bfloat16 [1, 4096, 4096], P(None, 'dp', 'tensor')
- ssm_grad: float32 [3, 1024, 16], P(None, 'tensor')
- ssm_first_new: float32 [3, 1024, 16], P(None, 'tensor')
- ssm_second_new: float32 [3, 1024, 16], P(None, 'tensor')
- ssm_new: float32 [3, 1024, 16], P(None, 'tensor')
- gains_grad: float32 [2, 1024], P(None, 'tensor')
- gains_first_new: float32 [2, 1024], P(None, 'tensor')
- gains_second_new: float32 [2, 1024], P(None, 'tensor')
- gains_new: float32 [2, 1024], P(None, 'tensor')
Inputs may be any that keep to these rules, and one draw needn't show every extreme that they name: `segments`: in each row ids start at 0, never fall, and each row holds exactly 8 documents. No group owns more than 2 of the first four matrices, and one group owns exactly that many; no group owns more than 1 of the last two, so these two have different owners. `attn_second`: positive. `mlp_second`: positive. `ssm_params`: the first row lies between -log(512) / 2 and log(512) / 2. `ssm_second`: positive. `gains_second`: positive.
All inputs are finite; a program needn't handle non-finite values.
Results may differ from a plain program's by a relative error of at most 0.012.
Values may be sent and summed in bfloat16 or wider, within the bound.
No kernel may reach another device: no remote copies, remote signals or barrier semaphores. Data moves between devices by JAX's collectives and lax.ppermute only.
A program may use at most 448 MiB of HBM per device.

v0:
```python
import jax
import jax.numpy as jnp
from jax import lax
from jax.sharding import PartitionSpec as P

D = 1024
HEAD_DIM = 128
FF = 4096
CTX = 128
BL = 512
OWNER_GROUPS = 4
STEP = 5


epsilon_norm = 1e-05
beta_first = 0.9
beta_second = 0.95
epsilon_adam = 1e-08
matrix_decay = 0.1
masked_score = -1e30
highest = lax.Precision.HIGHEST


def from_behind(array, axis, by):
    devices = lax.axis_size(axis)
    pairs = [(i, i + by) for i in range(devices) if 0 <= i + by < devices]
    return lax.ppermute(array, axis, pairs)


def entering(array, axis, combine, identity):
    devices, position = (lax.axis_size(axis), lax.axis_index(axis))
    everything = jax.tree.map(
        lambda part, kind: lax.all_gather(part.astype(kind), axis),
        array,
        (jnp.bfloat16, jnp.bfloat16),
    )
    start = jax.tree.map(
        lambda part, zero: jnp.broadcast_to(jnp.asarray(zero, part.dtype), part.shape),
        array,
        identity,
    )

    def turn(k, before):
        reached = k < position
        new = combine(
            before, jax.tree.map(lambda part, own: part[k].astype(own.dtype), everything, array)
        )
        return jax.tree.map(lambda a, b: jnp.where(reached, a, b), new, before)

    return lax.fori_loop(0, devices, turn, start)


def entering_2(array, axis, combine, identity):
    devices, position = (lax.axis_size(axis), lax.axis_index(axis))
    everything = jax.tree.map(
        lambda part, kind: lax.all_gather(part.astype(kind), axis),
        array,
        jax.tree.map(lambda a: jnp.bfloat16 if a.dtype == jnp.float32 else a.dtype, array),
    )
    start = jax.tree.map(
        lambda part, zero: jnp.broadcast_to(jnp.asarray(zero, part.dtype), part.shape),
        array,
        identity,
    )

    def turn(k, before):
        at = devices - 1 - k
        reached = at > position
        new = combine(
            before, jax.tree.map(lambda part, own: part[at].astype(own.dtype), everything, array)
        )
        return jax.tree.map(lambda a, b: jnp.where(reached, a, b), new, before)

    return lax.fori_loop(0, devices, turn, start)


def row_total(values):
    return lax.psum(values, "tensor")


def full_rows(values):
    return lax.all_gather(values, "tensor", axis=1, tiled=True)


def reduce_partial(values):
    return lax.psum_scatter(values, "tensor", scatter_dimension=1, tiled=True)


def contract_rows(left, right):
    return lax.dot_general(
        left, right, (((0,), (0,)), ((), ())), preferred_element_type=jnp.float32
    )


def contract_cols(left, right):
    return lax.dot_general(
        left, right, (((1,), (1,)), ((), ())), preferred_element_type=jnp.float32
    )


def activation(values):
    return jax.nn.gelu(values, approximate=True)


def rate_column(rate_list, rank):
    return jnp.asarray(rate_list, jnp.float32).reshape((-1,) + (1,) * (rank - 1))


def slot_numbers(owner_part):
    count = owner_part.shape[0]
    order = jnp.arange(count, dtype=jnp.int32)
    earlier = (order[None, :] < order[:, None]).astype(jnp.int32)
    same = (owner_part[:, None] == owner_part[None, :]).astype(jnp.int32)
    return jnp.sum(same * earlier, axis=1)


def slot_rates(owner_part, rate_list, slot_count, fallback):
    slots = slot_numbers(owner_part)
    slot_hit = slots[:, None, None] == jnp.arange(slot_count, dtype=jnp.int32)[None, :, None]
    group_hit = (
        owner_part[:, None, None] == jnp.arange(OWNER_GROUPS, dtype=jnp.int32)[None, None, :]
    )
    hits = jnp.logical_and(slot_hit, group_hit).astype(jnp.float32)
    rates = jnp.asarray(rate_list, jnp.float32)[:, None, None]
    return jnp.sum(hits * rates, axis=0) + (1.0 - jnp.sum(hits, axis=0)) * fallback


def pick_matrix(bank, slot, owner):
    return lax.dynamic_slice(bank, (slot, owner * D, jnp.int32(0)), (1, D, bank.shape[2]))[0]


def place_matrices(matrices, slots, owner_part, slot_count):
    bank = jnp.zeros((slot_count, OWNER_GROUPS * D, matrices.shape[2]), jnp.float32)
    for position in range(matrices.shape[0]):
        bank = lax.dynamic_update_slice(
            bank,
            matrices[position][None],
            (slots[position], owner_part[position] * D, jnp.int32(0)),
        )
    return bank


def adam_step(gradient, moment_one, moment_two, weight, step_count, rate_table, decay_weight):
    first_new = beta_first * moment_one + (1.0 - beta_first) * gradient
    second_new = beta_second * moment_two + (1.0 - beta_second) * gradient * gradient
    fixed_one = 1.0 - jnp.power(beta_first, step_count)
    fixed_two = 1.0 - jnp.power(beta_second, step_count)
    update = first_new / fixed_one / (jnp.sqrt(second_new / fixed_two) + epsilon_adam)
    return (first_new, second_new, weight - rate_table * (update + decay_weight * weight))


def norm_forward(values, gain_row):
    totals = row_total(jnp.sum(values * values, axis=1))
    inverse = lax.rsqrt(totals / D + epsilon_norm)
    scaled = values * inverse[:, None]
    return (full_rows((scaled * gain_row).astype(jnp.bfloat16)), scaled, inverse)


def norm_backward(grad_hidden, scaled, inverse, gain_row):
    weighted = grad_hidden * gain_row
    totals = row_total(jnp.sum(weighted * scaled, axis=1))
    grad_values = inverse[:, None] * (weighted - scaled * (totals / D)[:, None])
    return (grad_values, jnp.sum(grad_hidden * scaled, axis=0))


def ssm_terms(params):
    decay_rate = jnp.exp(params[0]) * (BL ** (-0.5) / 32.0)
    decay_step = jnp.exp(-decay_rate)
    drive_gain = jnp.sqrt(1.0 - decay_step * decay_step) * params[1]
    return (decay_rate, drive_gain, params[2])


def span_states(inputs, params, start_state, same_end, pass_flags):
    decay_rate, drive_gain, readout = ssm_terms(params)
    powers = (CTX - 1 - jnp.arange(CTX)).astype(jnp.float32)
    weights_end = jnp.exp(-decay_rate[None] * powers[:, None, None])
    full_decay = jnp.exp(-decay_rate * CTX)
    span_rows = inputs.reshape(-1, CTX, inputs.shape[1])

    def advance(carried, span_item):
        span_in, same_row, pass_flag = span_item
        weighted = weights_end * same_row[:, None, None]
        collected = jnp.einsum("jcn,jc->cn", weighted, span_in, precision=highest)
        return (full_decay * pass_flag * carried + drive_gain * collected, carried)

    return lax.scan(advance, start_state, (span_rows, same_end, pass_flags))


def ssm_totals(inputs, params, same_end, pass_flags):
    decay_rate = ssm_terms(params)[0]
    zero_state = jnp.zeros(params.shape[1:], jnp.float32)
    end_state, _ = span_states(inputs, params, zero_state, same_end, pass_flags)
    return (jnp.exp(-decay_rate * inputs.shape[0]) * jnp.prod(pass_flags), end_state)


def ssm_tails(inputs, params, carry_in, same_end, pass_flags, carry_ok, inner_same):
    decay_rate, drive_gain, readout = ssm_terms(params)
    _, befores = span_states(inputs, params, carry_in, same_end, pass_flags)
    block_count = carry_ok.shape[0]
    per_block = BL // CTX
    channels = inputs.shape[1]
    target_rows = inputs.reshape(block_count, per_block, CTX, channels)[:, per_block - 1]
    start_states = befores.reshape(block_count, per_block, channels, -1)[:, per_block - 1]
    offsets = jnp.arange(CTX).astype(jnp.float32)
    rising = jnp.exp(-decay_rate[None] * (offsets[:, None, None] + 1.0))
    carried_part = (
        jnp.einsum("icn,bcn->bic", rising, readout[None] * start_states, precision=highest)
        * carry_ok[:, :, None]
    )
    lifted = jnp.exp(decay_rate[None] * offsets[:, None, None])
    falling = jnp.exp(-decay_rate[None] * offsets[:, None, None])
    sources = lifted[None] * (drive_gain[None, None] * target_rows[..., None])
    summed = jnp.einsum("bij,bjcn->bicn", inner_same, sources, precision=highest)
    local_part = jnp.sum(summed * falling[None] * readout[None, None], axis=3)
    return carried_part + local_part


def carry_combine(earlier, latter):
    return (earlier[0] * latter[0], latter[0] * earlier[1] + latter[1])


def back_combine(earlier, latter):
    return (latter[0] * earlier[0], latter[1] + latter[0] * earlier[1])


def block_scores(query_block, key_rows, seg_block, ids_block):
    head_count = query_block.shape[1] // HEAD_DIM
    query_heads = query_block.reshape(BL, head_count, HEAD_DIM)
    key_heads = key_rows.reshape(-1, head_count, HEAD_DIM)
    scores = jnp.einsum(
        "ihd,jhd->hij", query_heads, key_heads, preferred_element_type=jnp.float32
    ) * HEAD_DIM ** (-0.5)
    positions = jnp.arange(BL)
    local_ok = jnp.logical_and(
        positions[None, :] <= positions[:, None], seg_block[None, :] == seg_block[:, None]
    )
    context_ok = ids_block[None, :] == seg_block[:, None] + 1
    allowed = jnp.concatenate([context_ok, local_ok], axis=1)
    return jnp.where(allowed[None], scores, masked_score)


def weighted_values(probs_low, value_rows):
    head_count = value_rows.shape[1] // HEAD_DIM
    value_heads = value_rows.reshape(-1, head_count, HEAD_DIM)
    mixed_rows = jnp.einsum(
        "hij,jhd->ihd", probs_low, value_heads, preferred_element_type=jnp.float32
    )
    return mixed_rows.reshape(BL, -1).astype(jnp.bfloat16)


def body(
    tokens,
    cotangent,
    segments,
    owners,
    attn_master,
    attn_first,
    attn_second,
    mlp_master,
    mlp_first,
    mlp_second,
    ssm_params,
    ssm_first,
    ssm_second,
    norm_gains,
    gains_first,
    gains_second,
):
    rows_here = tokens.shape[0]
    row_dev = tokens.shape[1]
    half_width = tokens.shape[2]
    row_count = rows_here * row_dev
    blocks_row = row_dev // BL
    block_count = rows_here * blocks_row
    per_block = BL // CTX
    head_count = half_width // HEAD_DIM
    score_scale = HEAD_DIM ** (-0.5)
    tensor_index = lax.axis_index("tensor")
    attn_owner = owners[:4]
    mlp_owner = owners[4:]
    attn_slots = slot_numbers(attn_owner)
    mlp_slots = slot_numbers(mlp_owner)
    low_attn = attn_master.astype(jnp.bfloat16)
    low_mlp = mlp_master.astype(jnp.bfloat16)
    attn_full, mlp_full = (
        lax.all_gather(low_attn, "dp", axis=1, tiled=True),
        lax.all_gather(low_mlp, "dp", axis=1, tiled=True),
    )
    weight_query = pick_matrix(attn_full, attn_slots[0], attn_owner[0])
    weight_key = pick_matrix(attn_full, attn_slots[1], attn_owner[1])
    weight_value = pick_matrix(attn_full, attn_slots[2], attn_owner[2])
    weight_out = pick_matrix(attn_full, attn_slots[3], attn_owner[3])
    weight_in = pick_matrix(mlp_full, mlp_slots[0], mlp_owner[0])
    weight_down = pick_matrix(mlp_full, mlp_slots[1], mlp_owner[1])
    prior_ids = from_behind(segments[:, row_dev - CTX :] + 1, "dp", 1)
    previous = jnp.concatenate([prior_ids[:, CTX - 1 :] - 1, segments[:, :-1]], axis=1)
    starts = segments != previous
    seg_spans = segments.reshape(rows_here, -1, CTX)
    start_spans = starts.reshape(rows_here, -1, CTX)
    same_end = (seg_spans == seg_spans[:, :, CTX - 1 :]).astype(jnp.float32)
    pass_flags = jnp.logical_and(
        jnp.logical_not(start_spans[:, :, 0]), seg_spans[:, :, 0] == seg_spans[:, :, CTX - 1]
    ).astype(jnp.float32)
    tail_ids = seg_spans.reshape(rows_here, blocks_row, per_block, CTX)[:, :, per_block - 1]
    tail_start = start_spans.reshape(rows_here, blocks_row, per_block, CTX)[:, :, per_block - 1, 0]
    carry_ok = jnp.logical_and(
        jnp.logical_not(tail_start)[..., None], tail_ids == tail_ids[..., :1]
    ).astype(jnp.float32)
    inner_order = jnp.arange(CTX)
    lower_part = inner_order[None, :] <= inner_order[:, None]
    inner_same = jnp.logical_and(
        lower_part[None, None], tail_ids[..., None, :] == tail_ids[..., :, None]
    ).astype(jnp.float32)

    def totals_fn(inputs, params):
        return jax.vmap(ssm_totals, in_axes=(0, None, 0, 0))(inputs, params, same_end, pass_flags)

    def tails_fn(inputs, params, carry_in):
        return jax.vmap(ssm_tails, in_axes=(0, None, 0, 0, 0, 0, 0))(
            inputs, params, carry_in, same_end, pass_flags, carry_ok, inner_same
        )

    flat_tokens = tokens.reshape(row_count, half_width).astype(jnp.float32)
    flat_cotangent = cotangent.reshape(row_count, half_width)
    hidden_one, scaled_one, inverse_one = norm_forward(flat_tokens, norm_gains[0])
    channels = (
        lax.dynamic_slice_in_dim(hidden_one, tensor_index * half_width, half_width, 1)
        .astype(jnp.float32)
        .reshape(rows_here, row_dev, half_width)
    )
    device_decay, end_state = totals_fn(channels, ssm_params)
    _, carry_in = entering(
        (device_decay, end_state),
        "dp",
        carry_combine,
        (jnp.ones_like(device_decay), jnp.zeros_like(end_state)),
    )
    tails_value = tails_fn(channels, ssm_params, carry_in).astype(jnp.bfloat16)
    handed = from_behind(tails_value[:, blocks_row - 1], "dp", 1)
    context_local = jnp.concatenate(
        [handed[:, None], tails_value[:, : blocks_row - 1]], axis=1
    ).reshape(block_count, CTX, half_width)
    context_full = lax.all_gather(context_local, "tensor", axis=2, tiled=True)
    context_flat = context_full.reshape(-1, D)
    context_ids = jnp.concatenate(
        [prior_ids[:, None], tail_ids[:, : blocks_row - 1] + 1], axis=1
    ).reshape(block_count, CTX)
    seg_blocks = segments.reshape(block_count, BL)
    queries = jnp.dot(hidden_one, weight_query, preferred_element_type=jnp.float32).astype(
        jnp.bfloat16
    )
    keys_tok = jnp.dot(hidden_one, weight_key, preferred_element_type=jnp.float32).astype(
        jnp.bfloat16
    )
    values_tok = jnp.dot(hidden_one, weight_value, preferred_element_type=jnp.float32).astype(
        jnp.bfloat16
    )
    context_keys = (
        jnp.dot(context_flat, weight_key, preferred_element_type=jnp.float32)
        .astype(jnp.bfloat16)
        .reshape(block_count, CTX, half_width)
    )
    context_values = (
        jnp.dot(context_flat, weight_value, preferred_element_type=jnp.float32)
        .astype(jnp.bfloat16)
        .reshape(block_count, CTX, half_width)
    )
    attn_inputs = (
        queries.reshape(block_count, BL, half_width),
        keys_tok.reshape(block_count, BL, half_width),
        values_tok.reshape(block_count, BL, half_width),
        context_keys,
        context_values,
        seg_blocks,
        context_ids,
    )

    def attend_forward(block_item):
        query_block, key_block, value_block, context_key, context_value, seg_block, ids_block = (
            block_item
        )
        scores = block_scores(
            query_block, jnp.concatenate([context_key, key_block], axis=0), seg_block, ids_block
        )
        row_top = jnp.max(scores, axis=2, keepdims=True)
        raised = jnp.exp(scores - row_top)
        totals = jnp.sum(raised, axis=2, keepdims=True)
        probs_low = (raised / totals).astype(jnp.bfloat16)
        mixed_rows = weighted_values(
            probs_low, jnp.concatenate([context_value, value_block], axis=0)
        )
        return (mixed_rows, (row_top + jnp.log(totals))[..., 0])

    attended, log_totals = lax.map(attend_forward, attn_inputs)
    attended_flat = attended.reshape(row_count, half_width)
    middle = flat_tokens + reduce_partial(contract_cols(attended_flat, weight_out))
    hidden_two, scaled_two, inverse_two = norm_forward(middle, norm_gains[1])
    pre_act = jnp.dot(hidden_two, weight_in, preferred_element_type=jnp.float32)
    act_value, act_pull = jax.vjp(activation, pre_act)
    act_low = act_value.astype(jnp.bfloat16)
    block_out = (middle + reduce_partial(contract_cols(act_low, weight_down))).astype(jnp.bfloat16)
    grad_out = full_rows(flat_cotangent)
    grad_down = contract_rows(grad_out, act_low)
    grad_act = jnp.dot(grad_out, weight_down, preferred_element_type=jnp.float32)
    grad_pre = act_pull(grad_act)[0].astype(jnp.bfloat16)
    grad_in = contract_rows(hidden_two, grad_pre)
    grad_hidden_two = reduce_partial(contract_cols(grad_pre, weight_in))
    grad_norm_two, gain_two = norm_backward(grad_hidden_two, scaled_two, inverse_two, norm_gains[1])
    grad_middle = flat_cotangent.astype(jnp.float32) + grad_norm_two
    mlp_grads = place_matrices(
        jnp.stack([grad_in, grad_down]), mlp_slots, mlp_owner, mlp_master.shape[0]
    )
    grad_mid_full = full_rows(grad_middle.astype(jnp.bfloat16))

    def attend_backward(block_item):
        (
            query_block,
            key_block,
            value_block,
            context_key,
            context_value,
            seg_block,
            ids_block,
            log_block,
            grad_rows,
        ) = block_item
        key_rows = jnp.concatenate([context_key, key_block], axis=0)
        value_rows = jnp.concatenate([context_value, value_block], axis=0)
        scores = block_scores(query_block, key_rows, seg_block, ids_block)
        probs_full = jnp.exp(scores - log_block[..., None])
        probs_low = probs_full.astype(jnp.bfloat16)
        mixed_rows = weighted_values(probs_low, value_rows)
        grad_mixed = jnp.dot(grad_rows, weight_out, preferred_element_type=jnp.float32).astype(
            jnp.bfloat16
        )
        grad_heads = grad_mixed.reshape(BL, head_count, HEAD_DIM)
        value_heads = value_rows.reshape(-1, head_count, HEAD_DIM)
        key_heads = key_rows.reshape(-1, head_count, HEAD_DIM)
        query_heads = query_block.reshape(BL, head_count, HEAD_DIM)
        grad_probs = jnp.einsum(
            "ihd,jhd->hij", grad_heads, value_heads, preferred_element_type=jnp.float32
        )
        centre = jnp.sum(probs_full * grad_probs, axis=2, keepdims=True)
        grad_scores = (probs_full * (grad_probs - centre)).astype(jnp.bfloat16)
        grad_query = (
            (
                jnp.einsum(
                    "hij,jhd->ihd", grad_scores, key_heads, preferred_element_type=jnp.float32
                )
                * score_scale
            )
            .astype(jnp.bfloat16)
            .reshape(BL, half_width)
        )
        grad_keys = (
            (
                jnp.einsum(
                    "hij,ihd->jhd", grad_scores, query_heads, preferred_element_type=jnp.float32
                )
                * score_scale
            )
            .astype(jnp.bfloat16)
            .reshape(-1, half_width)
        )
        grad_values = (
            jnp.einsum("hij,ihd->jhd", probs_low, grad_heads, preferred_element_type=jnp.float32)
            .astype(jnp.bfloat16)
            .reshape(-1, half_width)
        )
        return (
            mixed_rows,
            grad_query,
            grad_keys[CTX:],
            grad_values[CTX:],
            grad_keys[:CTX],
            grad_values[:CTX],
        )

    back_inputs = attn_inputs + (log_totals, grad_mid_full.reshape(block_count, BL, D))
    mixed_again, grad_query_all, grad_key_all, grad_value_all, grad_ctx_keys, grad_ctx_values = (
        lax.map(attend_backward, back_inputs)
    )
    mixed_flat = mixed_again.reshape(row_count, half_width)
    grad_query_flat = grad_query_all.reshape(row_count, half_width)
    grad_key_flat = grad_key_all.reshape(row_count, half_width)
    grad_value_flat = grad_value_all.reshape(row_count, half_width)
    grad_ctx_key_flat = grad_ctx_keys.reshape(-1, half_width)
    grad_ctx_value_flat = grad_ctx_values.reshape(-1, half_width)
    grad_out_weight = contract_rows(grad_mid_full, mixed_flat)
    grad_query_weight = contract_rows(hidden_one, grad_query_flat)
    grad_key_weight = contract_rows(hidden_one, grad_key_flat) + contract_rows(
        context_flat, grad_ctx_key_flat
    )
    grad_value_weight = contract_rows(hidden_one, grad_value_flat) + contract_rows(
        context_flat, grad_ctx_value_flat
    )
    partial_hidden = (
        contract_cols(grad_query_flat, weight_query)
        + contract_cols(grad_key_flat, weight_key)
        + contract_cols(grad_value_flat, weight_value)
    )
    partial_context = contract_cols(grad_ctx_key_flat, weight_key) + contract_cols(
        grad_ctx_value_flat, weight_value
    )
    reduced = reduce_partial(jnp.concatenate([partial_hidden, partial_context], axis=0))
    grad_hidden_one = reduced[:row_count]
    grad_context = reduced[row_count:].reshape(rows_here, blocks_row, CTX, half_width)
    handed_back = from_behind(grad_context[:, 0].astype(jnp.bfloat16), "dp", -1).astype(jnp.float32)
    grad_tails = jnp.concatenate([grad_context[:, 1:], handed_back[:, None]], axis=1)
    _, tails_pull = jax.vjp(tails_fn, channels, ssm_params, carry_in)
    grad_chan_one, grad_ssm_one, grad_carry = tails_pull(grad_tails)
    _, later_sum = entering_2(
        (device_decay, grad_carry),
        "dp",
        back_combine,
        (jnp.ones_like(device_decay), jnp.zeros_like(grad_carry)),
    )
    _, totals_pull = jax.vjp(totals_fn, channels, ssm_params)
    grad_chan_two, grad_ssm_two = totals_pull((later_sum * carry_in, later_sum))
    grad_hidden_one = grad_hidden_one + (grad_chan_one + grad_chan_two).reshape(
        row_count, half_width
    )
    grad_norm_one, gain_one = norm_backward(grad_hidden_one, scaled_one, inverse_one, norm_gains[0])
    grad_tokens = grad_middle + grad_norm_one
    attn_grads = place_matrices(
        jnp.stack([grad_query_weight, grad_key_weight, grad_value_weight, grad_out_weight]),
        attn_slots,
        attn_owner,
        attn_master.shape[0],
    )
    attn_reduced, mlp_reduced = (
        lax.psum_scatter(attn_grads, "dp", scatter_dimension=1, tiled=True),
        lax.psum_scatter(mlp_grads, "dp", scatter_dimension=1, tiled=True),
    )
    ssm_reduced, gains_reduced = lax.psum(
        (grad_ssm_one + grad_ssm_two, jnp.stack([gain_one, gain_two])), "dp"
    )
    group_index = lax.axis_index("dp") // (lax.axis_size("dp") // OWNER_GROUPS)
    step_count = jnp.float32(STEP)
    attn_table = slot_rates(
        attn_owner,
        [0.5 * D ** (-0.5)] * 3 + [0.5 * (D // 16) ** (-0.5)],
        attn_master.shape[0],
        0.5 * D ** (-0.5),
    )
    mlp_table = slot_rates(
        mlp_owner, [0.5 * D ** (-0.5), 0.5 * FF ** (-0.5)], mlp_master.shape[0], 0.5 * D ** (-0.5)
    )
    attn_rates = lax.dynamic_index_in_dim(attn_table, group_index, 1, keepdims=False)[:, None, None]
    mlp_rates = lax.dynamic_index_in_dim(mlp_table, group_index, 1, keepdims=False)[:, None, None]
    ssm_rates = rate_column([1.0, 0.8, 0.25], 3)
    gain_rates = rate_column([0.6, 0.6], 2)
    attn_one, attn_two, attn_new = adam_step(
        attn_reduced, attn_first, attn_second, attn_master, step_count, attn_rates, matrix_decay
    )
    mlp_one, mlp_two, mlp_new = adam_step(
        mlp_reduced, mlp_first, mlp_second, mlp_master, step_count, mlp_rates, matrix_decay
    )
    ssm_one, ssm_two, ssm_new = adam_step(
        ssm_reduced, ssm_first, ssm_second, ssm_params, step_count, ssm_rates, 0.0
    )
    gain_first_new, gain_second_new, gains_new = adam_step(
        gains_reduced, gains_first, gains_second, norm_gains, step_count, gain_rates, 0.0
    )
    block_rows = block_out.reshape(rows_here, row_dev, half_width)
    grad_rows_out = grad_tokens.reshape(rows_here, row_dev, half_width)
    return (
        block_rows,
        grad_rows_out,
        attn_reduced,
        attn_one,
        attn_two,
        attn_new,
        attn_new.astype(jnp.bfloat16),
        mlp_reduced,
        mlp_one,
        mlp_two,
        mlp_new,
        mlp_new.astype(jnp.bfloat16),
        ssm_reduced,
        ssm_one,
        ssm_two,
        ssm_new,
        gains_reduced,
        gain_first_new,
        gain_second_new,
        gains_new,
    )


def solution(mesh):
    in_specs = (
        P(None, "dp", "tensor"),
        P(None, "dp", "tensor"),
        P(None, "dp"),
        P(),
        P(None, "dp", "tensor"),
        P(None, "dp", "tensor"),
        P(None, "dp", "tensor"),
        P(None, "dp", "tensor"),
        P(None, "dp", "tensor"),
        P(None, "dp", "tensor"),
        P(None, "tensor", None),
        P(None, "tensor", None),
        P(None, "tensor", None),
        P(None, "tensor"),
        P(None, "tensor"),
        P(None, "tensor"),
    )
    out_specs = (
        P(None, "dp", "tensor"),
        P(None, "dp", "tensor"),
        P(None, "dp", "tensor"),
        P(None, "dp", "tensor"),
        P(None, "dp", "tensor"),
        P(None, "dp", "tensor"),
        P(None, "dp", "tensor"),
        P(None, "dp", "tensor"),
        P(None, "dp", "tensor"),
        P(None, "dp", "tensor"),
        P(None, "dp", "tensor"),
        P(None, "dp", "tensor"),
        P(None, "tensor", None),
        P(None, "tensor", None),
        P(None, "tensor", None),
        P(None, "tensor", None),
        P(None, "tensor"),
        P(None, "tensor"),
        P(None, "tensor"),
        P(None, "tensor"),
    )
    return jax.shard_map(body, mesh=mesh, in_specs=in_specs, out_specs=out_specs, check_vma=False)
```

profile of v0, /device:TPU:0, one launch (start us, length us, event | category | flops | bytes accessed | tf_op | source)
XLA Modules:
  0.0 1825.0 jit_solution(11754628169560126955)
XLA Ops:
  8.9 5.8 psum.42
  30.0 24.9 %all-gather = bf16[16,512,16]{1,2,0:T(8,128)(2,1)} all-gather(bf16[1,512,16]{1,2,0:T(8,128)(2,1)S(1)} %get-tuple-element.2960), channel_id=2, replica_groups=mesh['dp'=16,'tensor'=2] {'dp'}, dimensions={0}, use_global_device_ids=true | all-gather | bytes 278528 | tf_op jit(solution)/shard_map/all_gather | solution.py:33
  54.9 5.8 multiply_exponential_fusion.2
  60.7 5.4 copy.790
  66.1 5.3 copy.788
  73.6 30.1 %while.182 = (s32[]{:T(128)}, f32[1,512,16]{2,1,0:T(8,128)S(1)}, f32[8,1]{1,0:T(8,128)}, f32[512,16]{1,0:T(8,128)S(1)}, f32[8,1,128]{2,1,0:T(1,128)}, /*index=5*...) while((s32[]{:T(128)}, f32[1,512,16]{2,1,0:T(8,128)S(1)}, ...), condition=%wide.region_5.6_spmd.clone, body=%wide.region_4.5_spmd.clone.sunk | while | flops 4227075 | bytes 1083543 | solution.py:186
  103.8 19.1 %all-gather.1 = bf16[16,512,16]{1,2,0:T(8,128)(2,1)S(1)} all-gather(bf16[1,512,16]{1,2,0:T(8,128)(2,1)S(1)} %copy.774), channel_id=3, replica_groups=mesh['dp'=16,'tensor'=2] {'dp'}, dimensions={0}, use_global_device_ids=true | all-gather | bytes 278528 | tf_op jit(solution)/shard_map/all_gather | solution.py:33
  122.9 12.1 while.183
  135.1 35.7 %while.180 = (s32[]{:T(128)}, f32[1,512,16]{2,1,0:T(8,128)S(1)}, f32[8,1,512,16]{3,2,1,0:T(8,128)}, f32[8,1]{1,0:T(8,128)}, f32[512,16]{1,0:T(8,128)S(1)}, /*ind...) while((s32[]{:T(128)}, f32[1,512,16]{2,1,0:T(8,128)S(1)}, ...), condition=%wide.region_9.10_spmd.clone, body=%wide.region_8.9_spmd.clone.sunk | while | flops 4218882 | bytes 1378449 | solution.py:186
  172.8 11.6 multiply_reduce_fusion.6
  185.4 5.7 fusion.126
  206.9 9.8 all-gather.2
  216.7 4.3 convolution_convert_fusion.3
  223.2 4.1 convolution_convert_fusion.4
  229.6 4.1 convolution_convert_fusion.5
  242.0 29.2 %while.178 = (s32[]{:T(128)}, bf16[2,512,512]{2,1,0:T(8,128)(2,1)}, f32[2,4,512]{2,1,0:T(4,128)}, bf16[2,128,512]{1,2,0:T(8,128)(2,1)}, bf16[2,512,512]{1,2,0:T(...) while((s32[]{:T(128)}, bf16[2,512,512]{2,1,0:T(8,128)(2,1)}, ...), condition=%wide.region_14.15_spmd, body=%wide.region_11.14_spmd.sunk | while | flops 690878976 | bytes 29832904 | solution.py:394
  273.5 4.5 fusion.244
  278.1 52.1 %reduce-scatter.7.cloned.1.call-done = f32[1024,512]{1,0:T(8,128)} async-done(((f32[1024,1024]{1,0:T(8,128)}), f32[1024,512]{1,0:T(8,128)}) %reduce-scatter.7.cloned.1.call-update) | async-done | bytes 2097168 | tf_op jit(solution)/shard_map/reduce_scatter | solution.py:86
  333.4 4.9 psum.43
  346.2 28.2 %all-gather.16.cloned.1.call-done = bf16[1024,1024]{1,0:T(8,128)(2,1)} async-done(((bf16[1024,512]{1,0:T(8,128)(2,1)}), bf16[1024,1024]{1,0:T(8,128)(2,1)}) %all-gather.16.cloned.1.call-update) | async-done | bytes 2097168 | tf_op jit(solution)/shard_map/all_gather | solution.py:82
  374.4 129.8 %all-gather.18.cloned.1.call-done = bf16[1,4096,2048]{2,1,0:T(8,128)(2,1)} async-done(((bf16[1,256,2048]{2,1,0:T(8,128)(2,1)}), bf16[1,4096,2048]{2,1,0:T(8,128)(2,1)}) %all-gather.18.cloned.1.call-update) | async-done | bytes 16777232 | tf_op jit(solution)/shard_map/all_gather | solution.py:287
  504.2 10.6 fusion.88
  514.8 22.2 %all-gather.22.cloned.1.call-done = bf16[1,1024,1024]{2,1,0:T(8,128)(2,1)} async-done(((bf16[1,1024,512]{2,1,0:T(8,128)(2,1)}), bf16[1,1024,1024]{2,1,0:T(8,128)(2,1)}) %all-gather.22.cloned.1.call-update) | async-done | bytes 2097168 | tf_op jit(solution)/shard_map/all_gather | solution.py:82
  537.0 12.4 fusion.71
  551.4 8.5 fusion.86
  560.1 54.3 %reduce-scatter.11.cloned.1.call-done = f32[1024,512]{1,0:T(8,128)} async-done(((f32[1024,1024]{1,0:T(8,128)}), f32[1024,512]{1,0:T(8,128)}) %reduce-scatter.11.cloned.1.call-update) | async-done | bytes 2097168 | tf_op jit(solution)/shard_map/reduce_scatter | solution.py:86
  617.8 4.9 psum.44
  626.9 11.8 broadcast.642.clone
  638.7 65.5 %while.181 = (s32[]{:T(128)}, f32[1,512,16]{1,2,0:T(8,128)S(1)}, f32[8,1,512,16]{2,3,1,0:T(8,128)S(1)}, f32[8,1,128,1,1]{2,4,3,1,0:T(1,128)S(1)}, f32[8,1,128,51...) while((s32[]{:T(128)}, f32[1,512,16]{1,2,0:T(8,128)S(1)}, ...), condition=%wide.region_28.29_spmd.clone, body=%wide.region_27.28_spmd.clone.sunk | while | flops 6324226 | bytes 5443805 | solution.py:186
  709.7 67.0 %while.179 = (s32[]{:T(128)}, bf16[2,512,512]{2,1,0:T(8,128)(2,1)}, bf16[2,512,512]{2,1,0:T(8,128)(2,1)}, bf16[2,512,512]{2,1,0:T(8,128)(2,1)}, bf16[2,512,512]{...) while((s32[]{:T(128)}, bf16[2,512,512]{2,1,0:T(8,128)(2,1)}, ...), condition=%wide.region_24.25_spmd, body=%wide.region_22.24_spmd.sunk | while | flops 2583493120 | bytes 118372328 | solution.py:481
  723.1 4.2 fusion.338
  729.6 5.1 multiply_reduce_fusion.17
  756.5 4.2 fusion.338
  763.0 5.1 multiply_reduce_fusion.17
  793.7 11.6 broadcast.642.clone.1
  805.3 73.2 %while.186 = (s32[]{:T(128)}, f32[1,512,16]{1,2,0:T(8,128)S(1)}, f32[8,1,512,16]{2,3,1,0:T(8,128)S(1)}, f32[8,1,128,1,1]{2,4,3,1,0:T(1,128)S(1)}, f32[8,1,128,51...) while((s32[]{:T(128)}, f32[1,512,16]{1,2,0:T(8,128)S(1)}, ...), condition=%wide.region_34.35_spmd.clone, body=%wide.region_33.34_spmd.clone.sunk | while | flops 6340611 | bytes 5443816 | solution.py:186
  879.9 11.8 fusion.84
  895.8 8.0 broadcast_in_dim.168
  917.8 9.8 fusion.82
  927.6 7.9 fusion.158
  935.7 13.5 multiply_reduce_fusion.3
  949.2 6.9 multiply_reduce_fusion.4
  956.1 5.4 copy.835
  961.6 5.5 copy.837
  967.8 88.9 %while.184 = (s32[]{:T(128)}, f32[128,512,16]{1,2,0:T(8,128)}, f32[512,16]{0,1:T(8,128)S(1)}, f32[512,16]{0,1:T(8,128)S(1)}, f32[1,512,16]{1,2,0:T(8,128)S(1)}, ...) while((s32[]{:T(128)}, f32[128,512,16]{1,2,0:T(8,128)}, ...), condition=%wide.region_30.31_spmd.clone, body=%wide.region_29.30_spmd.clone.sunk | while | flops 6324228 | bytes 48205084 | solution.py:186
  1056.8 22.7 %all-gather.4 = bf16[16,512,16]{1,2,0:T(8,128)(2,1)S(1)} all-gather(bf16[1,512,16]{1,2,0:T(8,128)(2,1)S(1)} %convert_element_type.363), channel_id=6, replica_groups=mesh['dp'=16,'tensor'=2] {'dp'}, dimensions={0}, use_global_device_ids=true | all-gather | bytes 278528 | tf_op jit(solution)/shard_map/all_gather | solution.py:56
  1079.4 12.1 while.185
  1091.6 5.9 copy.831
  1097.8 84.1 %while.187 = (s32[]{:T(128)}, f32[128,512,16]{1,2,0:T(8,128)}, f32[512,16]{0,1:T(8,128)S(1)}, f32[512,16]{0,1:T(8,128)S(1)}, f32[1,512,16]{1,2,0:T(8,128)S(1)}, ...) while((s32[]{:T(128)}, f32[128,512,16]{1,2,0:T(8,128)}, ...), condition=%wide.region_36.37_spmd.clone, body=%wide.region_35.36_spmd.clone.sunk | while | flops 6299652 | bytes 48170776 | solution.py:186
  1181.9 6.6 copy.840
  1188.5 12.5 multiply_reduce_fusion.10
  1206.2 4.5 bitcast_dynamic-update-slice_fusion.11
  1212.3 12.6 convolution_bitcast_fusion
  1224.9 9.1 copy.830
  1234.0 12.4 broadcast_in_dim.169
  1246.4 6.9 bitcast_dynamic-update-slice_fusion.10
  1259.5 5.1 fusion.113
  1264.7 29.9 %psum.47 = f32[2,512]{1,0:T(2,128)S(1)} all-reduce(f32[2,512]{1,0:T(2,128)S(1)} %pad_maximum_fusion.8), channel_id=1, replica_groups=mesh['dp'=16,'tensor'=2] {'dp'}, use_global_device_ids=true, to_apply=%region_59.60 | all-reduce | flops 1024 | bytes 8192 | tf_op jit(solution)/shard_map/psum | solution.py:535
  1294.5 5.1 psum.45
  1300.3 6.6 fusion.112
  1308.8 163.6 %reduce-scatter.15.cloned.1.call-done = f32[2,256,512]{2,1,0:T(8,128)} async-done(((f32[2,4096,512]{2,1,0:T(8,128)}), f32[2,256,512]{2,1,0:T(8,128)}) %reduce-scatter.15.cloned.1.call-update) | async-done | bytes 1048592 | tf_op jit(solution)/shard_map/reduce_scatter | solution.py:532
  1472.5 4.6 fusion.234
  1477.0 332.6 %reduce-scatter.17.cloned.1.call-done = f32[1,256,2048]{2,1,0:T(8,128)} async-done(((f32[1,4096,2048]{2,1,0:T(8,128)}), f32[1,256,2048]{2,1,0:T(8,128)}) %reduce-scatter.17.cloned.1.call-update) | async-done | bytes 2097168 | tf_op jit(solution)/shard_map/reduce_scatter | solution.py:533
  1809.7 7.9 fusion.232
  (1033 shorter events, 595.9 us)
Async XLA Ops:
  7.2 10.9 copy-start.71
  7.2 12.2 copy-start.29
  7.2 14.9 copy-start.87
  7.2 17.1 copy-start.45
  7.2 64.8 %all-gather.12.cloned.1.call-start = ((), (), s32[]{:S(2)}) async-start(), calls=%async_computation.6 | async-start | bytes 3145728 | tf_op jit(solution)/shard_map/all_gather | solution.py:82
  14.7 14.2 copy-start.77
  15.5 13.5 copy-start.85
  15.5 607.2 %copy-start.79 = (f32[1,512]{1,0:T(1,128)}, f32[1,512]{1,0:T(1,128)S(1)}, u32[]{:S(2)}) copy-start(f32[1,512]{1,0:T(1,128)S(1)} %get-tuple-element.2964) | copy-start | bytes 6148
  18.0 198.7 %all-gather.14.cloned.1.call-start = ((), (), s32[]{:S(2)}) async-start(), calls=%async_computation.7 | async-start | bytes 8912896 | tf_op jit(solution)/shard_map/all_gather | solution.py:286
  18.1 6.6 collective-permute-start
  20.3 309.9 %reduce-scatter.7.cloned.1.call-start = ((), (), s32[]{:S(2)}) async-start(), calls=%async_computation.8 | async-start | bytes 6291456 | tf_op jit(solution)/shard_map/reduce_scatter | solution.py:86
  20.9 39.8 %copy-start.97 = (f32[128]{0:T(128)}, f32[128]{0:T(128)S(1)}, u32[]{:S(2)}) copy-start(f32[128]{0:T(128)S(1)} %iota_convert_fusion) | copy-start | bytes 1540
  20.9 151.9 %copy-start.83 = (s32[1,2,1,128]{3,2,1,0:T(1,128)}, s32[1,2,1,128]{3,2,1,0:T(1,128)S(1)}, u32[]{:S(2)}) copy-start(s32[1,2,1,128]{3,2,1,0:T(1,128)S(1)} %slice.204) | copy-start | bytes 3076
  28.8 143.9 %copy-start.55 = (f32[512,16]{0,1:T(8,128)}, f32[512,16]{0,1:T(8,128)S(1)}, u32[]{:S(2)}) copy-start(f32[512,16]{0,1:T(8,128)S(1)} %get-tuple-element.2961) | copy-start | bytes 98308
  29.0 31.7 %copy-start.36 = (f32[512,16]{1,0:T(8,128)}, f32[512,16]{1,0:T(8,128)S(1)}, u32[]{:S(2)}) copy-start(f32[512,16]{1,0:T(8,128)S(1)} %copy.787) | copy-start | bytes 98308
  29.1 156.3 %copy-start.38 = (f32[512,16]{1,0:T(8,128)}, f32[512,16]{1,0:T(8,128)S(1)}, u32[]{:S(2)}) copy-start(f32[512,16]{1,0:T(8,128)S(1)} %copy.785) | copy-start | bytes 98308
  135.0 425.1 %copy-start.42 = (f32[1,512,16]{1,2,0:T(8,128)}, f32[1,512,16]{1,2,0:T(8,128)S(1)}, u32[]{:S(2)}) copy-start(f32[1,512,16]{1,2,0:T(8,128)S(1)} %get-tuple-element.3789) | copy-start | bytes 98308
  170.8 13.6 copy-start.26
  172.8 11.6 copy-start.40
  172.8 12.6 copy-start.99
  172.8 12.6 copy-start.114
  184.4 9.5 copy-start.92
  184.4 21.7 %copy-start.106 = (s32[1,128]{1,0:T(1,128)S(1)}, s32[1,128]{1,0:T(1,128)}, u32[]{:S(2)}) copy-start(s32[1,128]{1,0:T(1,128)} %copy-done.105) | copy-start | bytes 1540
  184.4 21.7 %copy-start.107 = (s32[1,1,128]{2,1,0:T(1,128)S(1)}, s32[1,1,128]{2,1,0:T(1,128)}, u32[]{:S(2)}) copy-start(s32[1,1,128]{2,1,0:T(1,128)} %slice_add_fusion.1) | copy-start | bytes 1540
  191.6 14.5 collective-permute-start.1
  216.7 21.8 %copy-start.19 = (bf16[1,2,128,1024]{2,1,0,3:T(2,128)(2,1)}, bf16[1,2,128,1024]{2,1,0,3:T(2,128)(2,1)S(1)}, u32[]{:S(2)}) copy-start(bf16[1,2,128,1024]{2,1,0,3:T(2,128)(2,1)S(1)} %all-gather.2) | copy-start | bytes 1572868
  278.0 52.2 %copy-start.12 = (bf16[1,1024,512]{2,1,0:T(8,128)(2,1)S(1)}, bf16[1,1024,512]{2,1,0:T(8,128)(2,1)}, u32[]{:S(2)}) copy-start(bf16[1,1024,512]{2,1,0:T(8,128)(2,1)} %param.40) | copy-start | bytes 3145732
  278.0 96.4 %all-gather.16.cloned.1.call-start = ((), (), s32[]{:S(2)}) async-start(), calls=%async_computation.9 | async-start | bytes 3145728 | tf_op jit(solution)/shard_map/all_gather | solution.py:82
  338.3 284.4 %copy-start.73 = (f32[1024]{0:T(1024)}, f32[1024]{0:T(1024)S(1)}, u32[]{:S(2)}) copy-start(f32[1024]{0:T(1024)S(1)} %add_rsqrt_fusion) | copy-start | bytes 12292
  341.1 163.1 %all-gather.18.cloned.1.call-start = ((), (), s32[]{:S(2)}) async-start(), calls=%async_computation.10 | async-start | bytes 17825792 | tf_op jit(solution)/shard_map/all_gather | solution.py:287
  343.9 193.1 %all-gather.22.cloned.1.call-start = ((), (), s32[]{:S(2)}) async-start(), calls=%async_computation.18 | async-start | bytes 3145728 | tf_op jit(solution)/shard_map/all_gather | solution.py:82
  344.5 269.9 %reduce-scatter.11.cloned.1.call-start = ((), (), s32[]{:S(2)}) async-start(), calls=%async_computation.12 | async-start | bytes 6291456 | tf_op jit(solution)/shard_map/reduce_scatter | solution.py:86
  559.9 62.8 %copy-start.22 = (bf16[1,1024,512]{2,1,0:T(8,128)(2,1)S(1)}, bf16[1,1024,512]{2,1,0:T(8,128)(2,1)}, u32[]{:S(2)}) copy-start(bf16[1,1024,512]{2,1,0:T(8,128)(2,1)} %param.41) | copy-start | bytes 3145732
  559.9 145.6 %all-gather.20.cloned.1.call-start = ((), (), s32[]{:S(2)}) async-start(), calls=%async_computation.13 | async-start | bytes 3145728 | tf_op jit(solution)/shard_map/all_gather | solution.py:82
  626.5 284.4 %reduce-scatter.13.cloned.1.call-start = ((), (), s32[]{:S(2)}) async-start(), calls=%async_computation.14 | async-start | bytes 7864320 | tf_op jit(solution)/shard_map/reduce_scatter | solution.py:86
  626.9 11.9 copy-start.15
  626.9 11.9 copy-start.16
  626.9 11.9 copy-start.27
  793.5 506.8 %reduce-scatter.9.cloned.1.call-start = ((), (), s32[]{:S(2)}) async-start(), calls=%async_computation.11 | async-start | bytes 6291456 | tf_op jit(solution)/shard_map/reduce_scatter | solution.py:86
  793.7 11.7 copy-start.28
  793.7 11.7 copy-start.35
  879.9 11.8 copy-start.58
  879.9 11.8 copy-start.112
  891.7 415.2 %all-reduce.12.cloned.1.call-start = ((), (), s32[]{:S(2)}) async-start(), calls=%async_computation.17 | async-start | bytes 196608 | tf_op jit(solution)/shard_map/psum | solution.py:535
  912.2 5.0 collective-permute-start.2
  927.6 8.1 copy-start.84
  935.7 13.5 copy-start.5
  967.8 111.6 %copy-start.44 = (f32[1,512,16]{1,2,0:T(8,128)S(1)}, f32[1,512,16]{1,2,0:T(8,128)}, u32[]{:S(2)}) copy-start(f32[1,512,16]{1,2,0:T(8,128)} %custom-call.6) | copy-start | bytes 98308
  1056.8 40.8 %copy-start.24 = (f32[8,1,128,512]{3,2,1,0:T(8,128)}, f32[8,1,128,512]{3,2,1,0:T(8,128)S(1)}, u32[]{:S(2)}) copy-start(f32[8,1,128,512]{3,2,1,0:T(8,128)S(1)} %get-tuple-element.1224) | copy-start | bytes 6291460
  1188.5 15.8 copy-start.43
  1188.5 15.8 copy-start.46
  1205.8 266.7 %reduce-scatter.15.cloned.1.call-start = ((), (), s32[]{:S(2)}) async-start(), calls=%async_computation.15 | async-start | bytes 17825792 | tf_op jit(solution)/shard_map/reduce_scatter | solution.py:532
  1210.7 599.0 %reduce-scatter.17.cloned.1.call-start = ((), (), s32[]{:S(2)}) async-start(), calls=%async_computation.16 | async-start | bytes 35651584 | tf_op jit(solution)/shard_map/reduce_scatter | solution.py:533
  1234.0 12.4 copy-start.108
  1234.0 12.4 copy-start.117
  1259.4 40.2 %copy-start.89 = (f32[2,512]{1,0:T(2,128)S(1)}, f32[2,512]{1,0:T(2,128)}, u32[]{:S(2)}) copy-start(f32[2,512]{1,0:T(2,128)} %param.53) | copy-start | bytes 12292
  1259.5 40.2 %copy-start.94 = (f32[2,512]{1,0:T(2,128)S(1)}, f32[2,512]{1,0:T(2,128)}, u32[]{:S(2)}) copy-start(f32[2,512]{1,0:T(2,128)} %param.55) | copy-start | bytes 12292
  1259.5 40.2 %copy-start.95 = (f32[2,512]{1,0:T(2,128)S(1)}, f32[2,512]{1,0:T(2,128)}, u32[]{:S(2)}) copy-start(f32[2,512]{1,0:T(2,128)} %param.54) | copy-start | bytes 12292
  1259.5 40.8 %copy-start.7 = (f32[1024,512]{1,0:T(8,128)S(1)}, f32[1024,512]{1,0:T(8,128)}, u32[]{:S(2)}) copy-start(f32[1024,512]{1,0:T(8,128)} %get-tuple-element.2912) | copy-start | bytes 6291460
  1259.5 40.8 %copy-start.74 = (f32[1024]{0:T(1024)S(1)}, f32[1024]{0:T(1024)}, u32[]{:S(2)}) copy-start(f32[1024]{0:T(1024)} %copy-done.73) | copy-start | bytes 12292
  1259.5 40.8 %copy-start.80 = (f32[1,512]{1,0:T(1,128)S(1)}, f32[1,512]{1,0:T(1,128)}, u32[]{:S(2)}) copy-start(f32[1,512]{1,0:T(1,128)} %copy-done.79) | copy-start | bytes 6148
  1259.5 40.8 %copy-start.82 = (f32[1024]{0:T(1024)S(1)}, f32[1024]{0:T(1024)}, u32[]{:S(2)}) copy-start(f32[1024]{0:T(1024)} %copy-done.81) | copy-start | bytes 12292
  1294.5 12.4 copy-start.90
  1306.9 502.8 %copy-start.23 = (f32[1,256,2048]{2,1,0:T(8,128)S(1)}, f32[1,256,2048]{2,1,0:T(8,128)}, u32[]{:S(2)}) copy-start(f32[1,256,2048]{2,1,0:T(8,128)} %param.47) | copy-start | bytes 6291460
  (113 other events, 522.6 us)
Sparse Core Ops, SparseCore 0:
  18.1 34.9 all-gather.11
  55.9 77.3 all-gather.13
  278.2 51.9 reduce-scatter.6
  341.3 33.1 all-gather.15
  377.2 126.9 all-gather.17
  505.7 31.2 all-gather.21
  560.0 54.3 reduce-scatter.10
  626.6 33.1 all-gather.19
  793.6 65.6 reduce-scatter.12
  891.9 54.3 reduce-scatter.8
  1205.9 83.8 all-reduce.11
  1294.9 177.4 reduce-scatter.14
  1477.9 331.7 reduce-scatter.16
where the time goes:
time: 1840 us; the launch traced here: 1820 us
  waiting for transfers between devices  784 us (43%)
  local copies, waits for them, and re-layouts  342 us (19%)
  other arithmetic  331 us (18%)
  matrix products  203 us (11%)
  blocking collectives  127 us (7%)
  between operations  28.1 us (2%)
    reduce_scatter x1, waiting for transfers between devices, body(): lax.psum_scatter(mlp_grads, 'dp', scatter_dimension=1, tiled=True)  333 us
    reduce_scatter x1, waiting for transfers between devices, body(): lax.psum_scatter(attn_grads, 'dp', scatter_dimension=1, tiled=True)  164 us
    all_gather x1, waiting for transfers between devices, body(): lax.all_gather(low_mlp, 'dp', axis=1, tiled=True)  130 us
    reduce_scatter x4, waiting for transfers between devices, reduce_partial(): return lax.psum_scatter(values, 'tensor', scatter_dimension=1, tiled=True)  106 us
    dot_general x32, other arithmetic, advance(): collected = jnp.einsum('jcn,jc->cn', weighted, span_in, precision=highest)  66.1 us
    dynamic_update_slice x40, other arithmetic, span_states(): return lax.scan(advance, start_state, (span_rows, same_end, pass_flags))  52.8 us
    all_gather x4, waiting for transfers between devices, full_rows(): return lax.all_gather(values, 'tensor', axis=1, tiled=True)  50.3 us
    dynamic_slice x48, local copies, waits for them, and re-layouts, span_states(): return lax.scan(advance, start_state, (span_rows, same_end, pass_flags))  47.8 us
  transfers between devices with their start and end apart: 16, of which 7 were waited for; matrix products, arithmetic and copies ran while one was open for 35% of the time, Pallas kernels for 0%

commit v1 on v0

v1 whole, which is shorter than its diff:
```python
import functools
import itertools

import jax
import jax.numpy as jnp
from jax import lax
from jax.experimental import pallas as pl
from jax.experimental.pallas import tpu as pltpu
from jax.sharding import PartitionSpec as P

D = 1024
HEAD_DIM = 128
FF = 4096
STATE = 16
CTX = 128
BL = 512
OWNER_GROUPS = 4
STEP = 5

epsilon_norm = 1e-05
beta_first = 0.9
beta_second = 0.95
epsilon_adam = 1e-08
matrix_decay = 0.1
masked_score = -1e30
score_scale = HEAD_DIM ** (-0.5)
f32 = jnp.float32
bf16 = jnp.bfloat16
i32 = jnp.int32
VMEM_BYTES = 56 * 1024 * 1024
SWAP = [(0, 1), (1, 0)]
TILE = 256
QT = 128


def dot_nn(left, right):
    return lax.dot_general(left, right, (((1,), (0,)), ((), ())), preferred_element_type=f32)


def dot_nt(left, right):
    return lax.dot_general(left, right, (((1,), (1,)), ((), ())), preferred_element_type=f32)


def dot_tn(left, right):
    return lax.dot_general(left, right, (((0,), (0,)), ((), ())), preferred_element_type=f32)


def call(kernel, grid, in_specs, out_specs, out_shape, scratch=(), prefetch=0, flops=0, nbytes=0):
    return pl.pallas_call(
        kernel,
        grid_spec=pltpu.PrefetchScalarGridSpec(
            num_scalar_prefetch=prefetch,
            grid=grid,
            in_specs=in_specs,
            out_specs=out_specs,
            scratch_shapes=scratch,
        ),
        out_shape=out_shape,
        compiler_params=pltpu.CompilerParams(vmem_limit_bytes=VMEM_BYTES),
        cost_estimate=pl.CostEstimate(flops=flops, bytes_accessed=nbytes, transcendentals=0),
    )


def whole(shape):
    return pl.BlockSpec(shape, lambda *_: (0,) * len(shape))


def sds(shape, dtype):
    return jax.ShapeDtypeStruct(shape, dtype)


def swap_x(values):
    return lax.ppermute(values, "tensor", SWAP)


def gather_dp(values):
    count = lax.axis_size("dp")
    here = lax.axis_index("dp")
    held = values[None]
    step = 1
    while step < count:
        other = lax.ppermute(held, "dp", [(i, i ^ step) for i in range(count)])
        later = (here // step) % 2 == 1
        held = jnp.where(
            later,
            jnp.concatenate([other, held], axis=0),
            jnp.concatenate([held, other], axis=0),
        )
        step *= 2
    return held


def total_dp(values):
    count = lax.axis_size("dp")
    step = 1
    while step < count:
        values = values + lax.ppermute(values, "dp", [(i, i ^ step) for i in range(count)])
        step *= 2
    return values


def slot_numbers(owner_part):
    count = owner_part.shape[0]
    order = jnp.arange(count, dtype=i32)
    earlier = (order[None, :] < order[:, None]).astype(i32)
    same = (owner_part[:, None] == owner_part[None, :]).astype(i32)
    return jnp.sum(same * earlier, axis=1)


def slot_rates(owner_part, rate_list, slot_count, fallback):
    slots = slot_numbers(owner_part)
    slot_hit = slots[:, None, None] == jnp.arange(slot_count, dtype=i32)[None, :, None]
    group_hit = owner_part[:, None, None] == jnp.arange(OWNER_GROUPS, dtype=i32)[None, None, :]
    hits = jnp.logical_and(slot_hit, group_hit).astype(f32)
    rates = jnp.asarray(rate_list, f32)[:, None, None]
    return jnp.sum(hits * rates, axis=0) + (1.0 - jnp.sum(hits, axis=0)) * fallback


def routes(full_count, empty_count):
    groups = range(OWNER_GROUPS)
    ways = []
    for full in itertools.combinations(groups, full_count):
        rest = [g for g in groups if g not in full]
        for empty in itertools.combinations(rest, empty_count):
            ways.append((full, empty))
    return ways


ATTN_WAYS = routes(1, 1) + routes(2, 2)
MLP_WAYS = routes(2, 2)


def way_code(full, empty):
    code = 0
    for g in range(OWNER_GROUPS):
        digit = 2 if g in full else (0 if g in empty else 1)
        code += digit * 3**g
    return code


def plan(surplus, ways):
    weights = jnp.asarray([3**g for g in range(OWNER_GROUPS)], i32)
    code = jnp.sum(surplus * weights)
    hit = (code == jnp.asarray([way_code(*way) for way in ways], i32)).astype(i32)
    index = jnp.sum(hit * jnp.arange(len(ways), dtype=i32))
    taker = [[0] * OWNER_GROUPS for _ in ways]
    for w, (full, empty) in enumerate(ways):
        for a, b in zip(full, empty):
            taker[w][a] = b
    return index, jnp.sum(hit[:, None] * jnp.asarray(taker, i32), axis=0)


def move(values, index, ways, back):
    size = lax.axis_size("dp") // OWNER_GROUPS

    def branch(way):
        pairs = []
        for a, b in zip(*way):
            if back:
                a, b = b, a
            pairs += [(a * size + j, b * size + j) for j in range(size)]
        return lambda v: lax.ppermute(v, "dp", pairs)

    return lax.switch(index, [branch(way) for way in ways], values)


def first_half():
    return lax.broadcasted_iota(i32, (8, 128), 0) < 4


def flag(condition):
    return jnp.where(condition, f32(1.0), f32(0.0))


def keep_at(seg_ref, t, half):
    return jnp.where(
        half, flag(seg_ref[t + 1] == seg_ref[t]), flag(seg_ref[BL + t + 1] == seg_ref[BL + t])
    )


def scan_kernel(seg_ref, h_ref, rate_ref, c_ref, y_ref, s_ref, e_ref):
    half = first_half()
    decay = [jnp.exp(-rate_ref[n]) for n in range(STATE)]

    def step(t, states):
        keep = keep_at(seg_ref, t, half)
        row = h_ref[t]
        return [(states[n] * keep) * decay[n] + row for n in range(STATE)]

    def step_out(t, states):
        states = step(t, states)
        total = c_ref[0] * states[0]
        for n in range(1, STATE):
            total = total + c_ref[n] * states[n]
        y_ref[t - (BL - CTX)] = total
        return states

    states = [jnp.zeros((8, 128), f32)] * STATE
    states = lax.fori_loop(0, BL - CTX, step, states, unroll=4)
    states = lax.fori_loop(BL - CTX, BL, step_out, states, unroll=2)
    joined = flag(seg_ref[2 * BL] == seg_ref[BL])
    for n in range(STATE):
        s_ref[n] = states[n]
        e_ref[n] = states[n] + (joined * jnp.exp(-rate_ref[n] * BL)) * pltpu.roll(states[n], 4, 0)


def tail_kernel(seg_ref, carry_ref, s_ref, rate_ref, c_ref, y_ref, out_ref, start_ref):
    half = first_half()
    before = seg_ref[0]
    joined = flag(seg_ref[BL] == before)
    decay = [jnp.exp(-rate_ref[n]) for n in range(STATE)]
    weighted = []
    for n in range(STATE):
        carried = carry_ref[n]
        mid = pltpu.roll(s_ref[n], 4, 0) + (joined * jnp.exp(-rate_ref[n] * BL)) * carried
        start = jnp.where(half, carried, mid)
        start_ref[n] = start
        weighted.append(c_ref[n] * start * jnp.exp(-rate_ref[n] * (BL - CTX + 1)))

    def step(t, parts):
        mask = jnp.where(
            half,
            flag(seg_ref[t + 1 + BL - CTX] == before),
            flag(seg_ref[BL + t + 1 + BL - CTX] == seg_ref[BL]),
        )
        total = parts[0]
        for n in range(1, STATE):
            total = total + parts[n]
        out_ref[t] = y_ref[t] + mask * total
        return [parts[n] * decay[n] for n in range(STATE)]

    lax.fori_loop(0, CTX, step, weighted, unroll=4)


def back_total_kernel(seg_ref, g_ref, rate_ref, c_ref, own_ref, out_ref):
    half = first_half()
    decay = [jnp.exp(-rate_ref[n]) for n in range(STATE)]

    def step(k, sums):
        t = CTX - 1 - k
        mask = jnp.where(
            half,
            flag(seg_ref[t + 1 + BL - CTX] == seg_ref[1]),
            flag(seg_ref[BL + t + 1 + BL - CTX] == seg_ref[BL]),
        )
        grad = mask * g_ref[t]
        return [decay[n] * (sums[n] + grad) for n in range(STATE)]

    sums = lax.fori_loop(0, CTX, step, [jnp.zeros((8, 128), f32)] * STATE, unroll=4)
    joined = flag(seg_ref[1] == seg_ref[BL])
    for n in range(STATE):
        total = sums[n] * c_ref[n] * jnp.exp(-rate_ref[n] * (BL - CTX))
        own_ref[n] = total
        out_ref[n] = total + (joined * jnp.exp(-rate_ref[n] * BL)) * pltpu.roll(total, 4, 0)


def sens_kernel(seg_ref, h_ref, g_ref, start_ref, rate_ref, gc_ref, ga_ref, z_ref):
    half = first_half()
    group = 8
    for first in range(0, STATE, group):
        ids = range(first, first + group)
        decay = [jnp.exp(-rate_ref[n]) for n in ids]

        def step(t, both, decay=decay):
            keep = keep_at(seg_ref, t, half)
            row = h_ref[t]
            kept = [v * keep for v in both[0]]
            sens = [(both[1][n] * keep) * decay[n] + kept[n] for n in range(group)]
            states = [kept[n] * decay[n] + row for n in range(group)]
            return states, sens

        def step_sum(t, carried, step=step):
            states, sens = step(t, carried[:2])
            grad = g_ref[t - (BL - CTX)]
            by_c = [carried[2][n] + grad * states[n] for n in range(group)]
            by_a = [carried[3][n] + grad * sens[n] for n in range(group)]
            return states, sens, by_c, by_a

        zeros = [jnp.zeros((8, 128), f32)] * group
        both = ([start_ref[n] for n in ids], zeros)
        both = lax.fori_loop(0, BL - CTX, step, both, unroll=4)
        carried = lax.fori_loop(BL - CTX, BL, step_sum, (both[0], both[1], zeros, zeros), unroll=2)
        for k, n in enumerate(ids):
            z_ref[n] = carried[1][k]
            gc_ref[n] = carried[2][k]
            ga_ref[n] = carried[3][k]


def back_scan_kernel(
    seg_ref, g_ref, own_ref, later_ref, z_ref, ga_ref, rate_ref, c_ref, gh_ref, out_ref
):
    half = first_half()
    decay = [jnp.exp(-rate_ref[n]) for n in range(STATE)]
    joined = flag(seg_ref[2 * BL] == seg_ref[BL])
    sums = []
    for n in range(STATE):
        later = later_ref[n]
        first = pltpu.roll(own_ref[n], 4, 0) + (joined * jnp.exp(-rate_ref[n] * BL)) * later
        entering = jnp.where(half, first, later)
        sums.append(entering)
        out_ref[n] = ga_ref[n] * c_ref[n] + entering * z_ref[n]

    def finish(t, sums):
        total = sums[0]
        for n in range(1, STATE):
            total = total + sums[n]
        gh_ref[t] = total
        keep = keep_at(seg_ref, t, half)
        return [(v * keep) * decay[n] for n, v in enumerate(sums)]

    def step_tail(k, sums):
        t = BL - 1 - k
        grad = g_ref[t - (BL - CTX)]
        return finish(t, [sums[n] + c_ref[n] * grad for n in range(STATE)])

    def step(k, sums):
        return finish(BL - 1 - k, sums)

    sums = lax.fori_loop(0, CTX, step_tail, sums, unroll=2)
    lax.fori_loop(CTX, BL, step, sums, unroll=4)


def to_lanes(values, blocks, steps):
    return (
        values.reshape(blocks, steps, 4, 128).transpose(1, 0, 2, 3).reshape(steps, blocks * 4, 128)
    )


def from_lanes(values, blocks, steps):
    return values.reshape(steps, blocks, 4, 128).transpose(1, 0, 2, 3).reshape(blocks, steps, 512)


def attend_kernel(
    host_ref,
    hid_ref,
    ctx_ref,
    wq_ref,
    wk_ref,
    wv_ref,
    segq_ref,
    segk_ref,
    q_ref,
    k_ref,
    v_ref,
    ck_ref,
    cv_ref,
    pc_ref,
    pb_ref,
    mix_ref,
):
    hid = hid_ref[...]
    ctx = ctx_ref[...]
    q_ref[...] = dot_nn(hid, wq_ref[0]).astype(bf16)
    k_ref[...] = dot_nn(hid, wk_ref[0]).astype(bf16)
    v_ref[...] = dot_nn(hid, wv_ref[0]).astype(bf16)
    ck_ref[...] = dot_nn(ctx, wk_ref[0]).astype(bf16)
    cv_ref[...] = dot_nn(ctx, wv_ref[0]).astype(bf16)
    ctx_ids = segk_ref[:, :CTX]
    for i in range(BL // QT):
        rows = slice(i * QT, (i + 1) * QT)
        reach = (i + 1) * QT
        ids = segq_ref[rows]
        ctx_ok = ctx_ids == ids
        place_q = lax.broadcasted_iota(i32, (QT, reach), 0) + i * QT
        place_k = lax.broadcasted_iota(i32, (QT, reach), 1)
        block_ok = jnp.logical_and(place_k <= place_q, segk_ref[:, CTX : CTX + reach] == ids)
        for head in range(TILE // HEAD_DIM):
            cols = slice(head * HEAD_DIM, (head + 1) * HEAD_DIM)
            query = q_ref[rows, cols]
            sc = dot_nt(query, ck_ref[:, cols]) * score_scale
            sb = dot_nt(query, k_ref[:reach, cols]) * score_scale
            sc = jnp.where(ctx_ok, sc, masked_score)
            sb = jnp.where(block_ok, sb, masked_score)
            top = jnp.maximum(
                jnp.max(sc, axis=1, keepdims=True), jnp.max(sb, axis=1, keepdims=True)
            )
            ec = jnp.exp(sc - top)
            eb = jnp.exp(sb - top)
            total = jnp.sum(ec, axis=1, keepdims=True) + jnp.sum(eb, axis=1, keepdims=True)
            inverse = 1.0 / total
            pc = (ec * inverse).astype(bf16)
            pb = (eb * inverse).astype(bf16)
            pc_ref[head, rows, :] = pc
            pb_ref[head, rows, :reach] = pb
            if reach < BL:
                pb_ref[head, rows, reach:] = jnp.zeros((QT, BL - reach), bf16)
            mixed = dot_nn(pc, cv_ref[:, cols]) + dot_nn(pb, v_ref[:reach, cols])
            mix_ref[rows, cols] = mixed.astype(bf16)


def attend_forward(hosts, block, hidden, context, attn_full, seg_col, seg_row, half_width):
    pairs = half_width // TILE

    def weight(position):
        return pl.BlockSpec((1, D, TILE), lambda p, s: (s[position], 0, p))

    def tile(rows):
        return pl.BlockSpec((rows, TILE), lambda p, s: (0, p))

    heads = half_width // HEAD_DIM
    per = TILE // HEAD_DIM
    return call(
        attend_kernel,
        (pairs,),
        [
            pl.BlockSpec((BL, D), lambda p, s: (block, 0)),
            pl.BlockSpec((CTX, D), lambda p, s: (block, 0)),
            weight(0),
            weight(1),
            weight(2),
            pl.BlockSpec((BL, 1), lambda p, s: (block, 0)),
            whole((1, CTX + BL)),
        ],
        [
            tile(BL),
            tile(BL),
            tile(BL),
            tile(CTX),
            tile(CTX),
            pl.BlockSpec((per, BL, CTX), lambda p, s: (p, 0, 0)),
            pl.BlockSpec((per, BL, BL), lambda p, s: (p, 0, 0)),
            tile(BL),
        ],
        [
            sds((BL, half_width), bf16),
            sds((BL, half_width), bf16),
            sds((BL, half_width), bf16),
            sds((CTX, half_width), bf16),
            sds((CTX, half_width), bf16),
            sds((heads, BL, CTX), bf16),
            sds((heads, BL, BL), bf16),
            sds((BL, half_width), bf16),
        ],
        prefetch=1,
        flops=8 * 10**9,
        nbytes=12 * 10**6,
    )(hosts, hidden, context, attn_full, attn_full, attn_full, seg_col, seg_row)


def attend_back_kernel(
    host_ref,
    own_ref,
    other_ref,
    cot_ref,
    mid_ref,
    gain_ref,
    wo_ref,
    wq_ref,
    wk_ref,
    wv_ref,
    q_ref,
    k_ref,
    v_ref,
    ck_ref,
    cv_ref,
    pc_ref,
    pb_ref,
    low_ref,
    gmid_ref,
    ggain_ref,
    dq_ref,
    dk_ref,
    dv_ref,
    dck_ref,
    dcv_ref,
    hid_ref,
    ctx_ref,
    dsc_ref,
    dsb_ref,
):
    pair = pl.program_id(0)

    @pl.when(pair == 0)
    def _():
        grad = own_ref[...] + other_ref[...].astype(f32)
        middle = mid_ref[...]
        inverse = lax.rsqrt(jnp.mean(middle * middle, axis=1, keepdims=True) + epsilon_norm)
        scaled = middle * inverse
        ggain_ref[...] = jnp.sum(grad * scaled, axis=0, keepdims=True)
        weighted = grad * gain_ref[...]
        centre = jnp.mean(weighted * scaled, axis=1, keepdims=True)
        result = cot_ref[...].astype(f32) + inverse * (weighted - scaled * centre)
        gmid_ref[...] = result
        low_ref[...] = result.astype(bf16)
        hid_ref[...] = jnp.zeros_like(hid_ref)
        ctx_ref[...] = jnp.zeros_like(ctx_ref)

    grad_mixed = dot_nn(low_ref[...], wo_ref[0]).astype(bf16)
    for head in range(TILE // HEAD_DIM):
        cols = slice(head * HEAD_DIM, (head + 1) * HEAD_DIM)
        grad_head = grad_mixed[:, cols]
        for i in range(BL // QT):
            rows = slice(i * QT, (i + 1) * QT)
            reach = (i + 1) * QT
            grad_rows = grad_head[rows]
            gpc = dot_nt(grad_rows, cv_ref[:, cols])
            gpb = dot_nt(grad_rows, v_ref[:reach, cols])
            pc = pc_ref[head, rows, :].astype(f32)
            pb = pb_ref[head, rows, :reach].astype(f32)
            tc = pc * gpc
            tb = pb * gpb
            centre = jnp.sum(tc, axis=1, keepdims=True) + jnp.sum(tb, axis=1, keepdims=True)
            dsc_ref[rows, :] = (tc - pc * centre).astype(bf16)
            dsb_ref[rows, :reach] = (tb - pb * centre).astype(bf16)
            if reach < BL:
                dsb_ref[rows, reach:] = jnp.zeros((QT, BL - reach), bf16)
        dsc = dsc_ref[...]
        dsb = dsb_ref[...]
        dq = (dot_nn(dsc, ck_ref[:, cols]) + dot_nn(dsb, k_ref[:, cols])) * score_scale
        dq_ref[:, cols] = dq.astype(bf16)
        query = q_ref[:, cols]
        dk_ref[:, cols] = (dot_tn(dsb, query) * score_scale).astype(bf16)
        dck_ref[:, cols] = (dot_tn(dsc, query) * score_scale).astype(bf16)
        dv_ref[:, cols] = dot_tn(pb_ref[head], grad_head).astype(bf16)
        dcv_ref[:, cols] = dot_tn(pc_ref[head], grad_head).astype(bf16)
    hid_ref[...] += (
        dot_nt(dq_ref[...], wq_ref[0])
        + dot_nt(dk_ref[...], wk_ref[0])
        + dot_nt(dv_ref[...], wv_ref[0])
    )
    ctx_ref[...] += dot_nt(dck_ref[...], wk_ref[0]) + dot_nt(dcv_ref[...], wv_ref[0])


def attend_backward(hosts, block, own, other, cot_full, middle, gain, attn_full, kept, half_width):
    pairs = half_width // TILE
    per = TILE // HEAD_DIM

    def weight(position):
        return pl.BlockSpec((1, D, TILE), lambda p, s: (s[position], 0, p))

    def tile(rows):
        return pl.BlockSpec((rows, TILE), lambda p, s: (0, p))

    return call(
        attend_back_kernel,
        (pairs,),
        [
            whole((BL, D)),
            whole((BL, D)),
            pl.BlockSpec((BL, D), lambda p, s: (block, 0)),
            whole((BL, D)),
            whole((1, D)),
            weight(3),
            weight(0),
            weight(1),
            weight(2),
            tile(BL),
            tile(BL),
            tile(BL),
            tile(CTX),
            tile(CTX),
            pl.BlockSpec((per, BL, CTX), lambda p, s: (p, 0, 0)),
            pl.BlockSpec((per, BL, BL), lambda p, s: (p, 0, 0)),
        ],
        [
            whole((BL, D)),
            whole((BL, D)),
            whole((1, D)),
            tile(BL),
            tile(BL),
            tile(BL),
            tile(CTX),
            tile(CTX),
            whole((BL, D)),
            whole((CTX, D)),
        ],
        [
            sds((BL, D), bf16),
            sds((BL, D), f32),
            sds((1, D), f32),
            sds((BL, half_width), bf16),
            sds((BL, half_width), bf16),
            sds((BL, half_width), bf16),
            sds((CTX, half_width), bf16),
            sds((CTX, half_width), bf16),
            sds((BL, D), f32),
            sds((CTX, D), f32),
        ],
        scratch=[pltpu.VMEM((BL, CTX), bf16), pltpu.VMEM((BL, BL), bf16)],
        prefetch=1,
        flops=12 * 10**9,
        nbytes=20 * 10**6,
    )(
        hosts,
        own,
        other,
        cot_full,
        middle,
        gain,
        attn_full,
        attn_full,
        attn_full,
        attn_full,
        *kept,
    )


def attn_grad_kernel(host_ref, *refs):
    (hid0, hid1, ctx0, ctx1, low0, low1), rest = refs[:6], refs[6:]
    (dq0, dk0, dv0, dck0, dcv0, mix0), rest = rest[:6], rest[6:]
    (dq1, dk1, dv1, dck1, dcv1, mix1), (out_ref,) = rest[:6], rest[6:]
    matrix = pl.program_id(0)

    @pl.when(matrix == 0)
    def _():
        out_ref[0] = (dot_tn(hid0[...], dq0[...]) + dot_tn(hid1[...], dq1[...])).astype(bf16)

    @pl.when(matrix == 1)
    def _():
        out_ref[0] = (
            dot_tn(hid0[...], dk0[...])
            + dot_tn(hid1[...], dk1[...])
            + dot_tn(ctx0[...], dck0[...])
            + dot_tn(ctx1[...], dck1[...])
        ).astype(bf16)

    @pl.when(matrix == 2)
    def _():
        out_ref[0] = (
            dot_tn(hid0[...], dv0[...])
            + dot_tn(hid1[...], dv1[...])
            + dot_tn(ctx0[...], dcv0[...])
            + dot_tn(ctx1[...], dcv1[...])
        ).astype(bf16)

    @pl.when(matrix == 3)
    def _():
        out_ref[0] = (dot_tn(low0[...], mix0[...]) + dot_tn(low1[...], mix1[...])).astype(bf16)


def attn_grads(hosts, hidden, context, lows, blocks, half_width):
    hid_specs = [
        pl.BlockSpec((BL, D), lambda m, s: (0, 0)),
        pl.BlockSpec((BL, D), lambda m, s: (1, 0)),
        pl.BlockSpec((CTX, D), lambda m, s: (0, 0)),
        pl.BlockSpec((CTX, D), lambda m, s: (1, 0)),
    ]
    block_specs = [
        whole((BL, half_width)),
        whole((BL, half_width)),
        whole((BL, half_width)),
        whole((CTX, half_width)),
        whole((CTX, half_width)),
        whole((BL, half_width)),
    ]
    return call(
        attn_grad_kernel,
        (4,),
        hid_specs + [whole((BL, D))] * 2 + block_specs * 2,
        [pl.BlockSpec((1, D, half_width), lambda m, s: (s[m], 0, 0))],
        [sds((OWNER_GROUPS, D, half_width), bf16)],
        prefetch=1,
        flops=46 * 10**8,
        nbytes=14 * 10**6,
    )(hosts, hidden, hidden, context, context, *lows, *blocks[0], *blocks[1])[0]


def mlp_kernel(
    host_ref,
    own_ref,
    other_ref,
    wo_ref,
    woo_ref,
    tok_ref,
    gain_ref,
    cot_ref,
    w1_ref,
    w2_ref,
    mid_ref,
    hid_ref,
    act_ref,
    pre_ref,
    grad_ref,
    low_ref,
):
    step = pl.program_id(0)

    @pl.when(step == 0)
    def _():
        middle = (
            tok_ref[...].astype(f32)
            + dot_nt(own_ref[...], wo_ref[0])
            + dot_nt(other_ref[...], woo_ref[...])
        )
        inverse = lax.rsqrt(jnp.mean(middle * middle, axis=1, keepdims=True) + epsilon_norm)
        mid_ref[...] = middle
        hid_ref[...] = (middle * inverse * gain_ref[...]).astype(bf16)
        grad_ref[...] = jnp.zeros_like(grad_ref)

    w1 = w1_ref[0]
    w2 = w2_ref[0]
    pre = dot_nn(hid_ref[...], w1)
    grad_act = dot_nn(cot_ref[...], w2)
    inner = 0.7978845608028654 * (pre + 0.044715 * (pre * pre * pre))
    bent = jnp.tanh(inner)
    gate = 0.5 * (1.0 + bent)
    act_ref[...] = (pre * gate).astype(bf16)
    slope = gate + 0.5 * pre * (1.0 - bent * bent) * (
        0.7978845608028654 * (1.0 + 0.134145 * (pre * pre))
    )
    grad_pre = (slope * grad_act).astype(bf16)
    pre_ref[...] = grad_pre
    grad_ref[...] += dot_nt(grad_pre, w1)

    @pl.when(step == pl.num_programs(0) - 1)
    def _():
        low_ref[...] = grad_ref[...].astype(bf16)


def mlp_block(hosts, block, own, other, attn_full, wo_other, tok_full, gain, cot_full, mlp_full):
    half_width = own.shape[1]
    quarter = mlp_full.shape[2]
    hidden = 2 * quarter
    per = quarter // TILE

    def weight(position):
        return pl.BlockSpec(
            (1, D, TILE), lambda f, s: (s[4 + 2 * position + f // per], 0, lax.rem(f, per))
        )

    return call(
        mlp_kernel,
        (2 * per,),
        [
            whole((BL, half_width)),
            whole((BL, half_width)),
            pl.BlockSpec((1, D, half_width), lambda f, s: (s[3], 0, 0)),
            whole((D, half_width)),
            pl.BlockSpec((BL, D), lambda f, s: (block, 0)),
            whole((1, D)),
            pl.BlockSpec((BL, D), lambda f, s: (block, 0)),
            weight(0),
            weight(1),
        ],
        [
            whole((BL, D)),
            whole((BL, D)),
            pl.BlockSpec((BL, TILE), lambda f, s: (0, f)),
            pl.BlockSpec((BL, TILE), lambda f, s: (0, f)),
            whole((BL, D)),
            whole((BL, D)),
        ],
        [
            sds((BL, D), f32),
            sds((BL, D), bf16),
            sds((BL, hidden), bf16),
            sds((BL, hidden), bf16),
            sds((BL, D), f32),
            sds((BL, D), bf16),
        ],
        prefetch=1,
        flops=8 * 10**9,
        nbytes=24 * 10**6,
    )(hosts, own, other, attn_full, wo_other, tok_full, gain, cot_full, mlp_full, mlp_full)


def mlp_grad_kernel(host_ref, h0, h1, g0, g1, p0, p1, a0, a1, out_ref):
    matrix = pl.program_id(0)

    @pl.when(matrix == 0)
    def _():
        out_ref[0] = (dot_tn(h0[...], p0[...]) + dot_tn(h1[...], p1[...])).astype(bf16)

    @pl.when(matrix == 1)
    def _():
        out_ref[0] = (dot_tn(g0[...], a0[...]) + dot_tn(g1[...], a1[...])).astype(bf16)


def mlp_grads(hosts, hiddens, cot_full, pres, acts):
    hidden = acts[0].shape[1]
    quarter = hidden // 2
    per = quarter // TILE
    last = 2 * per - 1
    used_first = pl.BlockSpec((BL, TILE), lambda m, f, s: (0, jnp.where(m == 0, f, last)))
    used_second = pl.BlockSpec((BL, TILE), lambda m, f, s: (0, jnp.where(m == 1, f, 0)))
    return call(
        mlp_grad_kernel,
        (2, 2 * per),
        [
            whole((BL, D)),
            whole((BL, D)),
            pl.BlockSpec((BL, D), lambda m, f, s: (0, 0)),
            pl.BlockSpec((BL, D), lambda m, f, s: (1, 0)),
            used_first,
            used_first,
            used_second,
            used_second,
        ],
        [
            pl.BlockSpec(
                (1, D, TILE), lambda m, f, s: (s[4 + 2 * m + f // per], 0, lax.rem(f, per))
            )
        ],
        [sds((OWNER_GROUPS, D, quarter), bf16)],
        prefetch=1,
        flops=86 * 10**8,
        nbytes=20 * 10**6,
    )(hosts, hiddens[0], hiddens[1], cot_full, cot_full, pres[0], pres[1], acts[0], acts[1])[0]


def mlp_out_kernel(host_ref, a_ref, w2_ref, out_ref):
    step = pl.program_id(0)

    @pl.when(step == 0)
    def _():
        out_ref[...] = jnp.zeros_like(out_ref)

    out_ref[...] += dot_nt(a_ref[...], w2_ref[0])


def mlp_out(hosts, act, mlp_full):
    quarter = mlp_full.shape[2]
    per = quarter // TILE
    return call(
        mlp_out_kernel,
        (2 * per,),
        [
            pl.BlockSpec((BL, TILE), lambda f, s: (0, f)),
            pl.BlockSpec((1, D, TILE), lambda f, s: (s[6 + f // per], 0, lax.rem(f, per))),
        ],
        [whole((BL, D))],
        [sds((BL, D), f32)],
        prefetch=1,
        flops=22 * 10**8,
        nbytes=8 * 10**6,
    )(hosts, act, mlp_full)[0]


def adam_step(gradient, moment_one, moment_two, weight, rate_table, decay_weight):
    step_count = f32(STEP)
    first_new = beta_first * moment_one + (1.0 - beta_first) * gradient
    second_new = beta_second * moment_two + (1.0 - beta_second) * gradient * gradient
    fixed_one = 1.0 - jnp.power(beta_first, step_count)
    fixed_two = 1.0 - jnp.power(beta_second, step_count)
    update = first_new / fixed_one / (jnp.sqrt(second_new / fixed_two) + epsilon_adam)
    return (first_new, second_new, weight - rate_table * (update + decay_weight * weight))


def body(
    tokens,
    cotangent,
    segments,
    owners,
    attn_master,
    attn_first,
    attn_second,
    mlp_master,
    mlp_first,
    mlp_second,
    ssm_params,
    ssm_first,
    ssm_second,
    norm_gains,
    gains_first,
    gains_second,
):
    rows = tokens.shape[1]
    width = tokens.shape[2]
    blocks = rows // BL
    dp_count = lax.axis_size("dp")
    dp_here = lax.axis_index("dp")
    side = lax.axis_index("tensor")
    group = dp_here // (dp_count // OWNER_GROUPS)
    bank_rows = attn_master.shape[1]
    quarter = mlp_master.shape[2] // 2

    def both_sides(own, other):
        return jnp.where(
            side == 0,
            jnp.concatenate([own, other], axis=-1),
            jnp.concatenate([other, own], axis=-1),
        )

    def side_of(values, which):
        return lax.dynamic_slice_in_dim(values, which * width, width, values.ndim - 1)

    attn_owner = owners[:4]
    mlp_owner = owners[4:]
    groups = jnp.arange(OWNER_GROUPS, dtype=i32)
    attn_count = jnp.sum((attn_owner[:, None] == groups[None, :]).astype(i32), axis=0)
    mlp_count = jnp.sum((mlp_owner[:, None] == groups[None, :]).astype(i32), axis=0)
    attn_way, attn_taker = plan(attn_count, ATTN_WAYS)
    mlp_way, mlp_taker = plan(2 * mlp_count, MLP_WAYS)
    attn_slot = slot_numbers(attn_owner)
    attn_host = jnp.where(attn_slot == 0, attn_owner, attn_taker[attn_owner])
    mlp_host = jnp.stack([mlp_owner, mlp_taker[mlp_owner]], axis=1).reshape(-1)
    hosts = jnp.concatenate([attn_host, mlp_host]).astype(i32)
    attn_here = attn_count[group]
    mlp_here = mlp_count[group]

    attn_low = attn_master.astype(bf16)
    mlp_low = mlp_master[0].astype(bf16)
    attn_moved = move(attn_low[1], attn_way, ATTN_WAYS, False)
    mlp_moved = move(mlp_low[:, quarter:], mlp_way, MLP_WAYS, False)
    attn_block = jnp.where(attn_here == 0, attn_moved, attn_low[0])
    mlp_block_low = jnp.where(mlp_here == 0, mlp_moved, mlp_low[:, :quarter])
    attn_full = lax.all_gather(attn_block, "dp", axis=0, tiled=True)
    mlp_full = lax.all_gather(mlp_block_low, "dp", axis=0, tiled=True)
    attn_full = attn_full.reshape(OWNER_GROUPS, D, width)
    mlp_full = mlp_full.reshape(OWNER_GROUPS, D, quarter)

    tok = tokens.reshape(rows, width)
    cot = cotangent.reshape(rows, width)
    tok_f = tok.astype(f32)
    square_here = jnp.sum(tok_f * tok_f, axis=1)
    square_other = swap_x(square_here)
    tok_other = swap_x(tok)
    cot_other = swap_x(cot)
    gains_other = swap_x(norm_gains)
    inverse_one = lax.rsqrt((square_here + square_other) / D + epsilon_norm)
    scaled_own = tok_f * inverse_one[:, None]
    hidden_own = (scaled_own * norm_gains[0]).astype(bf16)
    hidden_other = (tok_other.astype(f32) * inverse_one[:, None] * gains_other[0]).astype(bf16)
    hidden_full = both_sides(hidden_own, hidden_other)
    tok_full = both_sides(tok, tok_other)
    cot_full = both_sides(cot, cot_other)
    gains_full = both_sides(norm_gains, gains_other)

    seg = segments.reshape(rows)
    prior = lax.ppermute(seg[rows - CTX :] + 1, "dp", [(i, i + 1) for i in range(dp_count - 1)]) - 1
    seg_ext = jnp.concatenate([prior[CTX - 1 :], seg])
    seg_col = seg[:, None]

    param_lanes = ssm_params.transpose(0, 2, 1)
    decay_rate = jnp.exp(param_lanes[0]) * (BL ** (-0.5) / 32.0)
    drive_root = jnp.sqrt(-jnp.expm1(-2.0 * decay_rate))
    reading = param_lanes[2] * drive_root * param_lanes[1]

    def doubled(values):
        lanes = values.reshape(STATE, 4, 128)
        return jnp.concatenate([lanes] * blocks, axis=1)

    rate_lanes = doubled(decay_rate)
    reading_lanes = doubled(reading)
    smem = pl.BlockSpec(memory_space=pltpu.SMEM)
    vmem = pl.BlockSpec(memory_space=pltpu.VMEM)
    state_shape = sds((STATE, 8, 128), f32)

    def plain(kernel, count, outs, cost):
        return pl.pallas_call(
            kernel,
            in_specs=[smem] + [vmem] * count,
            out_specs=[vmem] * len(outs),
            out_shape=outs,
            compiler_params=pltpu.CompilerParams(vmem_limit_bytes=VMEM_BYTES),
            cost_estimate=pl.CostEstimate(flops=cost, bytes_accessed=4 * 10**6, transcendentals=0),
        )

    hidden_lanes = to_lanes(hidden_own.astype(f32), blocks, BL)
    tail_lanes = sds((CTX, 8, 128), f32)
    tail_part, state_ends, device_end = plain(
        scan_kernel, 3, [tail_lanes, state_shape, state_shape], 4 * 10**9
    )(seg_ext, hidden_lanes, rate_lanes, reading_lanes)
    end_rows = device_end[:, 4:].reshape(STATE, width).astype(bf16)
    id_rows = jnp.where(
        (jnp.arange(STATE) == 0)[:, None], seg[rows - 1].astype(f32), seg[0].astype(f32)
    )
    id_rows = jnp.broadcast_to(id_rows, (STATE, 128)).astype(bf16)
    states_all = gather_dp(jnp.concatenate([end_rows, id_rows], axis=1))
    ids_all = states_all[:, :2, width].astype(f32)
    places = jnp.arange(dp_count, dtype=i32)
    gap_before = dp_here - 1 - places
    use_before = jnp.logical_and(gap_before >= 0, ids_all[:, 0] == seg_ext[0].astype(f32))
    power_before = jnp.exp(
        -decay_rate[None] * (rows * jnp.maximum(gap_before, 0)).astype(f32)[:, None, None]
    )
    carry_in = jnp.sum(
        jnp.where(
            use_before[:, None, None], power_before * states_all[:, :, :width].astype(f32), 0.0
        ),
        axis=0,
    )
    tails, state_starts = plain(tail_kernel, 5, [tail_lanes, state_shape], 10**9)(
        seg_ext, doubled(carry_in), state_ends, rate_lanes, reading_lanes, tail_part
    )
    tails = from_lanes(tails, blocks, CTX).astype(bf16)
    handed = lax.ppermute(tails[blocks - 1], "dp", [(i, i + 1) for i in range(dp_count - 1)])
    context_own = jnp.concatenate([handed[None], tails[: blocks - 1]], axis=0).reshape(-1, width)
    context_full = both_sides(context_own, swap_x(context_own))

    seg_rows = []
    for b in range(blocks):
        before = prior if b == 0 else seg[b * BL - CTX : b * BL]
        seg_rows.append(jnp.concatenate([before, seg[b * BL : (b + 1) * BL]])[None])
    kept = []
    mixed = []
    mixed_other = []
    for b in range(blocks):
        outs = attend_forward(
            hosts, b, hidden_full, context_full, attn_full, seg_col, seg_rows[b], width
        )
        kept.append(outs[:7])
        mixed.append(outs[7])
        mixed_other.append(swap_x(outs[7]))
    wo_other = swap_x(lax.dynamic_index_in_dim(attn_full, attn_host[3], 0, keepdims=False))

    gain_two = gains_full[1:2]
    middles, hiddens, acts, pres, grads, grads_other = [], [], [], [], [], []
    for b in range(blocks):
        middle, hidden_two, act, grad_pre, grad_two, grad_low = mlp_block(
            hosts,
            b,
            mixed[b],
            mixed_other[b],
            attn_full,
            wo_other,
            tok_full,
            gain_two,
            cot_full,
            mlp_full,
        )
        middles.append(middle)
        hiddens.append(hidden_two)
        acts.append(act)
        pres.append(grad_pre)
        grads.append(grad_two)
        grads_other.append(swap_x(grad_low))
    mlp_sum_in = mlp_grads(hosts, hiddens, cot_full, pres, acts)
    mlp_sum = lax.psum_scatter(
        mlp_sum_in.reshape(OWNER_GROUPS * D, quarter), "dp", scatter_dimension=0, tiled=True
    )
    out_rows = []
    for b in range(blocks):
        partial = mlp_out(hosts, acts[b], mlp_full)
        received = swap_x(side_of(partial, 1 - side).astype(bf16))
        out_rows.append(
            (side_of(middles[b], side) + side_of(partial, side) + received.astype(f32)).astype(bf16)
        )
    block_out = jnp.concatenate(out_rows, axis=0)

    lows, grad_mids, gain_twos, grad_blocks, parts, ctx_parts = [], [], [], [], [], []
    for b in range(blocks):
        outs = attend_backward(
            hosts,
            b,
            grads[b],
            grads_other[b],
            cot_full,
            middles[b],
            gain_two,
            attn_full,
            kept[b],
            width,
        )
        lows.append(outs[0])
        grad_mids.append(side_of(outs[1], side))
        gain_twos.append(side_of(outs[2], side))
        grad_blocks.append(list(outs[3:8]) + [mixed[b]])
        parts.append(outs[8])
        ctx_parts.append(outs[9])
    ctx_part = jnp.stack(ctx_parts)
    ctx_received = swap_x(side_of(ctx_part, 1 - side).astype(bf16))
    grad_context = side_of(ctx_part, side) + ctx_received.astype(f32)
    handed_back = lax.ppermute(
        grad_context[0].astype(bf16), "dp", [(i + 1, i) for i in range(dp_count - 1)]
    ).astype(f32)
    grad_tails = jnp.concatenate([grad_context[1:], handed_back[None]], axis=0)
    tail_grad_lanes = to_lanes(grad_tails.reshape(blocks * CTX, width), blocks, CTX)
    attn_sum_in = attn_grads(hosts, hidden_full, context_full, lows, grad_blocks, width)
    attn_sum = lax.psum_scatter(
        attn_sum_in.reshape(OWNER_GROUPS * D, width), "dp", scatter_dimension=0, tiled=True
    )

    own_back, device_back = plain(back_total_kernel, 3, [state_shape, state_shape], 10**9)(
        seg_ext, tail_grad_lanes, rate_lanes, reading_lanes
    )
    back_all = gather_dp(device_back[:, :4].reshape(STATE, width).astype(bf16))
    grad_c_lanes, grad_a_lanes, sens_end = plain(sens_kernel, 4, [state_shape] * 3, 8 * 10**9)(
        seg_ext, hidden_lanes, tail_grad_lanes, state_starts, rate_lanes
    )
    gap_after = places - dp_here - 1
    use_after = jnp.logical_and(gap_after >= 0, ids_all[:, 1] == seg[rows - 1].astype(f32))
    power_after = jnp.exp(
        -decay_rate[None] * (rows * jnp.maximum(gap_after, 0)).astype(f32)[:, None, None]
    )
    later = jnp.sum(
        jnp.where(use_after[:, None, None], power_after * back_all.astype(f32), 0.0), axis=0
    )
    grad_lanes, grad_a_lanes = plain(
        back_scan_kernel, 7, [sds((BL, 8, 128), f32), state_shape], 4 * 10**9
    )(
        seg_ext,
        tail_grad_lanes,
        own_back,
        doubled(later),
        sens_end,
        grad_a_lanes,
        rate_lanes,
        reading_lanes,
    )
    grad_channels = from_lanes(grad_lanes, blocks, BL).reshape(rows, width)

    part = jnp.concatenate(parts, axis=0)
    received = swap_x(side_of(part, 1 - side).astype(bf16))
    scaled_full_weight = hidden_scaled(tok_full, inverse_one, gains_full[0])
    row_here = jnp.sum(part * scaled_full_weight, axis=1) + jnp.sum(
        grad_channels * (scaled_own * norm_gains[0]), axis=1
    )
    row_total = row_here + swap_x(row_here)
    grad_hidden = side_of(part, side) + received.astype(f32) + grad_channels
    grad_tokens = jnp.concatenate(grad_mids, axis=0) + inverse_one[:, None] * (
        grad_hidden * norm_gains[0] - scaled_own * (row_total / D)[:, None]
    )
    gain_one = jnp.sum(grad_hidden * scaled_own, axis=0)
    gain_two_sum = sum(gain_twos)[0]

    def merged(values):
        return sum(values[:, 4 * b : 4 * b + 4] for b in range(blocks)).reshape(STATE, width)

    small = total_dp(
        jnp.concatenate(
            [merged(grad_c_lanes), merged(grad_a_lanes), gain_one[None], gain_two_sum[None]], axis=0
        )
    )
    grad_c, grad_a = small[:STATE], small[STATE : 2 * STATE]
    gains_grad = small[2 * STATE :]
    decay_step = jnp.exp(-decay_rate)
    grad_read = grad_c * drive_root * param_lanes[1]
    grad_drive = grad_c * drive_root * param_lanes[2]
    grad_a = grad_a - grad_c * param_lanes[1] * param_lanes[2] * decay_step / drive_root
    grad_log = -decay_rate * decay_step * grad_a
    ssm_grad = jnp.stack([grad_log, grad_drive, grad_read]).transpose(0, 2, 1)

    attn_back = move(attn_sum, attn_way, ATTN_WAYS, True)
    mlp_back = move(mlp_sum, mlp_way, MLP_WAYS, True)
    attn_grad = jnp.stack(
        [
            jnp.where(attn_here >= 1, attn_sum.astype(f32), 0.0),
            jnp.where(attn_here == 2, attn_back.astype(f32), 0.0),
        ]
    )
    mlp_grad = jnp.where(
        mlp_here == 1, jnp.concatenate([mlp_sum, mlp_back], axis=1).astype(f32), 0.0
    )[None]

    attn_table = slot_rates(
        attn_owner,
        [0.5 * D ** (-0.5)] * 3 + [0.5 * (D // 16) ** (-0.5)],
        attn_master.shape[0],
        0.5 * D ** (-0.5),
    )
    mlp_table = slot_rates(
        mlp_owner, [0.5 * D ** (-0.5), 0.5 * FF ** (-0.5)], mlp_master.shape[0], 0.5 * D ** (-0.5)
    )
    attn_rates = lax.dynamic_index_in_dim(attn_table, group, 1, keepdims=False)[:, None, None]
    mlp_rates = lax.dynamic_index_in_dim(mlp_table, group, 1, keepdims=False)[:, None, None]
    ssm_rates = jnp.asarray([1.0, 0.8, 0.25], f32)[:, None, None]
    gain_rates = jnp.asarray([0.6, 0.6], f32)[:, None]
    attn_one, attn_two, attn_new = adam_step(
        attn_grad, attn_first, attn_second, attn_master, attn_rates, matrix_decay
    )
    mlp_one, mlp_two, mlp_new = adam_step(
        mlp_grad, mlp_first, mlp_second, mlp_master, mlp_rates, matrix_decay
    )
    ssm_one, ssm_two, ssm_new = adam_step(
        ssm_grad, ssm_first, ssm_second, ssm_params, ssm_rates, 0.0
    )
    gain_first_new, gain_second_new, gains_new = adam_step(
        gains_grad, gains_first, gains_second, norm_gains, gain_rates, 0.0
    )
    return (
        block_out.reshape(tokens.shape),
        grad_tokens.reshape(tokens.shape),
        attn_grad,
        attn_one,
        attn_two,
        attn_new,
        attn_new.astype(bf16),
        mlp_grad,
        mlp_one,
        mlp_two,
        mlp_new,
        mlp_new.astype(bf16),
        ssm_grad,
        ssm_one,
        ssm_two,
        ssm_new,
        gains_grad,
        gain_first_new,
        gain_second_new,
        gains_new,
    )


def hidden_scaled(tok_full, inverse_one, gain):
    return tok_full.astype(f32) * inverse_one[:, None] * gain[None]


def solution(mesh):
    in_specs = (
        P(None, "dp", "tensor"),
        P(None, "dp", "tensor"),
        P(None, "dp"),
        P(),
        P(None, "dp", "tensor"),
        P(None, "dp", "tensor"),
        P(None, "dp", "tensor"),
        P(None, "dp", "tensor"),
        P(None, "dp", "tensor"),
        P(None, "dp", "tensor"),
        P(None, "tensor", None),
        P(None, "tensor", None),
        P(None, "tensor", None),
        P(None, "tensor"),
        P(None, "tensor"),
        P(None, "tensor"),
    )
    out_specs = (
        P(None, "dp", "tensor"),
        P(None, "dp", "tensor"),
        P(None, "dp", "tensor"),
        P(None, "dp", "tensor"),
        P(None, "dp", "tensor"),
        P(None, "dp", "tensor"),
        P(None, "dp", "tensor"),
        P(None, "dp", "tensor"),
        P(None, "dp", "tensor"),
        P(None, "dp", "tensor"),
        P(None, "dp", "tensor"),
        P(None, "dp", "tensor"),
        P(None, "tensor", None),
        P(None, "tensor", None),
        P(None, "tensor", None),
        P(None, "tensor", None),
        P(None, "tensor"),
        P(None, "tensor"),
        P(None, "tensor"),
        P(None, "tensor"),
    )
    return jax.shard_map(body, mesh=mesh, in_specs=in_specs, out_specs=out_specs, check_vma=False)
```

time: 1840 us -> 561 us (0.30)
  waiting for transfers between devices: 784 us -> 105 us
  local copies, waits for them, and re-layouts: 342 us -> 60.9 us
  other arithmetic: 331 us -> 119 us
  matrix products: 203 us -> 0 us
  Pallas kernels: 0 us -> 185 us
  blocking collectives: 127 us -> 0 us
  starting transfers between devices: 6.89 us -> 59.3 us
    reduce_scatter x6 -> x2, waiting for transfers between devices: 603 us -> 0.01 us  [the longest x1 0.01 us: body(): lax.psum_scatter(attn_sum_in.reshape(OWNER_GROUPS * D, width), 'dp', scat...]
    dot_general x46 -> x0, matrix products: 203 us -> none  [the longest x8 37.3 us: contract_rows(): lax.dot_general(left, right, (((0,), (0,)), ((), ())), preferred_element_...]
    pallas_call x0 -> x15, Pallas kernels: none -> 185 us  [the longest x2 37.6 us: mlp_block(): call(mlp_kernel, (2 * per,), [whole((BL, half_width)), whole((BL, half_wi...]
    all_gather x6 -> x2, waiting for transfers between devices: 180 us -> 0.01 us  [the longest x1 0.01 us: body(): attn_full = lax.all_gather(attn_block, 'dp', axis=0, tiled=True)]
    ppermute x3 -> x34, waiting for transfers between devices: 0.01 us -> 105 us  [the longest x4 40.7 us: branch(): return lambda v: lax.ppermute(v, 'dp', pairs)]
    all_gather x4 -> x0, blocking collectives: 76.5 us -> none  [the longest x2 44 us: entering(): lax.all_gather(part.astype(kind), axis)]
    dot_general x32 -> x0, other arithmetic: 66.1 us -> none  [advance(): collected = jnp.einsum('jcn,jc->cn', weighted, span_in, precision=highest)]
    while x150 -> x0, local copies, waits for them, and re-layouts: 65.7 us -> none
  transfers between devices with their start and end apart: 16 -> 38, of which waited for: 7 -> 19; matrix products, arithmetic and copies ran while one was open for 35% -> 28% of each run, Pallas kernels for 0% -> 28%
where the time goes in v1:
time: 561 us; the launch traced here: 553 us
  Pallas kernels  185 us (33%)
  other arithmetic  119 us (21%)
  waiting for transfers between devices  105 us (19%)
  local copies, waits for them, and re-layouts  60.9 us (11%)
  starting transfers between devices  59.3 us (11%)
  between operations  23.5 us (4%)
    ppermute x4, waiting for transfers between devices, branch(): return lambda v: lax.ppermute(v, 'dp', pairs)  40.7 us
    pallas_call x2, Pallas kernels, mlp_block(): call(mlp_kernel, (2 * per,), [whole((BL, half_width)), whole((BL, half_wi...  37.6 us
    pallas_call x2, Pallas kernels, attend_backward(): call(attend_back_kernel, (pairs,), [whole((BL, D)), whole((BL, D)), pl.Bl...  34.2 us
    ppermute x15, waiting for transfers between devices, swap_x(): return lax.ppermute(values, 'tensor', SWAP)  30.7 us
    ppermute x8, waiting for transfers between devices, gather_dp(): other = lax.ppermute(held, 'dp', [(i, i ^ step) for i in range(count)])  26.8 us
    pallas_call x2, Pallas kernels, attend_forward(): call(attend_kernel, (pairs,), [pl.BlockSpec((BL, D), lambda p, s: (block,...  24.3 us
    pallas_call x1, Pallas kernels, mlp_grads(): call(mlp_grad_kernel, (2, 2 * per), [whole((BL, D)), whole((BL, D)), pl.B...  20.8 us
    ppermute x15, starting transfers between devices, swap_x(): return lax.ppermute(values, 'tensor', SWAP)  19.3 us
  transfers between devices with their start and end apart: 38, of which 19 were waited for; matrix products, arithmetic and copies ran while one was open for 28% of the time, Pallas kernels for 28%

profile of v1, /device:TPU:0, one launch (start us, length us, event | category | flops | bytes accessed | tf_op | source)
XLA Modules:
  0.0 552.9 jit_solution(9099555892635310888)
XLA Ops:
  14.4 11.5 %conditional.7 = (bf16[256,512]{1,0:T(8,128)(2,1)}) conditional(s32[]{:T(128)} %clamp.8, bf16[256,512]{1,0:T(8,128)(2,1)S(1)} %slice_bitcast_fusion.1, bf16[256,512]{1,0:T(8,128)(2,1)S(1)} %slice_bitcast_fusion.1, bf16[256,512]{1,0:T(8,128)(2,1)S(1)} %slice_bitcast_fusion.1, ...), branch_computations={%region_10.11_spmd, %region_11.12_spmd, %region_12.13_spmd, %regio... | conditional | bytes 1048624 | solution.py:164
  14.5 6.6 %collective-permute-start.1 = (bf16[256,512]{1,0:T(8,128)(2,1)S(1)}, bf16[256,512]{1,0:T(8,128)(2,1)}, u32[]{:S(2)}, u32[]{:S(2)}) collective-permute-start(bf16[256,512]{1,0:T(8,128)(2,1)S(1)} %param.1), channel_id=1, source_target_pairs={{0,16},{2,18},{4,20},{6,22},{1,17},{3,19},{5,21},{7,23}} | collective-permute-start | bytes 786440 | tf_op jit(solution)/shard_map/cond/branch_1_fun/ppermute | solution.py:162
  21.1 4.9 collective-permute-done.1
  30.6 18.5 %conditional.8 = (bf16[256,1024]{1,0:T(8,128)(2,1)}) conditional(s32[]{:T(128)} %clamp.9, bf16[256,1024]{1,0:T(8,128)(2,1)S(1)} %slice.216, bf16[256,1024]{1,0:T(8,128)(2,1)S(1)} %slice.216, bf16[256,1024]{1,0:T(8,128)(2,1)S(1)} %slice.216, bf16[256,1024]{1,0:T(8,128)(2,1)S(1)} %slice.216, ...), branch_computations={%region_29.30_spmd, %region_30.31_spmd, %region_31.32_spmd, %regio... | conditional | bytes 2097200 | solution.py:164
  30.6 2.1 collective-permute-start.20
  32.7 16.3 %collective-permute-done.20 = bf16[256,1024]{1,0:T(8,128)(2,1)} collective-permute-done((bf16[256,1024]{1,0:T(8,128)(2,1)S(1)}, bf16[256,1024]{1,0:T(8,128)(2,1)}, u32[]{:S(2)}, u32[]{:S(2)}) %collective-permute-start.20) | collective-permute-done | bytes 524320 | tf_op jit(solution)/shard_map/cond/branch_2_fun/ppermute | solution.py:162
  67.8 8.6 %shard_map.401 = (f32[128,8,128]{2,1,0:T(8,128)}, f32[16,8,128]{2,1,0:T(8,128)}, f32[16,8,128]{2,1,0:T(8,128)}) custom-call(s32[1025]{0:T(1024)} %pad_add_fusion.seg_ref, f32[512,8,128]{2,1,0:T(8,128)} %bitcast.174, f32[16,8,128]{2,1,0:T(8,128)} %get-tuple-element.308.rate_ref, f32[16,8,128]{2,1,0:T(8,128)} %get-tuple-element.309.c_ref), custom_call_target="tpu_custom_call" | custom-call | flops 4000000000 | bytes 4000000 | tf_op jit(solution)/shard_map/pallas_call | solution.py:951
  79.2 3.8 collective-permute-start.53
  85.1 7.2 %collective-permute-start.54 = (bf16[4,16,640]{2,1,0:T(8,128)(2,1)S(1)}, bf16[4,16,640]{2,1,0:T(8,128)(2,1)S(1)}, u32[]{:S(2)}, u32[]{:S(2)}) collective-permute-start(bf16[4,16,640]{2,1,0:T(8,128)(2,1)S(1)} %maximum_select_fusion.6), channel_id=1, source_target_pairs={{0,8},{2,10},{4,12},{6,14},{8,0},{10,2},{12,4},{14,6},{16,24},{18,... | collective-permute-start | bytes 245768 | tf_op jit(solution)/shard_map/ppermute | solution.py:82
  92.9 1.9 collective-permute-done.54
  95.5 3.4 collective-permute-start.55
  101.7 14.5 %collective-permute-done.55 = bf16[8,16,640]{2,1,0:T(8,128)(2,1)} collective-permute-done((bf16[8,16,640]{2,1,0:T(8,128)(2,1)}, bf16[8,16,640]{2,1,0:T(8,128)(2,1)}, u32[]{:S(2)}, u32[]{:S(2)}) %collective-permute-start.55) | collective-permute-done | bytes 163872 | tf_op jit(solution)/shard_map/ppermute | solution.py:82
  116.2 2.1 pad_maximum_fusion.3
  118.2 3.8 copy.97
  122.0 3.8 copy.96
  125.8 2.8 broadcast_select_fusion
  129.2 14.8 %select_reduce_fusion.1 = f32[16,512]{0,1:T(8,128)} fusion(bf16[16,16,640]{0,1,2:T(8,128)(2,1)S(1)} %broadcast_select_fusion, f32[16]{0:T(128)S(1)} %copy-done.29, f32[16,512]{0,1:T(8,128)S(1)} %copy.98, pred[16]{0:T(512)(128)(4,1)S(1)} %get-tuple-element.298), kind=kLoop, calls=%fused_computation.4 | loop fusion | flops 647168 | bytes 327760 | tf_op jit(solution)/shard_map/reduce_sum | solution.py:967
  145.7 3.0 shard_map.402
  151.1 2.1 collective-permute-start.56
  164.7 5.4 collective-permute-done.57
  171.1 1.8 fusion.3
  172.9 1.9 maximum_select_fusion.hid_ref.refs_0_.refs_1_
  174.8 3.6 maximum_select_fusion.1.tok_ref
  178.4 4.5 maximum_select_fusion.2.cot_ref.g0.g1
  185.5 12.2 %shard_map.403 = (bf16[512,512]{1,0:T(8,128)(2,1)}, bf16[512,512]{1,0:T(8,128)(2,1)}, bf16[512,512]{1,0:T(8,128)(2,1)}, bf16[128,512]{1,0:T(8,128)(2,1)}, bf16[1...) custom-call(s32[8]{0:T(128)} %pad_add_fusion.4.host_ref, ...), custom_call_target="tpu_custom_call" | custom-call | flops 8000000000 | bytes 12000000 | tf_op jit(solution)/shard_map/pallas_call | solution.py:402
  198.5 12.1 %shard_map.406 = (bf16[512,512]{1,0:T(8,128)(2,1)}, bf16[512,512]{1,0:T(8,128)(2,1)}, bf16[512,512]{1,0:T(8,128)(2,1)}, bf16[128,512]{1,0:T(8,128)(2,1)}, bf16[1...) custom-call(s32[8]{0:T(128)} %pad_add_fusion.4.host_ref, ...), custom_call_target="tpu_custom_call" | custom-call | flops 8000000000 | bytes 12000000 | tf_op jit(solution)/shard_map/pallas_call | solution.py:402
  211.9 9.7 %collective-permute-done.58.other_ref = bf16[512,512]{1,0:T(8,128)(2,1)} collective-permute-done((bf16[512,512]{1,0:T(8,128)(2,1)}, bf16[512,512]{1,0:T(8,128)(2,1)}, u32[]{:S(2)}, u32[]{:S(2)}) %collective-permute-start.58) | collective-permute-done | bytes 524320 | tf_op jit(solution)/shard_map/ppermute | solution.py:73
  221.6 18.8 %shard_map.404 = (f32[512,1024]{1,0:T(8,128)}, bf16[512,1024]{1,0:T(8,128)(2,1)}, bf16[512,2048]{1,0:T(8,128)(2,1)}, bf16[512,2048]{1,0:T(8,128)(2,1)}, f32[512,1024]{1,0:T(8,128)}, /*index=5*/bf16[512,1024]{1,0:T(8,128)(2,1)}) custom-call(s32[8]{0:T(128)} %pad_add_fusion.4.host_ref, bf16[512,512]{1,0:T(8,128)(2,1)} %get-tuple-element.191.own_ref.refs_11_, ...), custom_call_target="tpu_custom_call" | custom-call | flops 8000000000 | bytes 24000000 | tf_op jit(solution)/shard_map/pallas_call | solution.py:721
  241.7 18.8 %shard_map.407 = (f32[512,1024]{1,0:T(8,128)}, bf16[512,1024]{1,0:T(8,128)(2,1)}, bf16[512,2048]{1,0:T(8,128)(2,1)}, bf16[512,2048]{1,0:T(8,128)(2,1)}, f32[512,1024]{1,0:T(8,128)}, /*index=5*/bf16[512,1024]{1,0:T(8,128)(2,1)}) custom-call(s32[8]{0:T(128)} %pad_add_fusion.4.host_ref, bf16[512,512]{1,0:T(8,128)(2,1)} %get-tuple-element.194.own_ref.refs_17_, ...), custom_call_target="tpu_custom_call" | custom-call | flops 8000000000 | bytes 24000000 | tf_op jit(solution)/shard_map/pallas_call | solution.py:721
  261.4 5.2 collective-permute-done.64.other_ref
  267.6 17.3 %shard_map.409 = (bf16[512,1024]{1,0:T(8,128)(2,1)}, f32[512,1024]{1,0:T(8,128)}, f32[1,1024]{1,0:T(1,128)}, bf16[512,512]{1,0:T(8,128)(2,1)}, bf16[512,512]{1,0...) custom-call(s32[8]{0:T(128)} %pad_add_fusion.4.host_ref, ...), custom_call_target="tpu_custom_call" | custom-call | flops 12000000000 | bytes 20000000 | tf_op jit(solution)/shard_map/pallas_call | solution.py:534
  284.9 1.9 collective-permute-done.65.other_ref
  287.7 16.9 %shard_map.410 = (bf16[512,1024]{1,0:T(8,128)(2,1)}, f32[512,1024]{1,0:T(8,128)}, f32[1,1024]{1,0:T(1,128)}, bf16[512,512]{1,0:T(8,128)(2,1)}, bf16[512,512]{1,0...) custom-call(s32[8]{0:T(128)} %pad_add_fusion.4.host_ref, ...), custom_call_target="tpu_custom_call" | custom-call | flops 12000000000 | bytes 20000000 | tf_op jit(solution)/shard_map/pallas_call | solution.py:534
  304.7 12.0 %shard_map.414 = bf16[4,1024,512]{2,1,0:T(8,128)(2,1)} custom-call(s32[8]{0:T(128)} %pad_add_fusion.4.host_ref, bf16[1024,1024]{1,0:T(8,128)(2,1)} %maximum_select_fusion.hid_ref.refs_0_.refs_1_, bf16[1024,1024]{1,0:T(8,128)(2,1)} %maximum_select_fusion.hid_ref.refs_0_.refs_1_, bf16[256,1024]{1,0:T(8,128)(2,1)} %maximum_select_fusion.3.ctx_ref.refs_2_.refs_3_, ...), custom_call_target="tpu_custom_call" | custom-call | flops 4600000000 | bytes 14000000 | tf_op jit(solution)/shard_map/pallas_call | solution.py:646
  316.8 20.8 %shard_map.415 = bf16[4,1024,1024]{2,1,0:T(8,128)(2,1)} custom-call(s32[8]{0:T(128)} %pad_add_fusion.4.host_ref, bf16[512,1024]{1,0:T(8,128)(2,1)} %get-tuple-element.239.h0, bf16[512,1024]{1,0:T(8,128)(2,1)} %get-tuple-element.240.h1, bf16[1024,1024]{1,0:T(8,128)(2,1)} %maximum_select_fusion.2.cot_ref.g0.g1, ...), custom_call_target="tpu_custom_call" | custom-call | flops 8600000512 | bytes 20000000 | tf_op jit(solution)/shard_map/pallas_call | solution.py:776
  339.7 9.4 %shard_map.405 = f32[512,1024]{1,0:T(8,128)} custom-call(s32[8]{0:T(128)} %pad_add_fusion.4.host_ref, bf16[512,2048]{1,0:T(8,128)(2,1)} %get-tuple-element.193.a_ref.a0, bf16[4,1024,1024]{2,1,0:T(8,128)(2,1)} %bitcast.165), custom_call_target="tpu_custom_call" | custom-call | flops 2200000000 | bytes 8000000 | tf_op jit(solution)/shard_map/pallas_call | solution.py:814
  349.1 2.1 dynamic-slice_convert_fusion.2
  352.5 9.3 %shard_map.408 = f32[512,1024]{1,0:T(8,128)} custom-call(s32[8]{0:T(128)} %pad_add_fusion.4.host_ref, bf16[512,2048]{1,0:T(8,128)(2,1)} %get-tuple-element.196.a_ref.a1, bf16[4,1024,1024]{2,1,0:T(8,128)(2,1)} %bitcast.166), custom_call_target="tpu_custom_call" | custom-call | flops 2200000000 | bytes 8000000 | tf_op jit(solution)/shard_map/pallas_call | solution.py:814
  361.8 2.2 dynamic-slice_convert_fusion.1
  368.0 2.6 copy-done.5
  373.3 8.1 %collective-permute-done.67 = bf16[2,128,512]{2,1,0:T(8,128)(2,1)S(1)} collective-permute-done((bf16[2,128,512]{2,1,0:T(8,128)(2,1)S(1)}, bf16[2,128,512]{2,1,0:T(8,128)(2,1)S(1)}, u32[]{:S(2)}, u32[]{:S(2)}) %collective-permute-start.67) | collective-permute-done | bytes 262176 | tf_op jit(solution)/shard_map/ppermute | solution.py:73
  385.2 1.7 concatenate.192
  387.0 1.7 reshape.548
  388.7 1.9 pad_maximum_fusion.1
  390.6 3.0 shard_map.411
  395.7 2.3 constant_dynamic-slice_fusion.3
  399.3 3.2 collective-permute-done.70
  402.6 14.5 %shard_map.412 = (f32[16,8,128]{2,1,0:T(8,128)}, f32[16,8,128]{2,1,0:T(8,128)}, f32[16,8,128]{2,1,0:T(8,128)}) custom-call(s32[1025]{0:T(1024)} %pad_add_fusion.seg_ref, f32[512,8,128]{2,1,0:T(8,128)} %bitcast.175, f32[128,8,128]{2,1,0:T(8,128)} %bitcast.191, f32[16,8,128]{2,1,0:T(8,128)} %get-tuple-element.223.start_ref, ...), custom_call_target="tpu_custom_call" | custom-call | flops 8000000000 | bytes 4000000 | tf_op jit(solution)/shard_map/pallas_call | solution.py:1068
  419.3 5.7 %collective-permute-done.72 = bf16[8,16,512]{2,1,0:T(8,128)(2,1)S(1)} collective-permute-done((bf16[8,16,512]{2,1,0:T(8,128)(2,1)S(1)}, bf16[8,16,512]{2,1,0:T(8,128)(2,1)S(1)}, u32[]{:S(2)}, u32[]{:S(2)}) %collective-permute-start.72) | collective-permute-done | bytes 131104 | tf_op jit(solution)/shard_map/ppermute | solution.py:82
  425.9 4.4 copy.105
  430.3 4.4 copy.104
  434.8 15.9 %select_reduce_fusion = f32[16,512]{0,1:T(8,128)} fusion(bf16[16,16,512]{0,1,2:T(8,128)(2,1)} %copy.104, bf16[16,16,512]{0,1,2:T(8,128)(2,1)} %copy.105, f32[16]{0:T(128)} %get-tuple-element.304, f32[16,512]{0,1:T(8,128)S(1)} %copy.98, pred[]{:T(512)S(6)} %eq.233, pred[16]{0:T(512)(128)(4,1)} %get-tuple-element.297), kind=kLoop, calls=%fused_computation.3 | loop fusion | flops 778240 | bytes 589905 | tf_op jit(solution)/shard_map/reduce_sum | solution.py:1076
  452.4 8.6 %shard_map.413 = (f32[512,8,128]{2,1,0:T(8,128)}, f32[16,8,128]{2,1,0:T(8,128)}) custom-call(s32[1025]{0:T(1024)} %pad_add_fusion.seg_ref, f32[128,8,128]{2,1,0:T(8,128)} %bitcast.192, f32[16,8,128]{2,1,0:T(8,128)} %get-tuple-element.221.own_ref, f32[16,8,128]{2,1,0:T(8,128)} %pad_maximum_fusion.11.later_ref, f32[16,8,128]{2,1,0:T(8,128)} %get-tuple-element.224.z_ref, ...), custom_call_target="tpu_custom_call" | custom-call | flops 4000000000 | bytes 4000000 | tf_op jit(solution)/shard_map/pallas_call | solution.py:1079
  461.0 16.0 %fusion.11 = f32[2,512]{1,0:T(2,128)S(1)} fusion(f32[2,512,4,128]{3,2,1,0:T(4,128)S(1)} %reshape.543, f32[4,128]{1,0:T(4,128)S(1)} %bitcast.221, f32[2,512]{1,0:T(2,128)S(1)} %mul.490, f32[512,2,4,128]{3,2,1,0:T(4,128)} %bitcast.170), kind=kLoop, calls=%fused_computation.25 | loop fusion | flops 2096128 | bytes 4204544 | tf_op jit(solution)/shard_map/reduce_sum | solution.py:1096
  477.0 4.2 collective-permute-start.73
  484.4 3.8 fusion.8
  492.5 3.3 collective-permute-done.75
  500.4 4.3 collective-permute-start.77
  509.4 9.7 %conditional.9 = (bf16[256,512]{1,0:T(8,128)(2,1)}) conditional(s32[]{:T(128)} %clamp.8, bf16[256,512]{1,0:T(8,128)(2,1)} %reduce-scatter.3.cloned.1.call-done, bf16[256,512]{1,0:T(8,128)(2,1)} %reduce-scatter.3.cloned.1.call-done, bf16[256,512]{1,0:T(8,128)(2,1)} %reduce-scatter.3.cloned.1.call-done, ...), branch_computations={%region_39.40_spmd, %region_40.41_spmd, %region_41.42_spmd, %regio... | conditional | bytes 1048624
  510.7 8.2 %collective-permute-done.25 = bf16[256,512]{1,0:T(8,128)(2,1)} collective-permute-done((bf16[256,512]{1,0:T(8,128)(2,1)}, bf16[256,512]{1,0:T(8,128)(2,1)}, u32[]{:S(2)}, u32[]{:S(2)}) %collective-permute-start.25) | collective-permute-done | bytes 262176 | tf_op jit(solution)/shard_map/cond/branch_1_fun/ppermute | solution.py:162
  521.2 4.3 fusion.44
  525.5 12.6 %conditional.10 = (bf16[1,256,1024]{2,1,0:T(8,128)(2,1)}) conditional(s32[]{:T(128)} %clamp.9, bf16[256,1024]{1,0:T(8,128)(2,1)} %reduce-scatter.5.cloned.1.call-done, bf16[256,1024]{1,0:T(8,128)(2,1)} %reduce-scatter.5.cloned.1.call-done, bf16[256,1024]{1,0:T(8,128)(2,1)} %reduce-scatter.5.cloned.1.call-done, ...), branch_computations={%region_60.61_spmd, %region_61.62_spmd, %region_62.63_spmd, %regio... | conditional | bytes 2097200 | solution.py:164
  526.8 11.4 %collective-permute-done.44 = bf16[256,1024]{1,0:T(8,128)(2,1)} collective-permute-done((bf16[256,1024]{1,0:T(8,128)(2,1)}, bf16[256,1024]{1,0:T(8,128)(2,1)}, u32[]{:S(2)}, u32[]{:S(2)}) %collective-permute-start.44) | collective-permute-done | bytes 524320 | tf_op jit(solution)/shard_map/cond/branch_2_fun/ppermute | solution.py:162
  538.1 7.8 %fusion.42 = (bf16[1,256,2048]{2,1,0:T(8,128)(2,1)}, f32[1,256,2048]{2,1,0:T(8,128)}, f32[1,256,2048]{2,1,0:T(8,128)}, f32[1,256,2048]{2,1,0:T(8,128)}, f32[1,256,2048]{2,1,0:T(8,128)}) fusion(f32[1,256,2048]{2,1,0:T(8,128)S(1)} %copy-done.4, f32[]{:T(128)} %bitcast.68, f32[1,256,2048]{2,1,0:T(8,128)} %param.83, f32[1,256,2048]{2,1,0:T(8,128)} %param.82, ...), kind=kLoop, calls=%fused_computation.183 | loop fusion | flops 11010048 | bytes 16777220 | tf_op jit(solution)/shard_map/convert_element_type | solution.py:1173
  (286 shorter events, 99.9 us)
Async XLA Ops:
  7.2 20.8 %copy-start.3 = (f32[1,256,2048]{2,1,0:T(8,128)S(1)}, f32[1,256,2048]{2,1,0:T(8,128)}, u32[]{:S(2)}) copy-start(f32[1,256,2048]{2,1,0:T(8,128)} %param.81) | copy-start | bytes 6291460
  7.2 175.7 %all-gather.3.cloned.1.call-start = ((), (), s32[]{:S(2)}) async-start(), calls=%async_computation.2 | async-start | bytes 4456448 | tf_op jit(solution)/shard_map/all_gather | solution.py:897
  9.0 51.3 %copy-start.37 = (s32[4]{0:T(128)}, s32[4]{0:T(128)S(1)}, u32[]{:S(2)}) copy-start(s32[4]{0:T(128)S(1)} %get-tuple-element.251) | copy-start | bytes 52
  14.5 11.5 %collective-permute-start.1 = (bf16[256,512]{1,0:T(8,128)(2,1)S(1)}, bf16[256,512]{1,0:T(8,128)(2,1)}, u32[]{:S(2)}, u32[]{:S(2)}) collective-permute-start(bf16[256,512]{1,0:T(8,128)(2,1)S(1)} %param.1), channel_id=1, source_target_pairs={{0,16},{2,18},{4,20},{6,22},{1,17},{3,19},{5,21},{7,23}} | collective-permute-start | bytes 786440 | tf_op jit(solution)/shard_map/cond/branch_1_fun/ppermute | solution.py:162
  26.7 194.9 %all-gather.5.cloned.1.call-start = ((), (), s32[]{:S(2)}) async-start(), calls=%async_computation.3 | async-start | bytes 8912896 | tf_op jit(solution)/shard_map/all_gather | solution.py:898
  28.2 21.8 %copy-start.22 = (s32[1,1024]{1,0:T(1,128)S(1)}, s32[1,1024]{1,0:T(1,128)}, u32[]{:S(2)}) copy-start(s32[1,1024]{1,0:T(1,128)} %param.76) | copy-start | bytes 12292
  28.2 23.6 %copy-start = (bf16[1,1024,512]{2,1,0:T(8,128)(2,1)S(1)}, bf16[1,1024,512]{2,1,0:T(8,128)(2,1)}, u32[]{:S(2)}) copy-start(bf16[1,1024,512]{2,1,0:T(8,128)(2,1)} %param.74) | copy-start | bytes 3145732
  28.2 29.9 %copy-start.16 = (f32[3,512,16]{1,2,0:T(8,128)S(1)}, f32[3,512,16]{1,2,0:T(8,128)}, u32[]{:S(2)}) copy-start(f32[3,512,16]{1,2,0:T(8,128)} %param.84) | copy-start | bytes 294916
  28.2 30.7 %copy-start.31 = (s32[18,4]{0,1:T(4,128)S(1)}, s32[18,4]{0,1:T(4,128)}, u32[]{:S(2)}) copy-start(s32[18,4]{0,1:T(4,128)} %constant.220.clone) | copy-start | bytes 868
  30.6 18.4 %collective-permute-start.20 = (bf16[256,1024]{1,0:T(8,128)(2,1)S(1)}, bf16[256,1024]{1,0:T(8,128)(2,1)}, u32[]{:S(2)}, u32[]{:S(2)}) collective-permute-start(bf16[256,1024]{1,0:T(8,128)(2,1)S(1)} %param.20), channel_id=1, source_target_pairs={{0,8},{2,10},{4,12},{6,14},{24,16},{26,18},{28,20},{30,22},{1,9},{... | collective-permute-start | bytes 1572872 | tf_op jit(solution)/shard_map/cond/branch_2_fun/ppermute | solution.py:162
  49.1 11.3 %copy-start.36 = (s32[6]{0:T(128)S(1)}, s32[6]{0:T(128)}, u32[]{:S(2)}) copy-start(s32[6]{0:T(128)} %param.77) | copy-start | bytes 76
  50.0 459.4 %reduce-scatter.3.cloned.1.call-start = ((), (), s32[]{:S(2)}) async-start(), calls=%async_computation.4 | async-start | bytes 4456448 | tf_op jit(solution)/shard_map/reduce_scatter | solution.py:1060
  50.5 12.3 %collective-permute-start.51 = (s32[128]{0:T(128)S(1)}, s32[128]{0:T(128)S(1)}, u32[]{:S(2)}, u32[]{:S(2)}) collective-permute-start(s32[128]{0:T(128)S(1)} %get-tuple-element.292), channel_id=1, source_target_pairs={{0,2},{2,4},{4,6},{6,8},{8,10},{10,12},{12,14},{14,16},{16,18},{18... | collective-permute-start | bytes 1544 | tf_op jit(solution)/shard_map/ppermute | solution.py:920
  52.1 12.7 %collective-permute-start.48 = (f32[1024]{0:T(1024)S(1)}, f32[1024]{0:T(1024)S(1)}, u32[]{:S(2)}, u32[]{:S(2)}) collective-permute-start(f32[1024]{0:T(1024)S(1)} %fusion.9), channel_id=1, source_target_pairs={{0,1},{1,0},{2,3},{3,2},{4,5},{5,4},{6,7},{7,6},{8,9},{9,8},{10,11... | collective-permute-start | bytes 12296 | tf_op jit(solution)/shard_map/ppermute | solution.py:73
  53.4 109.2 %collective-permute-start.50 = (f32[2,512]{1,0:T(2,128)}, f32[2,512]{1,0:T(2,128)}, u32[]{:S(2)}, u32[]{:S(2)}) collective-permute-start(f32[2,512]{1,0:T(2,128)} %param.87), channel_id=1, source_target_pairs={{0,1},{1,0},{2,3},{3,2},{4,5},{5,4},{6,7},{7,6},{8,9},{9,8},{10,11... | collective-permute-start | bytes 12296 | tf_op jit(solution)/shard_map/ppermute | solution.py:73
  54.2 124.2 %collective-permute-start.60 = (bf16[1024,512]{1,0:T(8,128)(2,1)}, bf16[1024,512]{1,0:T(8,128)(2,1)}, u32[]{:S(2)}, u32[]{:S(2)}) collective-permute-start(bf16[1024,512]{1,0:T(8,128)(2,1)} %bitcast.38), channel_id=1, source_target_pairs={{0,1},{1,0},{2,3},{3,2},{4,5},{5,4},{6,7},{7,6},{8,9},{9,8},{10,11... | collective-permute-start | bytes 3145736 | tf_op jit(solution)/shard_map/ppermute | solution.py:73
  55.5 115.7 %collective-permute-start.49 = (bf16[1024,512]{1,0:T(8,128)(2,1)S(1)}, bf16[1024,512]{1,0:T(8,128)(2,1)}, u32[]{:S(2)}, u32[]{:S(2)}) collective-permute-start(bf16[1024,512]{1,0:T(8,128)(2,1)S(1)} %bitcast.167), channel_id=1, source_target_pairs={{0,1},{1,0},{2,3},{3,2},{4,5},{5,4},{6,7},{7,6},{8,9},{9,8},{10,11... | collective-permute-start | bytes 3145736 | tf_op jit(solution)/shard_map/ppermute | solution.py:73
  67.8 15.2 %copy-start.30 = (s32[6,4]{0,1:T(4,128)S(1)}, s32[6,4]{0,1:T(4,128)}, u32[]{:S(2)}) copy-start(s32[6,4]{0,1:T(4,128)} %constant.222.clone) | copy-start | bytes 292
  77.4 1.8 collective-permute-start.52
  79.2 5.9 %collective-permute-start.53 = (bf16[2,16,640]{2,1,0:T(8,128)(2,1)S(1)}, bf16[2,16,640]{2,1,0:T(8,128)(2,1)S(1)}, u32[]{:S(2)}, u32[]{:S(2)}) collective-permute-start(bf16[2,16,640]{2,1,0:T(8,128)(2,1)S(1)} %maximum_select_fusion.8), channel_id=1, source_target_pairs={{0,4},{2,6},{4,0},{6,2},{8,12},{10,14},{12,8},{14,10},{16,20},{18,... | collective-permute-start | bytes 122888 | tf_op jit(solution)/shard_map/ppermute | solution.py:82
  85.1 9.7 %collective-permute-start.54 = (bf16[4,16,640]{2,1,0:T(8,128)(2,1)S(1)}, bf16[4,16,640]{2,1,0:T(8,128)(2,1)S(1)}, u32[]{:S(2)}, u32[]{:S(2)}) collective-permute-start(bf16[4,16,640]{2,1,0:T(8,128)(2,1)S(1)} %maximum_select_fusion.6), channel_id=1, source_target_pairs={{0,8},{2,10},{4,12},{6,14},{8,0},{10,2},{12,4},{14,6},{16,24},{18,... | collective-permute-start | bytes 245768 | tf_op jit(solution)/shard_map/ppermute | solution.py:82
  95.5 20.6 %collective-permute-start.55 = (bf16[8,16,640]{2,1,0:T(8,128)(2,1)}, bf16[8,16,640]{2,1,0:T(8,128)(2,1)}, u32[]{:S(2)}, u32[]{:S(2)}) collective-permute-start(bf16[8,16,640]{2,1,0:T(8,128)(2,1)} %maximum_select_fusion.4), channel_id=1, source_target_pairs={{0,16},{2,18},{4,20},{6,22},{8,24},{10,26},{12,28},{14,30},{16,0},... | collective-permute-start | bytes 491528 | tf_op jit(solution)/shard_map/ppermute | solution.py:82
  145.7 10.1 %copy-start.23 = (s32[640]{0:T(1024)S(1)}, s32[640]{0:T(1024)}, u32[]{:S(2)}) copy-start(s32[640]{0:T(1024)} %pad_add_fusion.2) | copy-start | bytes 7684
  145.7 12.4 %copy-start.25 = (s32[1,512]{1,0:T(1,128)S(1)}, s32[1,512]{1,0:T(1,128)}, u32[]{:S(2)}) copy-start(s32[1,512]{1,0:T(1,128)} %get-tuple-element.289) | copy-start | bytes 6148
  145.7 12.4 %copy-start.46 = (s32[128]{0:T(128)S(1)}, s32[128]{0:T(128)}, u32[]{:S(2)}) copy-start(s32[128]{0:T(128)} %copy-done.45) | copy-start | bytes 1540
  151.1 9.1 %collective-permute-start.56 = (bf16[128,512]{1,0:T(8,128)(2,1)}, bf16[128,512]{1,0:T(8,128)(2,1)}, u32[]{:S(2)}, u32[]{:S(2)}) collective-permute-start(bf16[128,512]{1,0:T(8,128)(2,1)} %bitcast.157), channel_id=1, source_target_pairs={{0,2},{2,4},{4,6},{6,8},{8,10},{10,12},{12,14},{14,16},{16,18},{18... | collective-permute-start | bytes 393224 | tf_op jit(solution)/shard_map/ppermute | solution.py:977
  161.3 8.9 %collective-permute-start.57 = (bf16[256,512]{1,0:T(8,128)(2,1)S(1)}, bf16[256,512]{1,0:T(8,128)(2,1)S(1)}, u32[]{:S(2)}, u32[]{:S(2)}) collective-permute-start(bf16[256,512]{1,0:T(8,128)(2,1)S(1)} %bitcast.183), channel_id=1, source_target_pairs={{0,1},{1,0},{2,3},{3,2},{4,5},{5,4},{6,7},{7,6},{8,9},{9,8},{10,11... | collective-permute-start | bytes 786440 | tf_op jit(solution)/shard_map/ppermute | solution.py:73
  184.2 37.4 %collective-permute-start.59 = (bf16[1024,512]{1,0:T(8,128)(2,1)S(1)}, bf16[1024,512]{1,0:T(8,128)(2,1)}, u32[]{:S(2)}, u32[]{:S(2)}) collective-permute-start(bf16[1024,512]{1,0:T(8,128)(2,1)S(1)} %dynamic-slice_bitcast_fusion), channel_id=1, source_target_pairs={{0,1},{1,0},{2,3},{3,2},{4,5},{5,4},{6,7},{7,6},{8,9},{9,8},{10,11... | collective-permute-start | bytes 3145736 | tf_op jit(solution)/shard_map/ppermute | solution.py:73
  197.6 24.0 %collective-permute-start.58 = (bf16[512,512]{1,0:T(8,128)(2,1)}, bf16[512,512]{1,0:T(8,128)(2,1)}, u32[]{:S(2)}, u32[]{:S(2)}) collective-permute-start(bf16[512,512]{1,0:T(8,128)(2,1)} %get-tuple-element.191.own_ref.refs_11_), channel_id=1, source_target_pairs={{0,1},{1,0},{2,3},{3,2},{4,5},{5,4},{6,7},{7,6},{8,9},{9,8},{10,11... | collective-permute-start | bytes 1572872 | tf_op jit(solution)/shard_map/ppermute | solution.py:73
  210.7 31.0 %collective-permute-start.62 = (bf16[512,512]{1,0:T(8,128)(2,1)}, bf16[512,512]{1,0:T(8,128)(2,1)}, u32[]{:S(2)}, u32[]{:S(2)}) collective-permute-start(bf16[512,512]{1,0:T(8,128)(2,1)} %get-tuple-element.194.own_ref.refs_17_), channel_id=1, source_target_pairs={{0,1},{1,0},{2,3},{3,2},{4,5},{5,4},{6,7},{7,6},{8,9},{9,8},{10,11... | collective-permute-start | bytes 1572872 | tf_op jit(solution)/shard_map/ppermute | solution.py:73
  240.4 26.2 %collective-permute-start.64 = (bf16[512,1024]{1,0:T(8,128)(2,1)}, bf16[512,1024]{1,0:T(8,128)(2,1)S(1)}, u32[]{:S(2)}, u32[]{:S(2)}) collective-permute-start(bf16[512,1024]{1,0:T(8,128)(2,1)} %get-tuple-element.198), channel_id=1, source_target_pairs={{0,1},{1,0},{2,3},{3,2},{4,5},{5,4},{6,7},{7,6},{8,9},{9,8},{10,11... | collective-permute-start | bytes 3145736 | tf_op jit(solution)/shard_map/ppermute | solution.py:73
  260.4 26.3 %collective-permute-start.65 = (bf16[512,1024]{1,0:T(8,128)(2,1)}, bf16[512,1024]{1,0:T(8,128)(2,1)S(1)}, u32[]{:S(2)}, u32[]{:S(2)}) collective-permute-start(bf16[512,1024]{1,0:T(8,128)(2,1)} %get-tuple-element.208), channel_id=1, source_target_pairs={{0,1},{1,0},{2,3},{3,2},{4,5},{5,4},{6,7},{7,6},{8,9},{9,8},{10,11... | collective-permute-start | bytes 3145736 | tf_op jit(solution)/shard_map/ppermute | solution.py:73
  316.7 208.8 %reduce-scatter.5.cloned.1.call-start = ((), (), s32[]{:S(2)}) async-start(), calls=%async_computation.5 | async-start | bytes 8912896 | tf_op jit(solution)/shard_map/reduce_scatter | solution.py:1019
  351.2 13.5 %copy-start.14 = (f32[128,1024]{1,0:T(8,128)S(1)}, f32[128,1024]{1,0:T(8,128)}, u32[]{:S(2)}) copy-start(f32[128,1024]{1,0:T(8,128)} %get-tuple-element.219) | copy-start | bytes 1572868
  351.2 13.5 %copy-start.15 = (f32[128,1024]{1,0:T(8,128)S(1)}, f32[128,1024]{1,0:T(8,128)}, u32[]{:S(2)}) copy-start(f32[128,1024]{1,0:T(8,128)} %get-tuple-element.220) | copy-start | bytes 1572868
  351.2 139.9 %collective-permute-start.61 = (bf16[512,512]{1,0:T(8,128)(2,1)}, bf16[512,512]{1,0:T(8,128)(2,1)}, u32[]{:S(2)}, u32[]{:S(2)}) collective-permute-start(bf16[512,512]{1,0:T(8,128)(2,1)} %dynamic-slice_convert_fusion.2), channel_id=1, source_target_pairs={{0,1},{1,0},{2,3},{3,2},{4,5},{5,4},{6,7},{7,6},{8,9},{9,8},{10,11... | collective-permute-start | bytes 1572872 | tf_op jit(solution)/shard_map/ppermute | solution.py:73
  364.1 133.3 %collective-permute-start.63 = (bf16[512,512]{1,0:T(8,128)(2,1)}, bf16[512,512]{1,0:T(8,128)(2,1)}, u32[]{:S(2)}, u32[]{:S(2)}) collective-permute-start(bf16[512,512]{1,0:T(8,128)(2,1)} %dynamic-slice_convert_fusion.1), channel_id=1, source_target_pairs={{0,1},{1,0},{2,3},{3,2},{4,5},{5,4},{6,7},{7,6},{8,9},{9,8},{10,11... | collective-permute-start | bytes 1572872 | tf_op jit(solution)/shard_map/ppermute | solution.py:73
  364.8 16.6 %collective-permute-start.67 = (bf16[2,128,512]{2,1,0:T(8,128)(2,1)S(1)}, bf16[2,128,512]{2,1,0:T(8,128)(2,1)S(1)}, u32[]{:S(2)}, u32[]{:S(2)}) collective-permute-start(bf16[2,128,512]{2,1,0:T(8,128)(2,1)S(1)} %fusion.15), channel_id=1, source_target_pairs={{0,1},{1,0},{2,3},{3,2},{4,5},{5,4},{6,7},{7,6},{8,9},{9,8},{10,11... | collective-permute-start | bytes 786440 | tf_op jit(solution)/shard_map/ppermute | solution.py:73
  372.1 11.3 %copy-start.17 = (f32[512,1024]{1,0:T(8,128)S(1)}, f32[512,1024]{1,0:T(8,128)}, u32[]{:S(2)}) copy-start(f32[512,1024]{1,0:T(8,128)} %get-tuple-element.206) | copy-start | bytes 6291460
  382.1 4.8 collective-permute-start.68
  394.5 4.0 collective-permute-start.69
  397.9 84.9 %collective-permute-start.66 = (bf16[1024,512]{1,0:T(8,128)(2,1)}, bf16[1024,512]{1,0:T(8,128)(2,1)}, u32[]{:S(2)}, u32[]{:S(2)}) collective-permute-start(bf16[1024,512]{1,0:T(8,128)(2,1)} %dynamic-slice_convert_fusion), channel_id=1, source_target_pairs={{0,1},{1,0},{2,3},{3,2},{4,5},{5,4},{6,7},{7,6},{8,9},{9,8},{10,11... | collective-permute-start | bytes 3145736 | tf_op jit(solution)/shard_map/ppermute | solution.py:73
  398.5 4.0 collective-permute-start.70
  402.5 14.6 %collective-permute-start.71 = (bf16[4,16,512]{2,1,0:T(8,128)(2,1)S(1)}, bf16[4,16,512]{2,1,0:T(8,128)(2,1)S(1)}, u32[]{:S(2)}, u32[]{:S(2)}) collective-permute-start(bf16[4,16,512]{2,1,0:T(8,128)(2,1)S(1)} %maximum_select_fusion.7), channel_id=1, source_target_pairs={{0,8},{2,10},{4,12},{6,14},{8,0},{10,2},{12,4},{14,6},{16,24},{18,... | collective-permute-start | bytes 196616 | tf_op jit(solution)/shard_map/ppermute | solution.py:82
  417.2 7.9 %collective-permute-start.72 = (bf16[8,16,512]{2,1,0:T(8,128)(2,1)S(1)}, bf16[8,16,512]{2,1,0:T(8,128)(2,1)S(1)}, u32[]{:S(2)}, u32[]{:S(2)}) collective-permute-start(bf16[8,16,512]{2,1,0:T(8,128)(2,1)S(1)} %maximum_select_fusion.5), channel_id=1, source_target_pairs={{0,16},{2,18},{4,20},{6,22},{8,24},{10,26},{12,28},{14,30},{16,0},... | collective-permute-start | bytes 393224 | tf_op jit(solution)/shard_map/ppermute | solution.py:82
  461.0 16.1 %copy-start.24 = (f32[1024]{0:T(1024)S(1)}, f32[1024]{0:T(1024)}, u32[]{:S(2)}) copy-start(f32[1024]{0:T(1024)} %multiply_reduce_fusion) | copy-start | bytes 12292
  461.0 21.2 %copy-start.6 = (f32[512,8,128]{2,1,0:T(8,128)S(1)}, f32[512,8,128]{2,1,0:T(8,128)}, u32[]{:S(2)}) copy-start(f32[512,8,128]{2,1,0:T(8,128)} %get-tuple-element.226) | copy-start | bytes 6291460
  461.0 21.9 %copy-start.10 = (f32[512,512]{1,0:T(8,128)S(1)}, f32[512,512]{1,0:T(8,128)}, u32[]{:S(2)}) copy-start(f32[512,512]{1,0:T(8,128)} %constant_dynamic-slice_fusion.4) | copy-start | bytes 3145732
  461.0 21.9 %copy-start.11 = (f32[512,512]{1,0:T(8,128)S(1)}, f32[512,512]{1,0:T(8,128)}, u32[]{:S(2)}) copy-start(f32[512,512]{1,0:T(8,128)} %constant_dynamic-slice_fusion.3) | copy-start | bytes 3145732
  477.0 5.8 %collective-permute-start.73 = (f32[1024]{0:T(1024)S(1)}, f32[1024]{0:T(1024)S(1)}, u32[]{:S(2)}, u32[]{:S(2)}) collective-permute-start(f32[1024]{0:T(1024)S(1)} %add.234), channel_id=1, source_target_pairs={{0,1},{1,0},{2,3},{3,2},{4,5},{5,4},{6,7},{7,6},{8,9},{9,8},{10,11... | collective-permute-start | bytes 12296 | tf_op jit(solution)/shard_map/ppermute | solution.py:73
  484.4 13.0 %copy-start.18 = (f32[512,1024]{1,0:T(8,128)S(1)}, f32[512,1024]{1,0:T(8,128)}, u32[]{:S(2)}) copy-start(f32[512,1024]{1,0:T(8,128)} %get-tuple-element.195.mid_ref) | copy-start | bytes 6291460
  488.3 2.8 collective-permute-start.74
  491.1 4.8 collective-permute-start.75
  495.9 11.4 %copy-start.27 = (f32[2,512]{1,0:T(2,128)S(1)}, f32[2,512]{1,0:T(2,128)}, u32[]{:S(2)}) copy-start(f32[2,512]{1,0:T(2,128)} %param.89) | copy-start | bytes 12292
  495.9 11.4 %copy-start.28 = (f32[2,512]{1,0:T(2,128)S(1)}, f32[2,512]{1,0:T(2,128)}, u32[]{:S(2)}) copy-start(f32[2,512]{1,0:T(2,128)} %param.88) | copy-start | bytes 12292
  495.9 4.5 collective-permute-start.76
  498.8 9.9 %copy-start.20 = (f32[3,512,16]{1,2,0:T(8,128)S(1)}, f32[3,512,16]{1,2,0:T(8,128)}, u32[]{:S(2)}) copy-start(f32[3,512,16]{1,2,0:T(8,128)} %param.86) | copy-start | bytes 294916
  498.8 9.9 %copy-start.21 = (f32[3,512,16]{1,2,0:T(8,128)S(1)}, f32[3,512,16]{1,2,0:T(8,128)}, u32[]{:S(2)}) copy-start(f32[3,512,16]{1,2,0:T(8,128)} %param.85) | copy-start | bytes 294916
  498.8 9.8 %copy-start.47 = (f32[3]{0:T(128)S(1)}, f32[3]{0:T(128)}, u32[]{:S(2)}) copy-start(f32[3]{0:T(128)} %constant.225.clone) | copy-start | bytes 40
  500.4 20.7 %copy-start.9 = (f32[2,256,512]{2,1,0:T(8,128)S(1)}, f32[2,256,512]{2,1,0:T(8,128)}, u32[]{:S(2)}) copy-start(f32[2,256,512]{2,1,0:T(8,128)} %param.78) | copy-start | bytes 3145732
  500.4 6.8 %collective-permute-start.77 = (f32[34,512]{1,0:T(8,128)S(1)}, f32[34,512]{1,0:T(8,128)S(1)}, u32[]{:S(2)}, u32[]{:S(2)}) collective-permute-start(f32[34,512]{1,0:T(8,128)S(1)} %add.254), channel_id=1, source_target_pairs={{0,16},{2,18},{4,20},{6,22},{8,24},{10,26},{12,28},{14,30},{16,0},... | collective-permute-start | bytes 208904 | tf_op jit(solution)/shard_map/ppermute | solution.py:97
  509.4 9.5 %collective-permute-start.25 = (bf16[256,512]{1,0:T(8,128)(2,1)}, bf16[256,512]{1,0:T(8,128)(2,1)}, u32[]{:S(2)}, u32[]{:S(2)}) collective-permute-start(bf16[256,512]{1,0:T(8,128)(2,1)} %param.25), channel_id=1, source_target_pairs={{16,0},{18,2},{20,4},{22,6},{17,1},{19,3},{21,5},{23,7}} | collective-permute-start | bytes 786440 | tf_op jit(solution)/shard_map/cond/branch_1_fun/ppermute | solution.py:162
  521.1 17.0 %copy-start.4 = (f32[1,256,2048]{2,1,0:T(8,128)S(1)}, f32[1,256,2048]{2,1,0:T(8,128)}, u32[]{:S(2)}) copy-start(f32[1,256,2048]{2,1,0:T(8,128)} %param.81) | copy-start | bytes 6291460
  525.5 12.6 %collective-permute-start.44 = (bf16[256,1024]{1,0:T(8,128)(2,1)}, bf16[256,1024]{1,0:T(8,128)(2,1)}, u32[]{:S(2)}, u32[]{:S(2)}) collective-permute-start(bf16[256,1024]{1,0:T(8,128)(2,1)} %param.44), channel_id=1, source_target_pairs={{8,0},{10,2},{12,4},{14,6},{16,24},{18,26},{20,28},{22,30},{9,1},{... | collective-permute-start | bytes 1572872 | tf_op jit(solution)/shard_map/cond/branch_2_fun/ppermute | solution.py:162
  (27 other events, 90.0 us)
Sparse Core Ops, SparseCore 0:
  26.8 58.0 all-gather.2
  87.6 79.9 all-gather.4
  316.8 70.1 reduce-scatter.2
  391.5 104.5 reduce-scatter.4

commit v2 on v1

v2 whole, which is shorter than its diff:
```python
import functools
import itertools

import jax
import jax.numpy as jnp
from jax import lax
from jax.experimental import pallas as pl
from jax.experimental.pallas import tpu as pltpu
from jax.sharding import PartitionSpec as P

D = 1024
HEAD_DIM = 128
FF = 4096
STATE = 16
CTX = 128
BL = 512
OWNER_GROUPS = 4
STEP = 5

epsilon_norm = 1e-05
beta_first = 0.9
beta_second = 0.95
epsilon_adam = 1e-08
matrix_decay = 0.1
masked_score = -1e30
score_scale = HEAD_DIM ** (-0.5)
f32 = jnp.float32
bf16 = jnp.bfloat16
i32 = jnp.int32
SWAP = [(0, 1), (1, 0)]
COST = 1000
TILE = 256
QT = 256
FT = 512
LOG2E = 1.4426950408889634


def dot_nn(left, right):
    return lax.dot_general(left, right, (((1,), (0,)), ((), ())), preferred_element_type=f32)


def dot_nt(left, right):
    return lax.dot_general(left, right, (((1,), (1,)), ((), ())), preferred_element_type=f32)


def dot_tn(left, right):
    return lax.dot_general(left, right, (((0,), (0,)), ((), ())), preferred_element_type=f32)


def call(
    kernel, grid, in_specs, out_specs, out_shape, scratch=(), prefetch=0, flops=0, nbytes=0, room=36
):
    return pl.pallas_call(
        kernel,
        grid_spec=pltpu.PrefetchScalarGridSpec(
            num_scalar_prefetch=prefetch,
            grid=grid,
            in_specs=in_specs,
            out_specs=out_specs,
            scratch_shapes=scratch,
        ),
        out_shape=out_shape,
        name=kernel.__name__,
        compiler_params=pltpu.CompilerParams(vmem_limit_bytes=room * 1024 * 1024),
        cost_estimate=pl.CostEstimate(flops=flops // COST, bytes_accessed=nbytes // COST, transcendentals=0),
    )


def whole(shape):
    return pl.BlockSpec(shape, lambda *_: (0,) * len(shape), pipeline_mode=pl.Buffered(1))


def sds(shape, dtype):
    return jax.ShapeDtypeStruct(shape, dtype)


def swap_x(values):
    return lax.ppermute(values, "tensor", SWAP)


def gate(value, *others):
    if not others:
        return value
    return lax.optimization_barrier((value,) + others)[0]


def together(*values):
    return lax.optimization_barrier(values)


def gather_rounds():
    return max(lax.axis_size("dp") - 1, 0).bit_length()


def gather_round(held, k):
    step = 1 << k
    count = lax.axis_size("dp")
    other = lax.ppermute(held, "dp", [(i, i ^ step) for i in range(count)])
    later = (lax.axis_index("dp") // step) % 2 == 1
    return jnp.where(
        later,
        jnp.concatenate([other, held], axis=0),
        jnp.concatenate([held, other], axis=0),
    )


def total_dp(values, beside):
    count = lax.axis_size("dp")
    for k in range(gather_rounds()):
        if k == 2:
            values, beside = together(values, beside)
        values = values + lax.ppermute(values, "dp", [(i, i ^ (1 << k)) for i in range(count)])
    return values, beside


def routes(full_count, empty_count):
    groups = range(OWNER_GROUPS)
    ways = []
    for full in itertools.combinations(groups, full_count):
        rest = [g for g in groups if g not in full]
        for empty in itertools.combinations(rest, empty_count):
            ways.append((full, empty))
    return ways


ATTN_WAYS = routes(1, 1) + routes(2, 2)


def way_code(full, empty):
    code = 0
    for g in range(OWNER_GROUPS):
        digit = 2 if g in full else (0 if g in empty else 1)
        code += digit * 3**g
    return code


def one_if(condition):
    return jnp.where(condition, jnp.int32(1), jnp.int32(0))


HOST_MLP, SIDE, WAY, NEAR, ATTN_HERE, MLP_HERE, PLAN_SIZE = 4, 8, 9, 10, 11, 12, 16
ATTN_RATES = [0.5 * D ** (-0.5)] * 3 + [0.5 * (D // 16) ** (-0.5)]
MLP_RATES = [0.5 * D ** (-0.5), 0.5 * FF ** (-0.5)]
IDLE_RATE = 0.5 * D ** (-0.5)


def plan_kernel(owner_ref, here_ref, out_ref, rate_ref):
    groups = range(OWNER_GROUPS)
    side, group = here_ref[0], here_ref[1]
    owner = [owner_ref[m] for m in range(6)]
    slot = [
        sum([one_if(owner[k] == owner[m]) for k in range(m)], jnp.int32(0)) for m in range(4)
    ]
    count = [sum([one_if(owner[m] == g) for m in range(4)], jnp.int32(0)) for g in groups]
    full_rank = [sum([one_if(count[h] == 2) for h in range(g)], jnp.int32(0)) for g in groups]
    empty_rank = [sum([one_if(count[h] == 0) for h in range(g)], jnp.int32(0)) for g in groups]
    taker = [
        sum(
            [
                jnp.where(
                    jnp.logical_and(count[h] == 0, empty_rank[h] == full_rank[g]), jnp.int32(h), 0
                )
                for h in groups
            ],
            jnp.int32(0),
        )
        for g in groups
    ]
    for m in range(4):
        second = sum([jnp.where(owner[m] == g, taker[g], 0) for g in groups], jnp.int32(0))
        out_ref[m] = jnp.where(slot[m] == 0, owner[m], second)
    code = sum([count[g] * 3**g for g in groups], jnp.int32(0))
    out_ref[WAY] = sum(
        [
            jnp.where(code == way_code(*way), jnp.int32(k), 0)
            for k, way in enumerate(ATTN_WAYS)
        ],
        jnp.int32(0),
    )
    low = sum([one_if(owner[m] < 2) for m in (4, 5)], jnp.int32(0))
    near = low == 1
    for k, m in enumerate((4, 5)):
        out_ref[HOST_MLP + 2 * k] = owner[m]
        bit = jnp.where(near, jnp.int32(1), jnp.int32(2))
        out_ref[HOST_MLP + 2 * k + 1] = jnp.bitwise_xor(owner[m], bit)
    out_ref[SIDE] = side
    out_ref[NEAR] = one_if(near)
    out_ref[ATTN_HERE] = sum([one_if(owner[m] == group) for m in range(4)], jnp.int32(0))
    out_ref[MLP_HERE] = sum([one_if(owner[m] == group) for m in (4, 5)], jnp.int32(0))
    for k in range(MLP_HERE + 1, PLAN_SIZE):
        out_ref[k] = jnp.int32(0)
    for place in range(2):
        rate = f32(IDLE_RATE)
        for m in range(4):
            hit = jnp.logical_and(owner[m] == group, slot[m] == place)
            rate = jnp.where(hit, f32(ATTN_RATES[m]), rate)
        rate_ref[place] = rate
    rate = f32(IDLE_RATE)
    for k, m in enumerate((4, 5)):
        rate = jnp.where(owner[m] == group, f32(MLP_RATES[k]), rate)
    rate_ref[2] = rate
    rate_ref[3] = f32(0.0)


def move(values, index, ways, back):
    size = lax.axis_size("dp") // OWNER_GROUPS

    def branch(way):
        pairs = []
        for a, b in zip(*way):
            if back:
                a, b = b, a
            pairs += [(a * size + j, b * size + j) for j in range(size)]
        return lambda v: lax.ppermute(v, "dp", pairs)

    return lax.switch(index, [branch(way) for way in ways], values)


def exchange_groups(values, near):
    size = lax.axis_size("dp") // OWNER_GROUPS

    def across(bit):
        return lax.ppermute(
            values,
            "dp",
            [(g * size + j, (g ^ bit) * size + j) for g in range(OWNER_GROUPS) for j in range(size)],
        )

    return jnp.where(near, across(1), across(2))


def ring_order(count):
    chips = count // 2
    if chips == 8:
        return [0, 2, 4, 6, 7, 5, 3, 1]
    return list(range(chips))


def join_kernel(host_ref, own_ref, other_ref, out_ref):
    @pl.when(pl.program_id(0) == 0)
    def _():
        out_ref[...] = own_ref[...]

    @pl.when(pl.program_id(0) == 1)
    def _():
        out_ref[...] = other_ref[...]


def join_scaled_kernel(
    host_ref, own_ref, other_ref, inverse_ref, gain_ref, gain_other_ref, out_ref
):
    @pl.when(pl.program_id(0) == 0)
    def _():
        out_ref[...] = (own_ref[...].astype(f32) * inverse_ref[...] * gain_ref[...]).astype(bf16)

    @pl.when(pl.program_id(0) == 1)
    def _():
        out_ref[...] = (
            other_ref[...].astype(f32) * inverse_ref[...] * gain_other_ref[...]
        ).astype(bf16)


def join_sides(hosts, own, other, scales=()):
    rows, width = own.shape
    return call(
        join_scaled_kernel if scales else join_kernel,
        (2,),
        [whole(v.shape) for v in (own, other) + tuple(scales)],
        [
            pl.BlockSpec(
                (rows, width), lambda d, s: (0, jnp.where(d == 0, s[SIDE], 1 - s[SIDE]))
            )
        ],
        [sds((rows, 2 * width), bf16)],
        prefetch=1,
        nbytes=8 * rows * width,
        room=12,
    )(hosts, own, other, *scales)[0]


class Ring:
    def __init__(self):
        self.count = lax.axis_size("dp")
        self.chips = self.count // 2
        order = ring_order(self.count)
        here = lax.axis_index("dp")
        self.core = here % 2
        chip = here // 2
        self.place = jnp.where(chip % 2 == 0, chip // 2, 7 - chip // 2) if self.chips == 8 else chip
        self.up = [
            (2 * order[p] + c, 2 * order[(p + 1) % self.chips] + c)
            for p in range(self.chips)
            for c in range(2)
        ]
        self.down = [(b, a) for a, b in self.up]
        self.cores = [(i, i ^ 1) for i in range(self.count)]
        self.far_up = self.chips // 2
        self.far_down = self.chips - 1 - self.far_up

    def chip(self, offset):
        place = (self.place + self.chips + offset) % self.chips
        if self.chips != 8:
            return place
        return jnp.where(place < 4, 2 * place, 15 - 2 * place)

    def reduce_scatter(self, blocks, values, last):
        pairs = blocks.reshape((self.chips, 2) + blocks.shape[1:])
        mine = lax.dynamic_index_in_dim(pairs, self.core, 1, keepdims=False)
        theirs = lax.dynamic_index_in_dim(pairs, 1 - self.core, 1, keepdims=False)
        received = lax.ppermute(theirs, "dp", self.cores)

        def block(offset):
            chip = self.chip(offset)
            return lax.dynamic_index_in_dim(mine, chip, 0, keepdims=False).astype(
                f32
            ) + lax.dynamic_index_in_dim(received, chip, 0, keepdims=False).astype(f32)

        held = gather_round(values[None], 0)
        up = block(self.far_up).astype(bf16)
        down = block(-self.far_down).astype(bf16)
        for step in range(max(self.far_up, gather_rounds() - 1)):
            if step == gather_rounds() - 2:
                up, down, held, last = together(up, down, held, last)
            else:
                up, down, held = together(up, down, held)
            if step + 1 < gather_rounds():
                held = gather_round(held, step + 1)
            if step < self.far_up:
                up = lax.ppermute(up, "dp", self.up)
                if step < self.far_up - 1:
                    up = (up.astype(f32) + block(self.far_up - 1 - step)).astype(bf16)
            if step < self.far_down:
                down = lax.ppermute(down, "dp", self.down)
                if step < self.far_down - 1:
                    down = (down.astype(f32) + block(step + 1 - self.far_down)).astype(bf16)
        return block(0) + up.astype(f32) + down.astype(f32), held, last

    def all_gather(self, block, values, gates):
        ups, downs, held = [block], [block], values[None]
        for step in range(max(self.far_up, gather_rounds())):
            joined = together(ups[-1], downs[-1], held, *gates.get(step, ()))
            ups[-1], downs[-1], held = joined[:3]
            if step < gather_rounds():
                held = gather_round(held, step)
            if step < self.far_up:
                ups.append(lax.ppermute(ups[-1], "dp", self.up))
            if step < self.far_down:
                downs.append(lax.ppermute(downs[-1], "dp", self.down))
        mine = jnp.stack(ups + downs[1:])
        theirs = lax.ppermute(mine, "dp", self.cores)
        offsets = [-k for k in range(self.far_up + 1)] + [k + 1 for k in range(self.far_down)]
        table = jnp.stack([self.chip(k) for k in offsets] + [self.core]).astype(i32)
        rows, columns = block.shape

        def place_kernel(table_ref, mine_ref, theirs_ref, out_ref):
            core = table_ref[self.chips]
            out_ref[0, core] = mine_ref[0]
            out_ref[0, 1 - core] = theirs_ref[0]

        spec = pl.BlockSpec((1, rows, columns), lambda k, s: (k, 0, 0))
        out = call(
            place_kernel,
            (self.chips,),
            [spec, spec],
            [pl.BlockSpec((1, 2, rows, columns), lambda k, s: (s[k], 0, 0, 0))],
            [sds((self.chips, 2, rows, columns), block.dtype)],
            prefetch=1,
            nbytes=4 * self.count * rows * columns,
        )(table, mine, theirs)[0]
        return out.reshape(self.count * rows, columns), held, mine


def shift_tails(values, by, cross):
    count = lax.axis_size("dp")
    pairs = [
        (2 * i + s, 2 * (i + by) + (1 - s if cross else s))
        for i in range(count)
        for s in range(2)
        if 0 <= i + by < count
    ]
    return lax.ppermute(values, ("dp", "tensor"), pairs)


def first_half():
    return lax.broadcasted_iota(i32, (8, 128), 0) < 4


def flag(condition):
    return jnp.where(condition, f32(1.0), f32(0.0))


def keep_at(seg_ref, t, half):
    return jnp.where(
        half, flag(seg_ref[t + 1] == seg_ref[t]), flag(seg_ref[BL + t + 1] == seg_ref[BL + t])
    )


def chunked(seg_ref, begin, end, plain, kept, carried, back=False):
    size = 8
    count = (end - begin) // size

    def chunk(c, carried):
        first = begin + (count - 1 - c if back else c) * size
        same = jnp.logical_and(
            seg_ref[first] == seg_ref[first + size],
            seg_ref[BL + first] == seg_ref[BL + first + size],
        )

        def run(step):
            def go(carried):
                for k in range(size):
                    carried = step(first + (size - 1 - k if back else k), carried)
                return carried

            return go

        return lax.cond(same, run(plain), run(kept), carried)

    return lax.fori_loop(0, count, chunk, carried)


def scan_kernel(seg_ref, h_ref, rate_ref, c_ref, y_ref, s_ref, e_ref):
    half = first_half()
    decay = [jnp.exp(-rate_ref[n]) for n in range(STATE)]

    def plain(t, states):
        row = h_ref[t]
        return [states[n] * decay[n] + row for n in range(STATE)]

    def kept(t, states):
        keep = keep_at(seg_ref, t, half)
        row = h_ref[t]
        return [(states[n] * keep) * decay[n] + row for n in range(STATE)]

    def reading(step):
        def go(t, states):
            states = step(t, states)
            total = c_ref[0] * states[0]
            for n in range(1, STATE):
                total = total + c_ref[n] * states[n]
            y_ref[t - (BL - CTX)] = total
            return states

        return go

    states = [jnp.zeros((8, 128), f32)] * STATE
    states = chunked(seg_ref, 0, BL - CTX, plain, kept, states)
    states = chunked(seg_ref, BL - CTX, BL, reading(plain), reading(kept), states)
    joined = flag(seg_ref[2 * BL] == seg_ref[BL])
    for n in range(STATE):
        s_ref[n] = states[n]
        ends = states[n] + (joined * jnp.exp(-rate_ref[n] * BL)) * pltpu.roll(states[n], 4, 0)
        e_ref[n] = ends


def tail_kernel(
    seg_ref, use_ref, all_ref, s_ref, rate_ref, c_ref, y_ref, out_ref, start_ref, carry_ref
):
    half = first_half()
    before = seg_ref[0]
    joined = flag(seg_ref[BL] == before)
    decay = [jnp.exp(-rate_ref[n]) for n in range(STATE)]
    carry_ref[...] = jnp.zeros_like(carry_ref)

    def gather(j, _):
        @pl.when(use_ref[j] > 0)
        def _():
            for m in range(STATE // 2):
                pair = all_ref[j, 16 * m : 16 * m + 16, :].astype(f32)
                for k in range(2):
                    n = 2 * m + k
                    power = jnp.exp(-rate_ref[n] * (2 * BL))
                    carry_ref[n] = carry_ref[n] * power + pair[8 * k : 8 * k + 8]

        return 0

    lax.fori_loop(0, all_ref.shape[0], gather, 0)
    weighted = []
    for n in range(STATE):
        carried = pltpu.roll(carry_ref[n], 4, 0)
        mid = pltpu.roll(s_ref[n], 4, 0) + (joined * jnp.exp(-rate_ref[n] * BL)) * carry_ref[n]
        start = jnp.where(half, carried, mid)
        start_ref[n] = start
        weighted.append(c_ref[n] * start * jnp.exp(-rate_ref[n] * (BL - CTX + 1)))

    def step(t, parts):
        mask = jnp.where(
            half,
            flag(seg_ref[t + 1 + BL - CTX] == before),
            flag(seg_ref[BL + t + 1 + BL - CTX] == seg_ref[BL]),
        )
        total = parts[0]
        for n in range(1, STATE):
            total = total + parts[n]
        out_ref[t] = y_ref[t] + mask * total
        return [parts[n] * decay[n] for n in range(STATE)]

    lax.fori_loop(0, CTX, step, weighted, unroll=4)


def back_total_kernel(seg_ref, g_ref, rate_ref, c_ref, own_ref, out_ref):
    half = first_half()
    decay = [jnp.exp(-rate_ref[n]) for n in range(STATE)]

    def step(k, sums):
        t = CTX - 1 - k
        mask = jnp.where(
            half,
            flag(seg_ref[t + 1 + BL - CTX] == seg_ref[1]),
            flag(seg_ref[BL + t + 1 + BL - CTX] == seg_ref[BL]),
        )
        grad = mask * g_ref[t]
        return [decay[n] * (sums[n] + grad) for n in range(STATE)]

    sums = lax.fori_loop(0, CTX, step, [jnp.zeros((8, 128), f32)] * STATE, unroll=4)
    joined = flag(seg_ref[1] == seg_ref[BL])
    for n in range(STATE):
        total = sums[n] * c_ref[n] * jnp.exp(-rate_ref[n] * (BL - CTX))
        own_ref[n] = total
        out_ref[n] = total + (joined * jnp.exp(-rate_ref[n] * BL)) * pltpu.roll(total, 4, 0)


def sens_steps(seg_ref, h_ref, half, decay, count):
    def plain(t, both):
        row = h_ref[t]
        sens = [both[1][n] * decay[n] + both[0][n] for n in range(count)]
        states = [both[0][n] * decay[n] + row for n in range(count)]
        return [states, sens] + list(both[2:])

    def kept(t, both):
        keep = keep_at(seg_ref, t, half)
        row = h_ref[t]
        held = [v * keep for v in both[0]]
        sens = [(both[1][n] * keep) * decay[n] + held[n] for n in range(count)]
        states = [held[n] * decay[n] + row for n in range(count)]
        return [states, sens] + list(both[2:])

    return plain, kept


SENS_GROUP = 8


def sens_kernel(seg_ref, h_ref, start_ref, rate_ref, s_ref, z_ref):
    half = first_half()
    for first in range(0, STATE, SENS_GROUP):
        ids = range(first, first + SENS_GROUP)
        decay = [jnp.exp(-rate_ref[n]) for n in ids]
        plain, kept = sens_steps(seg_ref, h_ref, half, decay, SENS_GROUP)
        both = [[start_ref[n] for n in ids], [jnp.zeros((8, 128), f32)] * SENS_GROUP]
        both = chunked(seg_ref, 0, BL - CTX, plain, kept, both)
        for k, n in enumerate(ids):
            s_ref[n] = both[0][k]
            z_ref[n] = both[1][k]


def sens_tail_kernel(seg_ref, h_ref, g_ref, s_ref, z_ref, rate_ref, gc_ref, ga_ref, zend_ref):
    half = first_half()
    for first in range(0, STATE, SENS_GROUP):
        ids = range(first, first + SENS_GROUP)
        decay = [jnp.exp(-rate_ref[n]) for n in ids]

        def summing(step):
            def go(t, carried):
                states, sens, by_c, by_a = step(t, carried)
                grad = g_ref[t - (BL - CTX)]
                by_c = [by_c[n] + grad * states[n] for n in range(SENS_GROUP)]
                by_a = [by_a[n] + grad * sens[n] for n in range(SENS_GROUP)]
                return [states, sens, by_c, by_a]

            return go

        plain, kept = sens_steps(seg_ref, h_ref, half, decay, SENS_GROUP)
        zeros = [jnp.zeros((8, 128), f32)] * SENS_GROUP
        carried = [[s_ref[n] for n in ids], [z_ref[n] for n in ids], zeros, zeros]
        carried = chunked(seg_ref, BL - CTX, BL, summing(plain), summing(kept), carried)
        for k, n in enumerate(ids):
            zend_ref[n] = carried[1][k]
            gc_ref[n] = carried[2][k]
            ga_ref[n] = carried[3][k]


def back_scan_kernel(
    seg_ref,
    use_ref,
    all_ref,
    g_ref,
    own_ref,
    z_ref,
    ga_ref,
    rate_ref,
    c_ref,
    gh_ref,
    out_ref,
    later_ref,
):
    half = first_half()
    decay = [jnp.exp(-rate_ref[n]) for n in range(STATE)]
    joined = flag(seg_ref[2 * BL] == seg_ref[BL])
    later_ref[...] = jnp.zeros_like(later_ref)
    count = all_ref.shape[0]

    def gather(k, _):
        j = count - 1 - k

        @pl.when(use_ref[j] > 0)
        def _():
            for m in range(STATE // 2):
                pair = all_ref[j, 16 * m : 16 * m + 16, :].astype(f32)
                for k in range(2):
                    n = 2 * m + k
                    power = jnp.exp(-rate_ref[n] * (2 * BL))
                    later_ref[n] = later_ref[n] * power + pair[8 * k : 8 * k + 8]

        return 0

    lax.fori_loop(0, count, gather, 0)
    sums = []
    for n in range(STATE):
        first = (
            pltpu.roll(own_ref[n], 4, 0) + (joined * jnp.exp(-rate_ref[n] * BL)) * later_ref[n]
        )
        entering = jnp.where(half, first, pltpu.roll(later_ref[n], 4, 0))
        sums.append(entering)
        out_ref[n] = ga_ref[n] * c_ref[n] + entering * z_ref[n]

    def total_of(t, sums):
        total = sums[0]
        for n in range(1, STATE):
            total = total + sums[n]
        gh_ref[t] = total

    def plain(t, sums):
        total_of(t, sums)
        return [v * decay[n] for n, v in enumerate(sums)]

    def kept(t, sums):
        total_of(t, sums)
        keep = keep_at(seg_ref, t, half)
        return [(v * keep) * decay[n] for n, v in enumerate(sums)]

    def entered(step):
        def go(t, sums):
            grad = g_ref[t - (BL - CTX)]
            return step(t, [sums[n] + c_ref[n] * grad for n in range(STATE)])

        return go

    sums = chunked(seg_ref, BL - CTX, BL, entered(plain), entered(kept), sums, back=True)
    chunked(seg_ref, 0, BL - CTX, plain, kept, sums, back=True)


def to_lanes(values, blocks, steps):
    return (
        values.reshape(blocks, steps, 4, 128).transpose(1, 0, 2, 3).reshape(steps, blocks * 4, 128)
    )


def from_lanes(values, blocks, steps):
    return values.reshape(steps, blocks, 4, 128).transpose(1, 0, 2, 3).reshape(blocks, steps, 512)


def attend_kernel(
    host_ref,
    hid_ref,
    ctx_ref,
    wq_ref,
    wk_ref,
    wv_ref,
    segq_ref,
    segk_ref,
    q_ref,
    k_ref,
    v_ref,
    ck_ref,
    cv_ref,
    pc_ref,
    pb_ref,
    mix_ref,
):
    hid = hid_ref[...]
    ctx = ctx_ref[...]
    q_ref[...] = dot_nn(hid, wq_ref[0]).astype(bf16)
    k_ref[...] = dot_nn(hid, wk_ref[0]).astype(bf16)
    v_ref[...] = dot_nn(hid, wv_ref[0]).astype(bf16)
    ck_ref[...] = dot_nn(ctx, wk_ref[0]).astype(bf16)
    cv_ref[...] = dot_nn(ctx, wv_ref[0]).astype(bf16)
    ctx_ids = segk_ref[:, :CTX]
    for i in range(BL // QT):
        rows = slice(i * QT, (i + 1) * QT)
        reach = (i + 1) * QT
        ids = segq_ref[rows]
        ctx_ok = ctx_ids == ids
        place_q = lax.broadcasted_iota(i32, (QT, reach), 0) + i * QT
        place_k = lax.broadcasted_iota(i32, (QT, reach), 1)
        block_ok = jnp.logical_and(place_k <= place_q, segk_ref[:, CTX : CTX + reach] == ids)
        for head in range(TILE // HEAD_DIM):
            cols = slice(head * HEAD_DIM, (head + 1) * HEAD_DIM)
            query = q_ref[rows, cols]
            sc = dot_nt(query, ck_ref[:, cols]) * (score_scale * LOG2E)
            sb = dot_nt(query, k_ref[:reach, cols]) * (score_scale * LOG2E)
            sc = jnp.where(ctx_ok, sc, masked_score)
            sb = jnp.where(block_ok, sb, masked_score)
            top = jnp.maximum(
                jnp.max(sc, axis=1, keepdims=True), jnp.max(sb, axis=1, keepdims=True)
            )
            ec = jnp.exp2(sc - top)
            eb = jnp.exp2(sb - top)
            total = jnp.sum(ec, axis=1, keepdims=True) + jnp.sum(eb, axis=1, keepdims=True)
            inverse = 1.0 / total
            pc = (ec * inverse).astype(bf16)
            pb = (eb * inverse).astype(bf16)
            pc_ref[head, rows, :] = pc
            pb_ref[head, rows, :reach] = pb
            if reach < BL:
                pb_ref[head, rows, reach:] = jnp.zeros((QT, BL - reach), bf16)
            mixed = dot_nn(pc, cv_ref[:, cols]) + dot_nn(pb, v_ref[:reach, cols])
            mix_ref[rows, cols] = mixed.astype(bf16)


def attend_forward(hosts, block, hidden, context, attn_full, seg_col, seg_row, half_width):
    pairs = half_width // TILE

    def weight(position):
        return pl.BlockSpec((1, D, TILE), lambda p, s: (s[position], 0, p))

    def tile(rows):
        return pl.BlockSpec((rows, TILE), lambda p, s: (0, p))

    heads = half_width // HEAD_DIM
    per = TILE // HEAD_DIM
    return call(
        attend_kernel,
        (pairs,),
        [
            pl.BlockSpec((BL, D), lambda p, s: (block, 0)),
            pl.BlockSpec((CTX, D), lambda p, s: (block, 0)),
            weight(0),
            weight(1),
            weight(2),
            pl.BlockSpec((BL, 1), lambda p, s: (block, 0)),
            whole((1, CTX + BL)),
        ],
        [
            tile(BL),
            tile(BL),
            tile(BL),
            tile(CTX),
            tile(CTX),
            pl.BlockSpec((per, BL, CTX), lambda p, s: (p, 0, 0)),
            pl.BlockSpec((per, BL, BL), lambda p, s: (p, 0, 0)),
            tile(BL),
        ],
        [
            sds((BL, half_width), bf16),
            sds((BL, half_width), bf16),
            sds((BL, half_width), bf16),
            sds((CTX, half_width), bf16),
            sds((CTX, half_width), bf16),
            sds((heads, BL, CTX), bf16),
            sds((heads, BL, BL), bf16),
            sds((BL, half_width), bf16),
        ],
        prefetch=1,
        flops=8 * 10**9,
        nbytes=12 * 10**6,
    )(hosts, hidden, context, attn_full, attn_full, attn_full, seg_col, seg_row)


def attend_back_kernel(
    host_ref,
    own_ref,
    other_ref,
    cot_ref,
    mid_ref,
    gain_ref,
    tok_ref,
    first_gain_ref,
    wo_ref,
    wq_ref,
    wk_ref,
    wv_ref,
    q_ref,
    k_ref,
    v_ref,
    ck_ref,
    cv_ref,
    pc_ref,
    pb_ref,
    low_ref,
    gmid_ref,
    ggain_ref,
    dq_ref,
    dk_ref,
    dv_ref,
    dck_ref,
    dcv_ref,
    hown_ref,
    hsend_ref,
    cown_ref,
    csend_ref,
    sum_ref,
    dsc_ref,
    dsb_ref,
):
    step = pl.program_id(0)
    pairs = pl.num_programs(0) - 2

    @pl.when(step == 0)
    def _():
        grad = own_ref[...].astype(f32) + other_ref[...].astype(f32)
        middle = mid_ref[...]
        inverse = lax.rsqrt(jnp.mean(middle * middle, axis=1, keepdims=True) + epsilon_norm)
        scaled = middle * inverse
        ggain_ref[...] = jnp.sum(grad * scaled, axis=0, keepdims=True)
        weighted = grad * gain_ref[...]
        centre = jnp.mean(weighted * scaled, axis=1, keepdims=True)
        result = cot_ref[...].astype(f32) + inverse * (weighted - scaled * centre)
        gmid_ref[...] = result
        low_ref[...] = result.astype(bf16)

    @pl.when(step < pairs)
    def _():
        grad_mixed = dot_nn(low_ref[...], wo_ref[0]).astype(bf16)
        base = step * TILE
        for head in range(TILE // HEAD_DIM):
            cols = slice(head * HEAD_DIM, (head + 1) * HEAD_DIM)
            to = pl.ds(pl.multiple_of(base + head * HEAD_DIM, HEAD_DIM), HEAD_DIM)
            grad_head = grad_mixed[:, cols]
            for i in range(BL // QT):
                rows = slice(i * QT, (i + 1) * QT)
                reach = (i + 1) * QT
                grad_rows = grad_head[rows]
                gpc = dot_nt(grad_rows, cv_ref[:, cols])
                gpb = dot_nt(grad_rows, v_ref[:reach, cols])
                pc = pc_ref[head, rows, :].astype(f32)
                pb = pb_ref[head, rows, :reach].astype(f32)
                tc = pc * gpc
                tb = pb * gpb
                centre = jnp.sum(tc, axis=1, keepdims=True) + jnp.sum(tb, axis=1, keepdims=True)
                dsc_ref[head, rows, :] = (tc - pc * centre).astype(bf16)
                dsb_ref[head, rows, :reach] = (tb - pb * centre).astype(bf16)
                if reach < BL:
                    dsb_ref[head, rows, reach:] = jnp.zeros((QT, BL - reach), bf16)
            dsc = dsc_ref[head]
            dsb = dsb_ref[head]
            dq = (dot_nn(dsc, ck_ref[:, cols]) + dot_nn(dsb, k_ref[:, cols])) * score_scale
            dq_ref[:, to] = dq.astype(bf16)
            query = q_ref[:, cols]
            dk_ref[:, to] = (dot_tn(dsb, query) * score_scale).astype(bf16)
            dck_ref[:, to] = (dot_tn(dsc, query) * score_scale).astype(bf16)
            dv_ref[:, to] = dot_tn(pb_ref[head], grad_head).astype(bf16)
            dcv_ref[:, to] = dot_tn(pc_ref[head], grad_head).astype(bf16)

    def half():
        part = (
            dot_nt(dq_ref[...], wq_ref[0])
            + dot_nt(dk_ref[...], wk_ref[0])
            + dot_nt(dv_ref[...], wv_ref[0])
        )
        ctx_part = dot_nt(dck_ref[...], wk_ref[0]) + dot_nt(dcv_ref[...], wv_ref[0])
        row_sum = jnp.sum(
            part * (tok_ref[...].astype(f32) * first_gain_ref[...]), axis=1, keepdims=True
        )
        return part, ctx_part, row_sum

    @pl.when(step == pairs)
    def _():
        part, ctx_part, row_sum = half()
        hsend_ref[...] = part.astype(bf16)
        csend_ref[...] = ctx_part.astype(bf16)
        sum_ref[...] = row_sum

    @pl.when(step == pairs + 1)
    def _():
        part, ctx_part, row_sum = half()
        hown_ref[...] = part
        cown_ref[...] = ctx_part
        sum_ref[...] += row_sum


def attend_backward(
    hosts, block, own, other, cot_full, middle, gain, tok_full, first_gain, attn_full, kept, width
):
    pairs = width // TILE
    per = TILE // HEAD_DIM

    def pair(p):
        return jnp.minimum(p, pairs - 1)

    def side(p, s):
        return jnp.where(p <= pairs, 1 - s[8], s[8])

    def weight(position):
        return pl.BlockSpec((1, width, width), lambda p, s: (s[position], side(p, s), 0))

    def tile(rows):
        return pl.BlockSpec((rows, TILE), lambda p, s: (0, pair(p)))

    return call(
        attend_back_kernel,
        (pairs + 2,),
        [
            whole((BL, D)),
            whole((BL, D)),
            pl.BlockSpec((BL, D), lambda p, s: (block, 0)),
            whole((BL, D)),
            whole((1, D)),
            pl.BlockSpec((BL, width), lambda p, s: (block, side(p, s))),
            pl.BlockSpec((1, width), lambda p, s: (0, side(p, s))),
            pl.BlockSpec((1, D, TILE), lambda p, s: (s[3], 0, pair(p))),
            weight(0),
            weight(1),
            weight(2),
            tile(BL),
            tile(BL),
            tile(BL),
            tile(CTX),
            tile(CTX),
            pl.BlockSpec((per, BL, CTX), lambda p, s: (pair(p), 0, 0)),
            pl.BlockSpec((per, BL, BL), lambda p, s: (pair(p), 0, 0)),
        ],
        [
            whole((BL, D)),
            whole((BL, D)),
            whole((1, D)),
            whole((BL, width)),
            whole((BL, width)),
            whole((BL, width)),
            whole((CTX, width)),
            whole((CTX, width)),
            whole((BL, width)),
            whole((BL, width)),
            whole((CTX, width)),
            whole((CTX, width)),
            whole((BL, 1)),
        ],
        [
            sds((BL, D), bf16),
            sds((BL, D), f32),
            sds((1, D), f32),
            sds((BL, width), bf16),
            sds((BL, width), bf16),
            sds((BL, width), bf16),
            sds((CTX, width), bf16),
            sds((CTX, width), bf16),
            sds((BL, width), f32),
            sds((BL, width), bf16),
            sds((CTX, width), f32),
            sds((CTX, width), bf16),
            sds((BL, 1), f32),
        ],
        scratch=[pltpu.VMEM((per, BL, CTX), bf16), pltpu.VMEM((per, BL, BL), bf16)],
        prefetch=1,
        flops=12 * 10**9,
        nbytes=20 * 10**6,
    )(
        hosts,
        own,
        other,
        cot_full,
        middle,
        gain,
        tok_full,
        first_gain,
        attn_full,
        attn_full,
        attn_full,
        attn_full,
        *kept,
    )


def attn_grad_kernel(host_ref, *refs):
    (hid0, hid1, ctx0, ctx1, low0, low1), rest = refs[:6], refs[6:]
    (dq0, dk0, dv0, dck0, dcv0, mix0), rest = rest[:6], rest[6:]
    (dq1, dk1, dv1, dck1, dcv1, mix1), (out_ref,) = rest[:6], rest[6:]
    matrix = pl.program_id(0)

    @pl.when(matrix == 0)
    def _():
        out_ref[0] = (dot_tn(hid0[...], dq0[...]) + dot_tn(hid1[...], dq1[...])).astype(bf16)

    @pl.when(matrix == 1)
    def _():
        out_ref[0] = (
            dot_tn(hid0[...], dk0[...])
            + dot_tn(hid1[...], dk1[...])
            + dot_tn(ctx0[...], dck0[...])
            + dot_tn(ctx1[...], dck1[...])
        ).astype(bf16)

    @pl.when(matrix == 2)
    def _():
        out_ref[0] = (
            dot_tn(hid0[...], dv0[...])
            + dot_tn(hid1[...], dv1[...])
            + dot_tn(ctx0[...], dcv0[...])
            + dot_tn(ctx1[...], dcv1[...])
        ).astype(bf16)

    @pl.when(matrix == 3)
    def _():
        out_ref[0] = (dot_tn(low0[...], mix0[...]) + dot_tn(low1[...], mix1[...])).astype(bf16)


def attn_grads(hosts, hidden, context, lows, blocks, half_width):
    hid_specs = [
        pl.BlockSpec((BL, D), lambda m, s: (0, 0)),
        pl.BlockSpec((BL, D), lambda m, s: (1, 0)),
        pl.BlockSpec((CTX, D), lambda m, s: (0, 0)),
        pl.BlockSpec((CTX, D), lambda m, s: (1, 0)),
    ]
    block_specs = [
        whole((BL, half_width)),
        whole((BL, half_width)),
        whole((BL, half_width)),
        whole((CTX, half_width)),
        whole((CTX, half_width)),
        whole((BL, half_width)),
    ]
    return call(
        attn_grad_kernel,
        (4,),
        hid_specs + [whole((BL, D))] * 2 + block_specs * 2,
        [pl.BlockSpec((1, D, half_width), lambda m, s: (s[m], 0, 0))],
        [sds((OWNER_GROUPS, D, half_width), bf16)],
        prefetch=1,
        flops=46 * 10**8,
        nbytes=14 * 10**6,
    )(hosts, hidden, hidden, context, context, *lows, *blocks[0], *blocks[1])[0]


def mlp_kernel(
    host_ref,
    own_ref,
    other_ref,
    wo_ref,
    woo_ref,
    tok_ref,
    gain_ref,
    cot_ref,
    w1_ref,
    w2_ref,
    mid_ref,
    hid_ref,
    act_ref,
    pre_ref,
    low_ref,
    grad_ref,
):
    step = pl.program_id(0)

    @pl.when(step == 0)
    def _():
        middle = (
            tok_ref[...].astype(f32)
            + dot_nt(own_ref[...], wo_ref[0])
            + dot_nt(other_ref[...], woo_ref[...])
        )
        inverse = lax.rsqrt(jnp.mean(middle * middle, axis=1, keepdims=True) + epsilon_norm)
        mid_ref[...] = middle
        hid_ref[...] = (middle * inverse * gain_ref[...]).astype(bf16)
        grad_ref[...] = jnp.zeros_like(grad_ref)

    w1 = w1_ref[0]
    w2 = w2_ref[0]
    pre = dot_nn(hid_ref[...], w1)
    grad_act = dot_nn(cot_ref[...], w2)
    root = 0.7978845608028654
    square = pre * pre
    gate = 0.5 + 0.5 * jnp.tanh(pre * (root + (root * 0.044715) * square))
    act = pre * gate
    act_ref[...] = act.astype(bf16)
    slope = gate + act * (1.0 - gate) * (2.0 * root + (6.0 * root * 0.044715) * square)
    grad_pre = (slope * grad_act).astype(bf16)
    pre_ref[...] = grad_pre
    grad_ref[...] += dot_nt(grad_pre, w1)

    @pl.when(step == pl.num_programs(0) - 1)
    def _():
        low_ref[...] = grad_ref[...].astype(bf16)


def mlp_block(hosts, block, own, other, attn_full, wo_other, tok_full, gain, cot_full, mlp_full):
    half_width = own.shape[1]
    quarter = mlp_full.shape[2]
    hidden = 2 * quarter
    per = quarter // FT

    def weight(position):
        return pl.BlockSpec(
            (1, D, FT), lambda f, s: (s[4 + 2 * position + f // per], 0, lax.rem(f, per))
        )

    return call(
        mlp_kernel,
        (2 * per,),
        [
            whole((BL, half_width)),
            whole((BL, half_width)),
            pl.BlockSpec((1, D, half_width), lambda f, s: (s[3], 0, 0)),
            whole((D, half_width)),
            pl.BlockSpec((BL, D), lambda f, s: (block, 0)),
            whole((1, D)),
            pl.BlockSpec((BL, D), lambda f, s: (block, 0)),
            weight(0),
            weight(1),
        ],
        [
            whole((BL, D)),
            whole((BL, D)),
            pl.BlockSpec((BL, FT), lambda f, s: (0, f)),
            pl.BlockSpec((BL, FT), lambda f, s: (0, f)),
            whole((BL, D)),
        ],
        [
            sds((BL, D), f32),
            sds((BL, D), bf16),
            sds((BL, hidden), bf16),
            sds((BL, hidden), bf16),
            sds((BL, D), bf16),
        ],
        scratch=[pltpu.VMEM((BL, D), f32)],
        prefetch=1,
        flops=8 * 10**9,
        nbytes=24 * 10**6,
    )(hosts, own, other, attn_full, wo_other, tok_full, gain, cot_full, mlp_full, mlp_full)


def mlp_grad_kernel(host_ref, h0, h1, g0, g1, p0, p1, a0, a1, out_ref):
    matrix = pl.program_id(0)

    @pl.when(matrix == 0)
    def _():
        out_ref[0] = (dot_tn(h0[...], p0[...]) + dot_tn(h1[...], p1[...])).astype(bf16)

    @pl.when(matrix == 1)
    def _():
        out_ref[0] = (dot_tn(g0[...], a0[...]) + dot_tn(g1[...], a1[...])).astype(bf16)


def mlp_grads(hosts, hiddens, cot_full, pres, acts):
    hidden = acts[0].shape[1]
    quarter = hidden // 2
    per = quarter // FT
    last = 2 * per - 1
    used_first = pl.BlockSpec((BL, FT), lambda m, f, s: (0, jnp.where(m == 0, f, last)))
    used_second = pl.BlockSpec((BL, FT), lambda m, f, s: (0, jnp.where(m == 1, f, 0)))
    return call(
        mlp_grad_kernel,
        (2, 2 * per),
        [
            whole((BL, D)),
            whole((BL, D)),
            pl.BlockSpec((BL, D), lambda m, f, s: (0, 0)),
            pl.BlockSpec((BL, D), lambda m, f, s: (1, 0)),
            used_first,
            used_first,
            used_second,
            used_second,
        ],
        [
            pl.BlockSpec(
                (1, D, FT), lambda m, f, s: (s[4 + 2 * m + f // per], 0, lax.rem(f, per))
            )
        ],
        [sds((OWNER_GROUPS, D, quarter), bf16)],
        prefetch=1,
        flops=86 * 10**8,
        nbytes=20 * 10**6,
    )(hosts, hiddens[0], hiddens[1], cot_full, cot_full, pres[0], pres[1], acts[0], acts[1])[0]


def mlp_out_kernel(host_ref, a0, a1, wa_ref, wb_ref, mid0, mid1, send_ref, own_ref):
    step = pl.program_id(0)
    quarter = wa_ref.shape[2]

    def rows(a_ref):
        return dot_nt(a_ref[:, :quarter], wa_ref[0]) + dot_nt(a_ref[:, quarter:], wb_ref[0])

    @pl.when(step == 0)
    def _():
        send_ref[:BL, :] = rows(a0).astype(bf16)
        send_ref[BL:, :] = rows(a1).astype(bf16)

    @pl.when(step == 1)
    def _():
        own_ref[:BL, :] = rows(a0) + mid0[...]
        own_ref[BL:, :] = rows(a1) + mid1[...]


def mlp_out(hosts, acts, mlp_full, middles, width):
    quarter = mlp_full.shape[2]

    def side(d, s):
        return jnp.where(d == 0, 1 - s[8], s[8])

    def weight(position):
        return pl.BlockSpec((1, width, quarter), lambda d, s: (s[position], side(d, s), 0))

    middle = pl.BlockSpec((BL, width), lambda d, s: (0, s[8]))
    return call(
        mlp_out_kernel,
        (2,),
        [whole((BL, 2 * quarter))] * 2 + [weight(6), weight(7), middle, middle],
        [whole((2 * BL, width))] * 2,
        [sds((2 * BL, width), bf16), sds((2 * BL, width), f32)],
        prefetch=1,
        flops=44 * 10**8,
        nbytes=12 * 10**6,
    )(hosts, *acts, mlp_full, mlp_full, *middles)


def adam_step(gradient, moment_one, moment_two, weight, rate_table, decay_weight):
    step_count = f32(STEP)
    first_new = beta_first * moment_one + (1.0 - beta_first) * gradient
    second_new = beta_second * moment_two + (1.0 - beta_second) * gradient * gradient
    fixed_one = 1.0 - jnp.power(beta_first, step_count)
    fixed_two = 1.0 - jnp.power(beta_second, step_count)
    update = first_new / fixed_one / (jnp.sqrt(second_new / fixed_two) + epsilon_adam)
    return (first_new, second_new, weight - rate_table * (update + decay_weight * weight))


def body(
    tokens,
    cotangent,
    segments,
    owners,
    attn_master,
    attn_first,
    attn_second,
    mlp_master,
    mlp_first,
    mlp_second,
    ssm_params,
    ssm_first,
    ssm_second,
    norm_gains,
    gains_first,
    gains_second,
):
    rows = tokens.shape[1]
    width = tokens.shape[2]
    blocks = rows // BL
    dp_count = lax.axis_size("dp")
    dp_here = lax.axis_index("dp")
    side = lax.axis_index("tensor")
    group = dp_here // (dp_count // OWNER_GROUPS)
    quarter = mlp_master.shape[2] // 2

    def both_sides(own, other):
        return jnp.where(
            side == 0,
            jnp.concatenate([own, other], axis=-1),
            jnp.concatenate([other, own], axis=-1),
        )

    def side_of(values, which):
        return lax.dynamic_slice_in_dim(values, which * width, width, values.ndim - 1)

    smem = pl.BlockSpec(memory_space=pltpu.SMEM)
    vmem = pl.BlockSpec(memory_space=pltpu.VMEM)
    hosts, rates = pl.pallas_call(
        plan_kernel,
        in_specs=[smem, smem],
        out_specs=[smem, smem],
        out_shape=[sds((PLAN_SIZE,), i32), sds((4,), f32)],
    )(owners, jnp.stack([side, group]).astype(i32))
    attn_here = hosts[ATTN_HERE]
    mlp_here = hosts[MLP_HERE]
    near = hosts[NEAR] == 1
    ring = Ring()

    attn_low = attn_master.astype(bf16)
    mlp_low = mlp_master[0].astype(bf16)
    attn_moved = move(attn_low[1], hosts[WAY], ATTN_WAYS, False)
    attn_block = jnp.where(attn_here == 0, attn_moved, attn_low[0])
    mlp_moved = exchange_groups(mlp_low[:, quarter:], near)

    tok = tokens.reshape(rows, width)
    cot = cotangent.reshape(rows, width)
    tok_f = tok.astype(f32)
    square_here = jnp.sum(tok_f * tok_f, axis=1)
    square_other = swap_x(square_here)
    tok_other = swap_x(tok)
    gains_other = swap_x(norm_gains)
    inverse_one = lax.rsqrt((square_here + square_other) / D + epsilon_norm)
    scaled_own = tok_f * inverse_one[:, None]
    hidden_own = (scaled_own * norm_gains[0]).astype(bf16)
    gains_full = both_sides(norm_gains, gains_other)

    seg = segments.reshape(rows)
    prior = lax.ppermute(seg[rows - CTX :] + 1, "dp", [(i, i + 1) for i in range(dp_count - 1)]) - 1
    seg_ext = jnp.concatenate([prior[CTX - 1 :], seg])
    seg_col = seg[:, None]

    param_lanes = ssm_params.transpose(0, 2, 1)
    decay_rate = jnp.exp(param_lanes[0]) * (BL ** (-0.5) / 32.0)
    drive_root = jnp.sqrt(-jnp.expm1(-2.0 * decay_rate))
    reading = param_lanes[2] * drive_root * param_lanes[1]

    def doubled(values):
        lanes = values.reshape(STATE, 4, 128)
        return jnp.concatenate([lanes] * blocks, axis=1)

    rate_lanes = doubled(decay_rate)
    reading_lanes = doubled(reading)
    state_shape = sds((STATE, 8, 128), f32)

    def plain(kernel, scalars, count, outs, cost, scratch=()):
        return pl.pallas_call(
            kernel,
            in_specs=[smem] * scalars + [vmem] * count,
            out_specs=[vmem] * len(outs),
            out_shape=outs,
            scratch_shapes=scratch,
            name=kernel.__name__,
            compiler_params=pltpu.CompilerParams(vmem_limit_bytes=16 * 1024 * 1024),
            cost_estimate=pl.CostEstimate(flops=cost // COST, bytes_accessed=10**6 // COST, transcendentals=0),
        )

    hidden_lanes = to_lanes(hidden_own.astype(f32), blocks, BL)
    tail_lanes = sds((CTX, 8, 128), f32)
    tail_part, state_ends, device_end = plain(
        scan_kernel, 1, 3, [tail_lanes, state_shape, state_shape], 4 * 10**9
    )(gate(seg_ext, attn_moved), hidden_lanes, rate_lanes, reading_lanes)
    id_rows = jnp.where(
        (jnp.arange(16) == 0)[:, None], seg[rows - 1].astype(f32), seg[0].astype(f32)
    )
    message = jnp.concatenate(
        [device_end.reshape(STATE * 8, 128), jnp.broadcast_to(id_rows, (16, 128))], axis=0
    ).astype(bf16)
    attn_full, states_all, gathered = ring.all_gather(attn_block, message, {0: (mlp_moved,), 2: (tok_other,)})
    mlp_block_low = jnp.where(
        mlp_here == 0, gate(mlp_moved, gathered, states_all), mlp_low[:, :quarter]
    )
    mlp_full = lax.all_gather(mlp_block_low, "dp", axis=0, tiled=True)
    mlp_full = mlp_full.reshape(OWNER_GROUPS, D, quarter)
    attn_full = attn_full.reshape(OWNER_GROUPS, D, width)
    hidden_full = join_sides(
        hosts,
        tok,
        tok_other,
        (inverse_one[:, None], norm_gains[0:1], gains_other[0:1]),
    )
    tok_full = join_sides(hosts, tok, tok_other)
    ids_all = states_all[:, STATE * 8 : STATE * 8 + 2, 0].astype(i32)
    places = jnp.arange(dp_count, dtype=i32)
    use_before = jnp.logical_and(places < dp_here, ids_all[:, 0] == seg_ext[0]).astype(i32)
    use_after = jnp.logical_and(places > dp_here, ids_all[:, 1] == seg[rows - 1]).astype(i32)
    tails, state_starts = plain(
        tail_kernel, 2, 5, [tail_lanes, state_shape], 10**9, [pltpu.VMEM((STATE, 8, 128), f32)]
    )(seg_ext, use_before, states_all, state_ends, rate_lanes, reading_lanes, tail_part)
    sens_states, sens_starts = plain(sens_kernel, 1, 3, [state_shape] * 2, 6 * 10**9)(
        seg_ext, hidden_lanes, state_starts, rate_lanes
    )
    tails = from_lanes(tails, blocks, CTX).astype(bf16)
    context_own = shift_tails(tails[blocks - 1], 1, False)
    context_other = shift_tails(tails[blocks - 1], 1, True)
    inner_own = tails[: blocks - 1]
    inner_other = swap_x(inner_own)
    context_full = jnp.concatenate(
        [
            both_sides(context_own, context_other)[None],
            both_sides(inner_own, inner_other),
        ],
        axis=0,
    ).reshape(-1, D)

    cot_other = swap_x(gate(cot, inner_other))

    seg_rows = []
    for b in range(blocks):
        before = prior if b == 0 else seg[b * BL - CTX : b * BL]
        seg_rows.append(jnp.concatenate([before, seg[b * BL : (b + 1) * BL]])[None])
    kept = []
    mixed = []
    mixed_other = []
    for b in range(blocks):
        outs = attend_forward(
            hosts, b, hidden_full, context_full, attn_full, seg_col, seg_rows[b], width
        )
        kept.append(outs[:7])
        mixed.append(outs[7])
        mixed_other.append(swap_x(outs[7]))
    wo_own = lax.dynamic_index_in_dim(attn_full, hosts[3], 0, keepdims=False)
    wo_half = lax.dynamic_slice_in_dim(wo_own, ring.core * (D // 2), D // 2, 0)
    wo_first = swap_x(wo_half)
    wo_second = lax.ppermute(gate(wo_first, mixed[0]), "dp", ring.cores)
    joined = together(*mixed_other, sens_states, sens_starts)
    mixed_other, (sens_states, sens_starts) = list(joined[:blocks]), joined[blocks:]
    wo_other = jnp.where(
        ring.core == 0,
        jnp.concatenate([wo_first, wo_second], axis=0),
        jnp.concatenate([wo_second, wo_first], axis=0),
    )

    cot_full = join_sides(hosts, gate(cot, mixed[0]), cot_other)

    gain_two = gains_full[1:2]
    middles, hiddens, acts, pres, grads, grads_other = [], [], [], [], [], []
    for b in range(blocks):
        middle, hidden_two, act, grad_pre, grad_low = mlp_block(
            hosts,
            b,
            mixed[b],
            mixed_other[b],
            attn_full,
            wo_other,
            tok_full,
            gain_two,
            cot_full,
            mlp_full,
        )
        middles.append(middle)
        hiddens.append(hidden_two)
        acts.append(act)
        pres.append(grad_pre)
        grads.append(grad_low)
        grads_other.append(swap_x(grad_low))
    mlp_sum_in = mlp_grads(hosts, hiddens, cot_full, pres, acts)
    grads_other[0], mlp_sum_in = lax.optimization_barrier((grads_other[0], mlp_sum_in))
    mlp_sum = lax.psum_scatter(
        mlp_sum_in.reshape(OWNER_GROUPS * D, quarter), "dp", scatter_dimension=0, tiled=True
    )

    lows, grad_mids, gain_twos, grad_blocks = [], [], [], []
    parts, parts_sent, ctx_parts, ctx_sent, row_sums = [], [], [], [], []
    for b in range(blocks):
        outs = attend_backward(
            hosts,
            b,
            gate(grads[b], *lows),
            grads_other[b],
            cot_full,
            middles[b],
            gain_two,
            tok_full,
            gains_full[0:1],
            attn_full,
            kept[b],
            width,
        )
        lows.append(outs[0])
        grad_mids.append(side_of(outs[1], side))
        gain_twos.append(side_of(outs[2], side))
        grad_blocks.append(list(outs[3:8]) + [mixed[b]])
        parts.append(outs[8])
        parts_sent.append(outs[9])
        ctx_parts.append(outs[10])
        ctx_sent.append(outs[11])
        row_sums.append(outs[12][:, 0])
    grad_tails = jnp.stack(
        [ctx_parts[b] + swap_x(ctx_sent[b]).astype(f32) for b in range(1, blocks)]
        + [
            shift_tails(ctx_parts[0].astype(bf16), -1, False).astype(f32)
            + shift_tails(ctx_sent[0], -1, True).astype(f32)
        ]
    )
    tail_grad_lanes = to_lanes(grad_tails.reshape(blocks * CTX, width), blocks, CTX)
    own_back, device_back = plain(back_total_kernel, 1, 3, [state_shape, state_shape], 10**9)(
        seg_ext, tail_grad_lanes, rate_lanes, reading_lanes
    )
    attn_sum_in = attn_grads(hosts, hidden_full, context_full, lows, grad_blocks, width)
    acts[0] = gate(acts[0], device_back)
    out_send, out_own = mlp_out(hosts, acts, mlp_full, middles, width)
    received = [swap_x(v) for v in parts_sent]
    block_out = (out_own + swap_x(gate(out_send, *received)).astype(f32)).astype(bf16)

    attn_sum, back_all, mlp_sum = ring.reduce_scatter(
        attn_sum_in.reshape(dp_count, -1, width),
        device_back.reshape(STATE * 8, 128).astype(bf16),
        mlp_sum,
    )
    mlp_back = exchange_groups(mlp_sum, near)
    attn_sum = attn_sum.astype(bf16)
    grad_c_lanes, grad_a_lanes, sens_end = plain(
        sens_tail_kernel, 1, 5, [state_shape] * 3, 2 * 10**9
    )(seg_ext, hidden_lanes, tail_grad_lanes, sens_states, sens_starts, rate_lanes)
    grad_lanes, grad_a_lanes = plain(
        back_scan_kernel,
        2,
        7,
        [sds((BL, 8, 128), f32), state_shape],
        4 * 10**9,
        [pltpu.VMEM((STATE, 8, 128), f32)],
    )(
        seg_ext,
        use_after,
        back_all,
        tail_grad_lanes,
        own_back,
        sens_end,
        grad_a_lanes,
        rate_lanes,
        reading_lanes,
    )
    grad_channels = lax.optimization_barrier(
        from_lanes(grad_lanes, blocks, BL).reshape(rows, width)
    )

    part = jnp.concatenate(parts, axis=0)
    received = jnp.concatenate(received, axis=0)
    row_here = inverse_one * jnp.concatenate(row_sums) + jnp.sum(
        grad_channels * (scaled_own * norm_gains[0]), axis=1
    )
    row_total = row_here + swap_x(row_here)
    grad_hidden = part + received.astype(f32) + grad_channels
    grad_tokens = jnp.concatenate(grad_mids, axis=0) + inverse_one[:, None] * (
        grad_hidden * norm_gains[0] - scaled_own * (row_total / D)[:, None]
    )
    gain_one = jnp.sum(grad_hidden * scaled_own, axis=0)
    gain_two_sum = sum(gain_twos)[0]

    def merged(values):
        return sum(values[:, 4 * b : 4 * b + 4] for b in range(blocks)).reshape(STATE, width)

    small, mlp_back = total_dp(
        jnp.concatenate(
            [merged(grad_c_lanes), merged(grad_a_lanes), gain_one[None], gain_two_sum[None]], axis=0
        ),
        mlp_back,
    )
    grad_c, grad_a = small[:STATE], small[STATE : 2 * STATE]
    gains_grad = small[2 * STATE :]
    decay_step = jnp.exp(-decay_rate)
    grad_read = grad_c * drive_root * param_lanes[1]
    grad_drive = grad_c * drive_root * param_lanes[2]
    grad_a = grad_a - grad_c * param_lanes[1] * param_lanes[2] * decay_step / drive_root
    grad_log = -decay_rate * decay_step * grad_a
    ssm_grad = jnp.stack([grad_log, grad_drive, grad_read]).transpose(0, 2, 1)

    attn_back = move(attn_sum, hosts[WAY], ATTN_WAYS, True)
    attn_grad = jnp.stack(
        [
            jnp.where(attn_here >= 1, attn_sum.astype(f32), 0.0),
            jnp.where(attn_here == 2, attn_back.astype(f32), 0.0),
        ]
    )
    mlp_grad = jnp.where(
        mlp_here == 1, jnp.concatenate([mlp_sum, mlp_back], axis=1).astype(f32), 0.0
    )[None]

    attn_rates = rates[:2, None, None]
    mlp_rates = rates[2]
    ssm_rates = jnp.asarray([1.0, 0.8, 0.25], f32)[:, None, None]
    gain_rates = jnp.asarray([0.6, 0.6], f32)[:, None]
    attn_one, attn_two, attn_new = adam_step(
        attn_grad, attn_first, attn_second, attn_master, attn_rates, matrix_decay
    )
    mlp_one, mlp_two, mlp_new = adam_step(
        mlp_grad, mlp_first, mlp_second, mlp_master, mlp_rates, matrix_decay
    )
    ssm_one, ssm_two, ssm_new = adam_step(
        ssm_grad, ssm_first, ssm_second, ssm_params, ssm_rates, 0.0
    )
    gain_first_new, gain_second_new, gains_new = adam_step(
        gains_grad, gains_first, gains_second, norm_gains, gain_rates, 0.0
    )
    return (
        block_out.reshape(tokens.shape),
        grad_tokens.reshape(tokens.shape),
        attn_grad,
        attn_one,
        attn_two,
        attn_new,
        attn_new.astype(bf16),
        mlp_grad,
        mlp_one,
        mlp_two,
        mlp_new,
        mlp_new.astype(bf16),
        ssm_grad,
        ssm_one,
        ssm_two,
        ssm_new,
        gains_grad,
        gain_first_new,
        gain_second_new,
        gains_new,
    )


def solution(mesh):
    in_specs = (
        P(None, "dp", "tensor"),
        P(None, "dp", "tensor"),
        P(None, "dp"),
        P(),
        P(None, "dp", "tensor"),
        P(None, "dp", "tensor"),
        P(None, "dp", "tensor"),
        P(None, "dp", "tensor"),
        P(None, "dp", "tensor"),
        P(None, "dp", "tensor"),
        P(None, "tensor", None),
        P(None, "tensor", None),
        P(None, "tensor", None),
        P(None, "tensor"),
        P(None, "tensor"),
        P(None, "tensor"),
    )
    out_specs = (
        P(None, "dp", "tensor"),
        P(None, "dp", "tensor"),
        P(None, "dp", "tensor"),
        P(None, "dp", "tensor"),
        P(None, "dp", "tensor"),
        P(None, "dp", "tensor"),
        P(None, "dp", "tensor"),
        P(None, "dp", "tensor"),
        P(None, "dp", "tensor"),
        P(None, "dp", "tensor"),
        P(None, "dp", "tensor"),
        P(None, "dp", "tensor"),
        P(None, "tensor", None),
        P(None, "tensor", None),
        P(None, "tensor", None),
        P(None, "tensor", None),
        P(None, "tensor"),
        P(None, "tensor"),
        P(None, "tensor"),
        P(None, "tensor"),
    )
    return jax.shard_map(body, mesh=mesh, in_specs=in_specs, out_specs=out_specs, check_vma=False)
```

time: 561 us -> 464 us (0.83)
  other arithmetic: 119 us -> 54.5 us
  Pallas kernels: 185 us -> 132 us
  local copies, waits for them, and re-layouts: 60.9 us -> 82.8 us
  waiting for transfers between devices: 105 us -> 93.7 us
  starting transfers between devices: 59.3 us -> 68.7 us
    reduce_sum x14 -> x0, other arithmetic: 52.9 us -> none  [the longest x1 16 us: body(): jnp.sum(grad_channels * (scaled_own * norm_gains[0]), axis=1)]
    unnamed x112 -> x261, local copies, waits for them, and re-layouts: 9.84 us -> 62.4 us
    ppermute x14 -> x37, waiting for transfers between devices: 33.2 us -> 64.9 us  [the longest x8 23.2 us: gather_round(): other = lax.ppermute(held, 'dp', [(i, i ^ step) for i in range(count)])]
    ppermute x15, waiting for transfers between devices: 30.7 us -> 5.49 us  [swap_x(): return lax.ppermute(values, 'tensor', SWAP)]
    pallas_call x9 -> x14, Pallas kernels: 90.6 us -> 70 us  [the longest x2 26.9 us: attend_backward(): call(attend_back_kernel, (pairs + 2,), [whole((BL, D)), whole((BL, D)), p...]
    concatenate x7 -> x1, local copies, waits for them, and re-layouts: 20 us -> 0.01 us  [body(): jnp.concatenate([device_end.reshape(STATE * 8, 128), jnp.broadcast_to(id_...]
    ppermute x14 -> x37, starting transfers between devices: 27.3 us -> 45 us  [the longest x4 14.3 us: shift_tails(): return lax.ppermute(values, ('dp', 'tensor'), pairs)]
    ppermute x4 -> x2, waiting for transfers between devices: 40.7 us -> 23.3 us  [branch(): return lambda v: lax.ppermute(v, 'dp', pairs)]
  transfers between devices with their start and end apart: 38 -> 57, of which waited for: 19 -> 22; matrix products, arithmetic and copies ran while one was open for 28% -> 17% of each run, Pallas kernels for 28% -> 26%
where the time goes in v2:
time: 464 us; the launch traced here: 456 us
  Pallas kernels  132 us (28%)
  waiting for transfers between devices  93.7 us (20%)
  local copies, waits for them, and re-layouts  82.8 us (18%)
  starting transfers between devices  68.7 us (15%)
  other arithmetic  54.5 us (12%)
  between operations  23.4 us (5%)
    unnamed x261, local copies, waits for them, and re-layouts  62.4 us
    pallas_call x2, Pallas kernels, attend_backward(): call(attend_back_kernel, (pairs + 2,), [whole((BL, D)), whole((BL, D)), p...  26.9 us
    pallas_call x2, Pallas kernels, mlp_block(): call(mlp_kernel, (2 * per,), [whole((BL, half_width)), whole((BL, half_wi...  26.3 us
    ppermute x2, waiting for transfers between devices, branch(): return lambda v: lax.ppermute(v, 'dp', pairs)  23.3 us
    ppermute x8, waiting for transfers between devices, gather_round(): other = lax.ppermute(held, 'dp', [(i, i ^ step) for i in range(count)])  23.2 us
    ppermute x15, starting transfers between devices, swap_x(): return lax.ppermute(values, 'tensor', SWAP)  17.4 us
    ppermute x3, waiting for transfers between devices, reduce_scatter(): down = lax.ppermute(down, 'dp', self.down)  15.9 us
    pallas_call x2, Pallas kernels, attend_forward(): call(attend_kernel, (pairs,), [pl.BlockSpec((BL, D), lambda p, s: (block,...  14.4 us
  transfers between devices with their start and end apart: 57, of which 22 were waited for; matrix products, arithmetic and copies ran while one was open for 17% of the time, Pallas kernels for 26%

profile of v2, /device:TPU:0, one launch (start us, length us, event | category | flops | bytes accessed | tf_op | source)
XLA Modules:
  0.0 455.6 jit_solution(15467756230514747766)
XLA Ops:
  7.3 1.9 convert_bitcast_fusion
  11.0 4.0 collective-permute-start.41
  24.3 19.0 %conditional.5 = (bf16[256,512]{1,0:T(8,128)(2,1)}) conditional(s32[]{:T(128)} %bitcast.7, bf16[256,512]{1,0:T(8,128)(2,1)S(1)} %slice_bitcast_fusion.1, bf16[256,512]{1,0:T(8,128)(2,1)S(1)} %slice_bitcast_fusion.1, bf16[256,512]{1,0:T(8,128)(2,1)S(1)} %slice_bitcast_fusion.1, ...), branch_computations={%region_1.2_spmd, %region_2.3_spmd, %region_3.4_spmd, %region_4.5_... | conditional | bytes 1048624 | solution.py:216
  24.3 3.7 collective-permute-start
  28.0 15.2 %collective-permute-done = bf16[256,512]{1,0:T(8,128)(2,1)} collective-permute-done((bf16[256,512]{1,0:T(8,128)(2,1)S(1)}, bf16[256,512]{1,0:T(8,128)(2,1)}, u32[]{:S(2)}, u32[]{:S(2)}) %collective-permute-start) | collective-permute-done | bytes 262176 | tf_op jit(solution)/shard_map/cond/branch_0_fun/ppermute | solution.py:214
  53.3 3.4 fusion.17
  56.8 4.6 %scan_kernel.1 = (f32[128,8,128]{2,1,0:T(8,128)S(1)}, f32[16,8,128]{2,1,0:T(8,128)S(1)}, f32[16,8,128]{2,1,0:T(8,128)S(1)}) custom-call(s32[1025]{0:T(1024)S(1)} %pad_add_fusion.seg_ref, f32[512,8,128]{2,1,0:T(8,128)S(1)} %bitcast.238, f32[16,8,128]{2,1,0:T(8,128)S(1)} %get-tuple-element.372.rate_ref, f32[16,8,128]{2,1,0:T(8,128)S(1)} %get-tuple-element.373.c_ref), custom_call_target="tpu_custom_call" | custom-call | flops 4000000 | bytes 1000 | tf_op jit(solution)/shard_map/scan_kernel/pallas_call | solution.py:1325
  62.3 1.9 broadcast_select_fusion.1
  65.8 2.0 collective-permute-start.42
  69.0 4.3 collective-permute-done.43
  74.5 1.7 collective-permute-start.47
  76.5 1.7 collective-permute-start.46
  78.2 1.7 bitcast_dynamic-update-slice_fusion.7
  79.9 3.1 collective-permute-done.45
  83.7 2.0 collective-permute-start.48
  87.4 1.7 collective-permute-done.50
  89.1 1.9 collective-permute-done.48
  96.2 3.6 collective-permute-done.55
  110.2 1.8 fusion.45
  114.2 1.8 tail_kernel.1
  121.6 2.6 collective-permute-start.53
  124.2 9.1 %collective-permute-start.52 = (bf16[128,512]{1,0:T(8,128)(2,1)}, bf16[128,512]{1,0:T(8,128)(2,1)}, u32[]{:S(2)}, u32[]{:S(2)}) collective-permute-start(bf16[128,512]{1,0:T(8,128)(2,1)} %bitcast.214), channel_id=1, source_target_pairs={{0,2},{1,3},{2,4},{3,5},{4,6},{5,7},{6,8},{7,9},{8,10},{9,11},{10,... | collective-permute-start | bytes 393224 | tf_op jit(solution)/shard_map/ppermute | solution.py:381
  135.0 5.1 %place_kernel.1 = bf16[8,2,256,512]{3,2,1,0:T(8,128)(2,1)S(1)} custom-call(s32[9]{0:T(128)S(1)} %stack.108.table_ref, bf16[8,256,512]{2,1,0:T(8,128)(2,1)} %bitcast_dynamic-update-slice_fusion.mine_ref, bf16[8,256,512]{2,1,0:T(8,128)(2,1)} %collective-permute-done.56.theirs_ref), custom_call_target="tpu_custom_call" | custom-call | bytes 8388 | tf_op jit(solution)/shard_map/place_kernel/pallas_call | solution.py:361
  141.1 1.9 copy-done
  147.4 2.9 join_scaled_kernel.1.hid_ref.refs_0_.refs_1_
  150.4 1.9 maximum_select_fusion.4
  152.6 7.2 %attend_kernel.3 = (bf16[512,512]{1,0:T(8,128)(2,1)S(1)}, bf16[512,512]{1,0:T(8,128)(2,1)S(1)}, bf16[512,512]{1,0:T(8,128)(2,1)S(1)}, bf16[128,512]{1,0:T(8,128)...) custom-call(s32[16]{0:T(128)S(1)} %copy-done.69, ...), custom_call_target="tpu_custom_call" | custom-call | flops 8000000 | bytes 12000 | tf_op jit(solution)/shard_map/attend_kernel/pallas_call | solution.py:732
  167.2 7.2 %attend_kernel.2 = (bf16[512,512]{1,0:T(8,128)(2,1)S(1)}, bf16[512,512]{1,0:T(8,128)(2,1)S(1)}, bf16[512,512]{1,0:T(8,128)(2,1)S(1)}, bf16[128,512]{1,0:T(8,128)...) custom-call(s32[16]{0:T(128)S(1)} %copy-done.69, ...), custom_call_target="tpu_custom_call" | custom-call | flops 8000000 | bytes 12000 | tf_op jit(solution)/shard_map/attend_kernel/pallas_call | solution.py:732
  182.1 2.1 join_kernel.2.tok_ref
  185.5 5.5 %sens_kernel.1 = (f32[16,8,128]{2,1,0:T(8,128)S(1)}, f32[16,8,128]{2,1,0:T(8,128)S(1)}) custom-call(s32[1025]{0:T(1024)S(1)} %pad_add_fusion.seg_ref, f32[512,8,128]{2,1,0:T(8,128)S(1)} %bitcast.239, f32[16,8,128]{2,1,0:T(8,128)S(1)} %get-tuple-element.231.start_ref, f32[16,8,128]{2,1,0:T(8,128)S(1)} %get-tuple-element.372.rate_ref), custom_call_target="tpu_custom_call" | custom-call | flops 6000000 | bytes 1000 | tf_op jit(solution)/shard_map/sens_kernel/pallas_call | solution.py:1355
  191.1 2.1 join_kernel.3.cot_ref.g0.g1
  193.3 2.9 maximum_select_fusion.woo_ref
  198.9 13.1 %mlp_kernel.2 = (f32[512,1024]{1,0:T(8,128)S(1)}, bf16[512,1024]{1,0:T(8,128)(2,1)S(1)}, bf16[512,2048]{1,0:T(8,128)(2,1)S(1)}, bf16[512,2048]{1,0:T(8,128)(2,1)S(1)}, bf16[512,1024]{1,0:T(8,128)(2,1)S(1)}) custom-call(s32[16]{0:T(128)S(1)} %copy-done.69, bf16[512,512]{1,0:T(8,128)(2,1)} %get-tuple-element.229.own_ref.refs_11_, ...), custom_call_target="tpu_custom_call" | custom-call | flops 8000000 | bytes 24000 | tf_op jit(solution)/shard_map/mlp_kernel/pallas_call | solution.py:1096
  214.8 13.2 %mlp_kernel.3 = (f32[512,1024]{1,0:T(8,128)S(1)}, bf16[512,1024]{1,0:T(8,128)(2,1)S(1)}, bf16[512,2048]{1,0:T(8,128)(2,1)S(1)}, bf16[512,2048]{1,0:T(8,128)(2,1)S(1)}, bf16[512,1024]{1,0:T(8,128)(2,1)S(1)}) custom-call(s32[16]{0:T(128)S(1)} %copy-done.69, bf16[512,512]{1,0:T(8,128)(2,1)} %get-tuple-element.230.own_ref.refs_17_, ...), custom_call_target="tpu_custom_call" | custom-call | flops 8000000 | bytes 24000 | tf_op jit(solution)/shard_map/mlp_kernel/pallas_call | solution.py:1096
  229.4 13.1 %mlp_grad_kernel.1 = bf16[4,1024,1024]{2,1,0:T(8,128)(2,1)} custom-call(s32[16]{0:T(128)S(1)} %copy-done.69, bf16[512,1024]{1,0:T(8,128)(2,1)S(1)} %get-tuple-element.243.h0, bf16[512,1024]{1,0:T(8,128)(2,1)S(1)} %get-tuple-element.244.h1, bf16[1024,1024]{1,0:T(8,128)(2,1)S(1)} %join_kernel.3.cot_ref.g0.g1, bf16[1024,1024]{1,0:T(8,128)(2,1)S(1)} %join_kernel.3.cot_ref.g0.g1, ...), custom_call_target="tpu_custom_call" | custom-call | flops 8600000 | bytes 20000 | tf_op jit(solution)/shard_map/mlp_grad_kernel/pallas_call | solution.py:1150
  257.1 13.6 %attend_back_kernel.2 = (bf16[512,1024]{1,0:T(8,128)(2,1)S(1)}, f32[512,1024]{1,0:T(8,128)S(1)}, f32[1,1024]{1,0:T(1,128)S(1)}, bf16[512,512]{1,0:T(8,128)(2,1)S...) custom-call(s32[16]{0:T(128)S(1)} %copy-done.69, ...), custom_call_target="tpu_custom_call" | custom-call | flops 12000000 | bytes 20000 | tf_op jit(solution)/shard_map/attend_back_kernel/pallas_call | solution.py:900
  274.4 13.3 %attend_back_kernel.3 = (bf16[512,1024]{1,0:T(8,128)(2,1)S(1)}, f32[512,1024]{1,0:T(8,128)S(1)}, f32[1,1024]{1,0:T(1,128)S(1)}, bf16[512,512]{1,0:T(8,128)(2,1)S...) custom-call(s32[16]{0:T(128)S(1)} %copy-done.69, ...), custom_call_target="tpu_custom_call" | custom-call | flops 12000000 | bytes 20000 | tf_op jit(solution)/shard_map/attend_back_kernel/pallas_call | solution.py:900
  288.7 8.4 %attn_grad_kernel.1 = bf16[4,1024,512]{2,1,0:T(8,128)(2,1)S(1)} custom-call(s32[16]{0:T(128)S(1)} %copy-done.69, bf16[1024,1024]{1,0:T(8,128)(2,1)S(1)} %copy-done.3, bf16[1024,1024]{1,0:T(8,128)(2,1)S(1)} %copy-done.3, bf16[256,1024]{1,0:T(8,128)(2,1)S(1)} %bitcast.249, bf16[256,1024]{1,0:T(8,128)(2,1)S(1)} %bitcast.250, ...), custom_call_target="tpu_custom_call" | custom-call | flops 4600000 | bytes 14000 | tf_op jit(solution)/shard_map/attn_grad_kernel/pallas_call | solution.py:1022
  308.6 5.3 %collective-permute-done.66 = bf16[128,512]{1,0:T(8,128)(2,1)S(1)} collective-permute-done((bf16[128,512]{1,0:T(8,128)(2,1)S(1)}, bf16[128,512]{1,0:T(8,128)(2,1)S(1)}, u32[]{:S(2)}, u32[]{:S(2)}) %collective-permute-start.66) | collective-permute-done | bytes 131104 | tf_op jit(solution)/shard_map/ppermute | solution.py:381
  314.2 1.7 back_total_kernel.1
  316.7 2.3 constant_dynamic-slice_fusion.2
  319.0 2.1 fusion.31
  331.0 7.4 %mlp_out_kernel.1 = (bf16[1024,512]{1,0:T(8,128)(2,1)S(1)}, f32[1024,512]{1,0:T(8,128)S(1)}) custom-call(s32[16]{0:T(128)S(1)} %copy-done.69, bf16[512,2048]{1,0:T(8,128)(2,1)S(1)} %copy-done.19, bf16[512,2048]{1,0:T(8,128)(2,1)S(1)} %copy-done.24, bf16[4,1024,1024]{2,1,0:T(8,128)(2,1)} %bitcast.264, bf16[4,1024,1024]{2,1,0:T(8,128)(2,1)} %bitcast.265, ...), custom_call_target="tpu_custom_call" | custom-call | flops 4400000 | bytes 12000 | tf_op jit(solution)/shard_map/mlp_out_kernel/pallas_call | solution.py:1203
  339.5 3.4 sens_tail_kernel.1
  348.5 3.2 collective-permute-done.77
  351.8 1.9 collective-permute-done.75
  353.7 1.8 collective-permute-done.76
  355.5 2.2 fusion.24
  358.3 1.8 collective-permute-start.80
  360.1 3.3 collective-permute-done.69
  363.4 3.2 fusion.16
  368.6 15.9 %collective-permute-done.80 = bf16[8,128,128]{2,1,0:T(8,128)(2,1)S(1)} collective-permute-done((bf16[8,128,128]{2,1,0:T(8,128)(2,1)S(1)}, bf16[8,128,128]{2,1,0:T(8,128)(2,1)S(1)}, u32[]{:S(2)}, u32[]{:S(2)}) %collective-permute-start.80) | collective-permute-done | bytes 262176 | tf_op jit(solution)/shard_map/ppermute | solution.py:98
  385.7 14.1 %collective-permute-done.79 = bf16[256,512]{1,0:T(8,128)(2,1)S(1)} collective-permute-done((bf16[256,512]{1,0:T(8,128)(2,1)S(1)}, bf16[256,512]{1,0:T(8,128)(2,1)S(1)}, u32[]{:S(2)}, u32[]{:S(2)}) %collective-permute-start.79) | collective-permute-done | bytes 262176 | tf_op jit(solution)/shard_map/ppermute | solution.py:333
  400.1 5.2 %back_scan_kernel.1 = (f32[512,8,128]{2,1,0:T(8,128)S(1)}, f32[16,8,128]{2,1,0:T(8,128)S(1)}) custom-call(s32[1025]{0:T(1024)S(1)} %pad_add_fusion.seg_ref, s32[16]{0:T(128)S(1)} %copy-done.86, bf16[16,128,128]{2,1,0:T(8,128)(2,1)S(1)} %maximum_select_fusion.2.all_ref, f32[128,8,128]{2,1,0:T(8,128)S(1)} %bitcast.253, ...), custom_call_target="tpu_custom_call" | custom-call | flops 4000000 | bytes 1000 | tf_op jit(solution)/shard_map/back_scan_kernel/pallas_call | solution.py:1481
  407.2 2.3 fusion.9
  411.1 2.2 collective-permute-done.81
  413.3 1.8 collective-permute-start.84
  415.1 3.8 fusion.8
  418.9 2.1 select_bitcast_fusion.1
  421.0 9.5 %conditional.6 = (bf16[256,512]{1,0:T(8,128)(2,1)}) conditional(s32[]{:T(128)} %bitcast.7, bf16[256,512]{1,0:T(8,128)(2,1)S(1)} %get-tuple-element.343, bf16[256,512]{1,0:T(8,128)(2,1)S(1)} %get-tuple-element.343, bf16[256,512]{1,0:T(8,128)(2,1)S(1)} %get-tuple-element.343, ...), branch_computations={%region_21.22_spmd, %region_22.23_spmd, %region_23.24_spmd, %regio... | conditional | bytes 1048624
  422.3 8.0 %collective-permute-done.18 = bf16[256,512]{1,0:T(8,128)(2,1)} collective-permute-done((bf16[256,512]{1,0:T(8,128)(2,1)S(1)}, bf16[256,512]{1,0:T(8,128)(2,1)}, u32[]{:S(2)}, u32[]{:S(2)}) %collective-permute-start.18) | collective-permute-done | bytes 262176 | tf_op jit(solution)/shard_map/cond/branch_0_fun/ppermute | solution.py:214
  431.8 8.1 %fusion.51 = (bf16[1,256,2048]{2,1,0:T(8,128)(2,1)}, f32[1,256,2048]{2,1,0:T(8,128)}, f32[1,256,2048]{2,1,0:T(8,128)}, f32[1,256,2048]{2,1,0:T(8,128)}, f32[1,256,2048]{2,1,0:T(8,128)}) fusion(f32[1,256,2048]{2,1,0:T(8,128)S(1)} %copy-done.93, f32[]{:T(128)} %bitcast.95, f32[1,256,2048]{2,1,0:T(8,128)} %param.63, f32[1,256,2048]{2,1,0:T(8,128)} %param.62, ...), kind=kLoop, calls=%fused_computation.151 | loop fusion | flops 11010048 | bytes 16777220 | tf_op jit(solution)/shard_map/convert_element_type | solution.py:1573
  441.1 2.5 fusion.53
  443.7 2.7 collective-permute-done.88
  (434 shorter events, 136.2 us)
Async XLA Ops:
  7.2 188.9 %all-gather.2.cloned.1.call-start = ((), (), s32[]{:S(2)}) async-start(), calls=%async_computation.1 | async-start | bytes 8912896 | tf_op jit(solution)/shard_map/all_gather | solution.py:1338
  10.1 37.1 %copy-start.104 = (f32[3,512,16]{1,2,0:T(8,128)S(1)}, f32[3,512,16]{1,2,0:T(8,128)}, u32[]{:S(2)}) copy-start(f32[3,512,16]{1,2,0:T(8,128)} %param.64) | copy-start | bytes 294916
  11.0 51.4 %collective-permute-start.41 = (bf16[256,1024]{1,0:T(8,128)(2,1)}, bf16[256,1024]{1,0:T(8,128)(2,1)}, u32[]{:S(2)}, u32[]{:S(2)}) collective-permute-start(bf16[256,1024]{1,0:T(8,128)(2,1)} %slice.185), channel_id=1, source_target_pairs={{0,16},{2,18},{4,20},{6,22},{8,24},{10,26},{12,28},{14,30},{16,0},... | collective-permute-start | bytes 1572872 | tf_op jit(solution)/shard_map/ppermute | solution.py:223
  15.0 47.3 %collective-permute-start.40 = (bf16[256,1024]{1,0:T(8,128)(2,1)}, bf16[256,1024]{1,0:T(8,128)(2,1)}, u32[]{:S(2)}, u32[]{:S(2)}) collective-permute-start(bf16[256,1024]{1,0:T(8,128)(2,1)} %slice.185), channel_id=1, source_target_pairs={{0,8},{2,10},{4,12},{6,14},{8,0},{10,2},{12,4},{14,6},{16,24},{18,... | collective-permute-start | bytes 1572872 | tf_op jit(solution)/shard_map/ppermute | solution.py:223
  17.1 34.0 %collective-permute-start.39 = (s32[128]{0:T(128)S(1)}, s32[128]{0:T(128)S(1)}, u32[]{:S(2)}, u32[]{:S(2)}) collective-permute-start(s32[128]{0:T(128)S(1)} %get-tuple-element.360), channel_id=1, source_target_pairs={{0,2},{2,4},{4,6},{6,8},{8,10},{10,12},{12,14},{14,16},{16,18},{18... | collective-permute-start | bytes 1544 | tf_op jit(solution)/shard_map/ppermute | solution.py:1294
  18.7 33.8 %collective-permute-start.37 = (f32[1024]{0:T(1024)S(1)}, f32[1024]{0:T(1024)S(1)}, u32[]{:S(2)}, u32[]{:S(2)}) collective-permute-start(f32[1024]{0:T(1024)S(1)} %fusion.10), channel_id=1, source_target_pairs={{0,1},{1,0},{2,3},{3,2},{4,5},{5,4},{6,7},{7,6},{8,9},{9,8},{10,11... | collective-permute-start | bytes 12296 | tf_op jit(solution)/shard_map/ppermute | solution.py:78
  24.3 19.0 %collective-permute-start = (bf16[256,512]{1,0:T(8,128)(2,1)S(1)}, bf16[256,512]{1,0:T(8,128)(2,1)}, u32[]{:S(2)}, u32[]{:S(2)}) collective-permute-start(bf16[256,512]{1,0:T(8,128)(2,1)S(1)} %param), channel_id=1, source_target_pairs={{0,8},{2,10},{4,12},{6,14},{1,9},{3,11},{5,13},{7,15}} | collective-permute-start | bytes 786440 | tf_op jit(solution)/shard_map/cond/branch_0_fun/ppermute | solution.py:214
  43.3 36.6 %collective-permute-start.36 = (bf16[1024,512]{1,0:T(8,128)(2,1)S(1)}, bf16[1024,512]{1,0:T(8,128)(2,1)}, u32[]{:S(2)}, u32[]{:S(2)}) collective-permute-start(bf16[1024,512]{1,0:T(8,128)(2,1)S(1)} %bitcast.235), channel_id=1, source_target_pairs={{0,1},{1,0},{2,3},{3,2},{4,5},{5,4},{6,7},{7,6},{8,9},{9,8},{10,11... | collective-permute-start | bytes 3145736 | tf_op jit(solution)/shard_map/ppermute | solution.py:78
  50.5 95.9 %copy-start.82 = (f32[1,512]{1,0:T(1,128)}, f32[1,512]{1,0:T(1,128)S(1)}, u32[]{:S(2)}) copy-start(f32[1,512]{1,0:T(1,128)S(1)} %slice.138.gain_ref) | copy-start | bytes 6148
  56.8 128.7 %copy-start.9 = (f32[2,512,4,128]{3,2,0,1:T(4,128)}, f32[2,512,4,128]{3,2,0,1:T(4,128)S(1)}, u32[]{:S(2)}) copy-start(f32[2,512,4,128]{3,2,0,1:T(4,128)S(1)} %fusion.17) | copy-start | bytes 6291460
  64.3 9.0 %collective-permute-start.43 = (bf16[256,512]{1,0:T(8,128)(2,1)}, bf16[256,512]{1,0:T(8,128)(2,1)}, u32[]{:S(2)}, u32[]{:S(2)}) collective-permute-start(bf16[256,512]{1,0:T(8,128)(2,1)} %fusion.33), channel_id=1, source_target_pairs={{8,0},{10,2},{16,8},{18,10},{24,16},{26,18},{28,24},{30,26},{20,28... | collective-permute-start | bytes 786440 | tf_op jit(solution)/shard_map/ppermute | solution.py:348
  65.8 8.7 %collective-permute-start.42 = (bf16[256,512]{1,0:T(8,128)(2,1)}, bf16[256,512]{1,0:T(8,128)(2,1)}, u32[]{:S(2)}, u32[]{:S(2)}) collective-permute-start(bf16[256,512]{1,0:T(8,128)(2,1)} %fusion.33), channel_id=1, source_target_pairs={{0,8},{2,10},{8,16},{10,18},{16,24},{18,26},{24,28},{26,30},{28,20... | collective-permute-start | bytes 786440 | tf_op jit(solution)/shard_map/ppermute | solution.py:346
  67.8 1.2 collective-permute-start.44
  74.5 5.4 %collective-permute-start.47 = (bf16[2,144,128]{2,1,0:T(8,128)(2,1)S(1)}, bf16[2,144,128]{2,1,0:T(8,128)(2,1)S(1)}, u32[]{:S(2)}, u32[]{:S(2)}) collective-permute-start(bf16[2,144,128]{2,1,0:T(8,128)(2,1)S(1)} %maximum_select_fusion.9), channel_id=1, source_target_pairs={{0,4},{2,6},{4,0},{6,2},{8,12},{10,14},{12,8},{14,10},{16,20},{18,... | collective-permute-start | bytes 221192 | tf_op jit(solution)/shard_map/ppermute | solution.py:98
  76.2 6.8 %collective-permute-start.45 = (bf16[256,512]{1,0:T(8,128)(2,1)}, bf16[256,512]{1,0:T(8,128)(2,1)S(1)}, u32[]{:S(2)}, u32[]{:S(2)}) collective-permute-start(bf16[256,512]{1,0:T(8,128)(2,1)} %collective-permute-done.42), channel_id=1, source_target_pairs={{0,8},{2,10},{8,16},{10,18},{16,24},{18,26},{24,28},{26,30},{28,20... | collective-permute-start | bytes 786440 | tf_op jit(solution)/shard_map/ppermute | solution.py:346
  76.5 7.2 %collective-permute-start.46 = (bf16[256,512]{1,0:T(8,128)(2,1)}, bf16[256,512]{1,0:T(8,128)(2,1)S(1)}, u32[]{:S(2)}, u32[]{:S(2)}) collective-permute-start(bf16[256,512]{1,0:T(8,128)(2,1)} %collective-permute-done.43), channel_id=1, source_target_pairs={{8,0},{10,2},{16,8},{18,10},{24,16},{26,18},{28,24},{30,26},{20,28... | collective-permute-start | bytes 786440 | tf_op jit(solution)/shard_map/ppermute | solution.py:348
  83.7 5.4 %collective-permute-start.50 = (bf16[4,144,128]{2,1,0:T(8,128)(2,1)S(1)}, bf16[4,144,128]{2,1,0:T(8,128)(2,1)S(1)}, u32[]{:S(2)}, u32[]{:S(2)}) collective-permute-start(bf16[4,144,128]{2,1,0:T(8,128)(2,1)S(1)} %maximum_select_fusion.7), channel_id=1, source_target_pairs={{0,8},{2,10},{4,12},{6,14},{8,0},{10,2},{12,4},{14,6},{16,24},{18,... | collective-permute-start | bytes 442376 | tf_op jit(solution)/shard_map/ppermute | solution.py:98
  83.7 7.3 %collective-permute-start.48 = (bf16[256,512]{1,0:T(8,128)(2,1)S(1)}, bf16[256,512]{1,0:T(8,128)(2,1)S(1)}, u32[]{:S(2)}, u32[]{:S(2)}) collective-permute-start(bf16[256,512]{1,0:T(8,128)(2,1)S(1)} %collective-permute-done.45), channel_id=1, source_target_pairs={{0,8},{2,10},{8,16},{10,18},{16,24},{18,26},{24,28},{26,30},{28,20... | collective-permute-start | bytes 786440 | tf_op jit(solution)/shard_map/ppermute | solution.py:346
  85.7 6.4 %collective-permute-start.49 = (bf16[256,512]{1,0:T(8,128)(2,1)S(1)}, bf16[256,512]{1,0:T(8,128)(2,1)S(1)}, u32[]{:S(2)}, u32[]{:S(2)}) collective-permute-start(bf16[256,512]{1,0:T(8,128)(2,1)S(1)} %collective-permute-done.46), channel_id=1, source_target_pairs={{8,0},{10,2},{16,8},{18,10},{24,16},{26,18},{28,24},{30,26},{20,28... | collective-permute-start | bytes 786440 | tf_op jit(solution)/shard_map/ppermute | solution.py:348
  92.1 7.7 %collective-permute-start.55 = (bf16[256,512]{1,0:T(8,128)(2,1)S(1)}, bf16[256,512]{1,0:T(8,128)(2,1)S(1)}, u32[]{:S(2)}, u32[]{:S(2)}) collective-permute-start(bf16[256,512]{1,0:T(8,128)(2,1)S(1)} %collective-permute-done.48), channel_id=1, source_target_pairs={{0,8},{2,10},{8,16},{10,18},{16,24},{18,26},{24,28},{26,30},{28,20... | collective-permute-start | bytes 786440 | tf_op jit(solution)/shard_map/ppermute | solution.py:346
  94.2 10.6 %collective-permute-start.51 = (bf16[8,144,128]{2,1,0:T(8,128)(2,1)S(1)}, bf16[8,144,128]{2,1,0:T(8,128)(2,1)S(1)}, u32[]{:S(2)}, u32[]{:S(2)}) collective-permute-start(bf16[8,144,128]{2,1,0:T(8,128)(2,1)S(1)} %maximum_select_fusion.3), channel_id=1, source_target_pairs={{0,16},{2,18},{4,20},{6,22},{8,24},{10,26},{12,28},{14,30},{16,0},... | collective-permute-start | bytes 884744 | tf_op jit(solution)/shard_map/ppermute | solution.py:98
  106.6 251.1 %reduce-scatter.2.cloned.1.call-start = ((), (), s32[]{:S(2)}) async-start(), calls=%async_computation.2 | async-start | bytes 8912896 | tf_op jit(solution)/shard_map/reduce_scatter | solution.py:1424
  106.6 28.4 %collective-permute-start.56 = (bf16[8,256,512]{2,1,0:T(8,128)(2,1)}, bf16[8,256,512]{2,1,0:T(8,128)(2,1)}, u32[]{:S(2)}, u32[]{:S(2)}) collective-permute-start(bf16[8,256,512]{2,1,0:T(8,128)(2,1)} %bitcast_dynamic-update-slice_fusion.mine_ref), channel_id=1, source_target_pairs={{0,2},{2,0},{4,6},{6,4},{8,10},{10,8},{12,14},{14,12},{16,18},{18,... | collective-permute-start | bytes 6291464 | tf_op jit(solution)/shard_map/ppermute | solution.py:350
  106.7 39.0 %collective-permute-start.38 = (f32[2,512]{1,0:T(2,128)}, f32[2,512]{1,0:T(2,128)}, u32[]{:S(2)}, u32[]{:S(2)}) collective-permute-start(f32[2,512]{1,0:T(2,128)} %param.67), channel_id=1, source_target_pairs={{0,1},{1,0},{2,3},{3,2},{4,5},{5,4},{6,7},{7,6},{8,9},{9,8},{10,11... | collective-permute-start | bytes 12296 | tf_op jit(solution)/shard_map/ppermute | solution.py:78
  117.8 15.6 %collective-permute-start.54 = (bf16[1,128,512]{2,1,0:T(8,128)(2,1)S(1)}, bf16[1,128,512]{2,1,0:T(8,128)(2,1)S(1)}, u32[]{:S(2)}, u32[]{:S(2)}) collective-permute-start(bf16[1,128,512]{2,1,0:T(8,128)(2,1)S(1)} %slice.157), channel_id=1, source_target_pairs={{0,1},{1,0},{2,3},{3,2},{4,5},{5,4},{6,7},{7,6},{8,9},{9,8},{10,11... | collective-permute-start | bytes 393224 | tf_op jit(solution)/shard_map/ppermute | solution.py:78
  121.6 28.8 %collective-permute-start.53 = (bf16[128,512]{1,0:T(8,128)(2,1)}, bf16[128,512]{1,0:T(8,128)(2,1)}, u32[]{:S(2)}, u32[]{:S(2)}) collective-permute-start(bf16[128,512]{1,0:T(8,128)(2,1)} %bitcast.214), channel_id=1, source_target_pairs={{0,3},{1,2},{2,5},{3,4},{4,7},{5,6},{6,9},{7,8},{8,11},{9,10},{10,... | collective-permute-start | bytes 393224 | tf_op jit(solution)/shard_map/ppermute | solution.py:381
  124.2 26.2 %collective-permute-start.52 = (bf16[128,512]{1,0:T(8,128)(2,1)}, bf16[128,512]{1,0:T(8,128)(2,1)}, u32[]{:S(2)}, u32[]{:S(2)}) collective-permute-start(bf16[128,512]{1,0:T(8,128)(2,1)} %bitcast.214), channel_id=1, source_target_pairs={{0,2},{1,3},{2,4},{3,5},{4,6},{5,7},{6,8},{7,9},{8,10},{9,11},{10,... | collective-permute-start | bytes 393224 | tf_op jit(solution)/shard_map/ppermute | solution.py:381
  133.5 57.6 %collective-permute-start.61 = (bf16[1024,512]{1,0:T(8,128)(2,1)}, bf16[1024,512]{1,0:T(8,128)(2,1)}, u32[]{:S(2)}, u32[]{:S(2)}) collective-permute-start(bf16[1024,512]{1,0:T(8,128)(2,1)} %bitcast.255), channel_id=1, source_target_pairs={{0,1},{1,0},{2,3},{3,2},{4,5},{5,4},{6,7},{7,6},{8,9},{9,8},{10,11... | collective-permute-start | bytes 3145736 | tf_op jit(solution)/shard_map/ppermute | solution.py:78
  143.0 37.6 %collective-permute-start.59 = (bf16[512,512]{1,0:T(8,128)(2,1)}, bf16[512,512]{1,0:T(8,128)(2,1)}, u32[]{:S(2)}, u32[]{:S(2)}) collective-permute-start(bf16[512,512]{1,0:T(8,128)(2,1)} %dynamic-slice_bitcast_fusion.1), channel_id=1, source_target_pairs={{0,1},{1,0},{2,3},{3,2},{4,5},{5,4},{6,7},{7,6},{8,9},{9,8},{10,11... | collective-permute-start | bytes 1572872 | tf_op jit(solution)/shard_map/ppermute | solution.py:78
  165.7 27.6 %collective-permute-start.58 = (bf16[512,512]{1,0:T(8,128)(2,1)}, bf16[512,512]{1,0:T(8,128)(2,1)}, u32[]{:S(2)}, u32[]{:S(2)}) collective-permute-start(bf16[512,512]{1,0:T(8,128)(2,1)} %get-tuple-element.230.own_ref.refs_17_), channel_id=1, source_target_pairs={{0,1},{1,0},{2,3},{3,2},{4,5},{5,4},{6,7},{7,6},{8,9},{9,8},{10,11... | collective-permute-start | bytes 1572872 | tf_op jit(solution)/shard_map/ppermute | solution.py:78
  180.2 13.1 %collective-permute-start.57 = (bf16[512,512]{1,0:T(8,128)(2,1)}, bf16[512,512]{1,0:T(8,128)(2,1)}, u32[]{:S(2)}, u32[]{:S(2)}) collective-permute-start(bf16[512,512]{1,0:T(8,128)(2,1)} %get-tuple-element.229.own_ref.refs_11_), channel_id=1, source_target_pairs={{0,1},{1,0},{2,3},{3,2},{4,5},{5,4},{6,7},{7,6},{8,9},{9,8},{10,11... | collective-permute-start | bytes 1572872 | tf_op jit(solution)/shard_map/ppermute | solution.py:78
  180.7 12.6 %collective-permute-start.60 = (bf16[512,512]{1,0:T(8,128)(2,1)}, bf16[512,512]{1,0:T(8,128)(2,1)}, u32[]{:S(2)}, u32[]{:S(2)}) collective-permute-start(bf16[512,512]{1,0:T(8,128)(2,1)} %collective-permute-done.59), channel_id=1, source_target_pairs={{0,2},{2,0},{4,6},{6,4},{8,10},{10,8},{12,14},{14,12},{16,18},{18,... | collective-permute-start | bytes 1572872 | tf_op jit(solution)/shard_map/ppermute | solution.py:1390
  213.3 29.2 %collective-permute-start.62 = (bf16[512,1024]{1,0:T(8,128)(2,1)S(1)}, bf16[512,1024]{1,0:T(8,128)(2,1)S(1)}, u32[]{:S(2)}, u32[]{:S(2)}) collective-permute-start(bf16[512,1024]{1,0:T(8,128)(2,1)S(1)} %get-tuple-element.242.own_ref), channel_id=1, source_target_pairs={{0,1},{1,0},{2,3},{3,2},{4,5},{5,4},{6,7},{7,6},{8,9},{9,8},{10,11... | collective-permute-start | bytes 3145736 | tf_op jit(solution)/shard_map/ppermute | solution.py:78
  243.6 30.2 %collective-permute-start.63 = (bf16[512,1024]{1,0:T(8,128)(2,1)}, bf16[512,1024]{1,0:T(8,128)(2,1)}, u32[]{:S(2)}, u32[]{:S(2)}) collective-permute-start(bf16[512,1024]{1,0:T(8,128)(2,1)} %copy-done.36), channel_id=1, source_target_pairs={{0,1},{1,0},{2,3},{3,2},{4,5},{5,4},{6,7},{7,6},{8,9},{9,8},{10,11... | collective-permute-start | bytes 3145736 | tf_op jit(solution)/shard_map/ppermute | solution.py:78
  257.0 17.3 %copy-start.45 = (bf16[512,512]{1,0:T(8,128)(2,1)S(1)}, bf16[512,512]{1,0:T(8,128)(2,1)}, u32[]{:S(2)}) copy-start(bf16[512,512]{1,0:T(8,128)(2,1)} %copy-done.44) | copy-start | bytes 1572868
  257.0 17.3 %copy-start.47 = (bf16[512,512]{1,0:T(8,128)(2,1)S(1)}, bf16[512,512]{1,0:T(8,128)(2,1)}, u32[]{:S(2)}) copy-start(bf16[512,512]{1,0:T(8,128)(2,1)} %copy-done.46) | copy-start | bytes 1572868
  257.0 17.3 %copy-start.49 = (bf16[4,512,128]{2,1,0:T(8,128)(2,1)S(1)}, bf16[4,512,128]{2,1,0:T(8,128)(2,1)}, u32[]{:S(2)}) copy-start(bf16[4,512,128]{2,1,0:T(8,128)(2,1)} %copy-done.48) | copy-start | bytes 1572868
  299.7 19.3 %collective-permute-start.70 = (bf16[8,256,512]{2,1,0:T(8,128)(2,1)}, bf16[8,256,512]{2,1,0:T(8,128)(2,1)}, u32[]{:S(2)}, u32[]{:S(2)}) collective-permute-start(bf16[8,256,512]{2,1,0:T(8,128)(2,1)} %dynamic-slice_bitcast_fusion), channel_id=1, source_target_pairs={{0,2},{2,0},{4,6},{6,4},{8,10},{10,8},{12,14},{14,12},{16,18},{18,... | collective-permute-start | bytes 6291464 | tf_op jit(solution)/shard_map/ppermute | solution.py:310
  299.7 7.2 %collective-permute-start.64 = (bf16[128,512]{1,0:T(8,128)(2,1)}, bf16[128,512]{1,0:T(8,128)(2,1)S(1)}, u32[]{:S(2)}, u32[]{:S(2)}) collective-permute-start(bf16[128,512]{1,0:T(8,128)(2,1)} %get-tuple-element.268), channel_id=1, source_target_pairs={{0,1},{1,0},{2,3},{3,2},{4,5},{5,4},{6,7},{7,6},{8,9},{9,8},{10,11... | collective-permute-start | bytes 393224 | tf_op jit(solution)/shard_map/ppermute | solution.py:78
  303.8 4.8 %collective-permute-start.65 = (bf16[128,512]{1,0:T(8,128)(2,1)S(1)}, bf16[128,512]{1,0:T(8,128)(2,1)S(1)}, u32[]{:S(2)}, u32[]{:S(2)}) collective-permute-start(bf16[128,512]{1,0:T(8,128)(2,1)S(1)} %convert_element_type.377), channel_id=1, source_target_pairs={{2,0},{3,1},{4,2},{5,3},{6,4},{7,5},{8,6},{9,7},{10,8},{11,9},{12,... | collective-permute-start | bytes 393224 | tf_op jit(solution)/shard_map/ppermute | solution.py:381
  305.1 8.8 %collective-permute-start.66 = (bf16[128,512]{1,0:T(8,128)(2,1)S(1)}, bf16[128,512]{1,0:T(8,128)(2,1)S(1)}, u32[]{:S(2)}, u32[]{:S(2)}) collective-permute-start(bf16[128,512]{1,0:T(8,128)(2,1)S(1)} %copy-done.92), channel_id=1, source_target_pairs={{2,1},{3,0},{4,3},{5,2},{6,5},{7,4},{8,7},{9,6},{10,9},{11,8},{12,... | collective-permute-start | bytes 393224 | tf_op jit(solution)/shard_map/ppermute | solution.py:381
  306.4 32.0 %collective-permute-start.68 = (bf16[512,512]{1,0:T(8,128)(2,1)}, bf16[512,512]{1,0:T(8,128)(2,1)}, u32[]{:S(2)}, u32[]{:S(2)}) collective-permute-start(bf16[512,512]{1,0:T(8,128)(2,1)} %get-tuple-element.276), channel_id=1, source_target_pairs={{0,1},{1,0},{2,3},{3,2},{4,5},{5,4},{6,7},{7,6},{8,9},{9,8},{10,11... | collective-permute-start | bytes 1572872 | tf_op jit(solution)/shard_map/ppermute | solution.py:78
  306.9 31.5 %collective-permute-start.67 = (bf16[512,512]{1,0:T(8,128)(2,1)}, bf16[512,512]{1,0:T(8,128)(2,1)}, u32[]{:S(2)}, u32[]{:S(2)}) collective-permute-start(bf16[512,512]{1,0:T(8,128)(2,1)} %get-tuple-element.275), channel_id=1, source_target_pairs={{0,1},{1,0},{2,3},{3,2},{4,5},{5,4},{6,7},{7,6},{8,9},{9,8},{10,11... | collective-permute-start | bytes 1572872 | tf_op jit(solution)/shard_map/ppermute | solution.py:78
  315.9 3.1 collective-permute-start.71
  321.1 22.5 %collective-permute-start.72 = (bf16[256,512]{1,0:T(8,128)(2,1)}, bf16[256,512]{1,0:T(8,128)(2,1)}, u32[]{:S(2)}, u32[]{:S(2)}) collective-permute-start(bf16[256,512]{1,0:T(8,128)(2,1)} %get-tuple-element.293), channel_id=1, source_target_pairs={{0,8},{2,10},{8,16},{10,18},{16,24},{18,26},{24,28},{26,30},{28,20... | collective-permute-start | bytes 786440 | tf_op jit(solution)/shard_map/ppermute | solution.py:329
  322.0 21.7 %collective-permute-start.73 = (bf16[256,512]{1,0:T(8,128)(2,1)S(1)}, bf16[256,512]{1,0:T(8,128)(2,1)}, u32[]{:S(2)}, u32[]{:S(2)}) collective-permute-start(bf16[256,512]{1,0:T(8,128)(2,1)S(1)} %get-tuple-element.294), channel_id=1, source_target_pairs={{8,0},{10,2},{16,8},{18,10},{24,16},{26,18},{28,24},{30,26},{20,28... | collective-permute-start | bytes 786440 | tf_op jit(solution)/shard_map/ppermute | solution.py:333
  338.4 25.0 %collective-permute-start.69 = (bf16[1024,512]{1,0:T(8,128)(2,1)S(1)}, bf16[1024,512]{1,0:T(8,128)(2,1)}, u32[]{:S(2)}, u32[]{:S(2)}) collective-permute-start(bf16[1024,512]{1,0:T(8,128)(2,1)S(1)} %get-tuple-element.277), channel_id=1, source_target_pairs={{0,1},{1,0},{2,3},{3,2},{4,5},{5,4},{6,7},{7,6},{8,9},{9,8},{10,11... | collective-permute-start | bytes 3145736 | tf_op jit(solution)/shard_map/ppermute | solution.py:78
  339.3 4.3 collective-permute-start.74
  345.2 6.5 %collective-permute-start.77 = (bf16[4,128,128]{2,1,0:T(8,128)(2,1)S(1)}, bf16[4,128,128]{2,1,0:T(8,128)(2,1)S(1)}, u32[]{:S(2)}, u32[]{:S(2)}) collective-permute-start(bf16[4,128,128]{2,1,0:T(8,128)(2,1)S(1)} %maximum_select_fusion.8), channel_id=1, source_target_pairs={{0,8},{2,10},{4,12},{6,14},{8,0},{10,2},{12,4},{14,6},{16,24},{18,... | collective-permute-start | bytes 393224 | tf_op jit(solution)/shard_map/ppermute | solution.py:98
  346.5 7.2 %collective-permute-start.75 = (bf16[256,512]{1,0:T(8,128)(2,1)S(1)}, bf16[256,512]{1,0:T(8,128)(2,1)S(1)}, u32[]{:S(2)}, u32[]{:S(2)}) collective-permute-start(bf16[256,512]{1,0:T(8,128)(2,1)S(1)} %get-tuple-element.296), channel_id=1, source_target_pairs={{0,8},{2,10},{8,16},{10,18},{16,24},{18,26},{24,28},{26,30},{28,20... | collective-permute-start | bytes 786440 | tf_op jit(solution)/shard_map/ppermute | solution.py:329
  347.3 8.1 %collective-permute-start.76 = (bf16[256,512]{1,0:T(8,128)(2,1)S(1)}, bf16[256,512]{1,0:T(8,128)(2,1)S(1)}, u32[]{:S(2)}, u32[]{:S(2)}) collective-permute-start(bf16[256,512]{1,0:T(8,128)(2,1)S(1)} %get-tuple-element.297), channel_id=1, source_target_pairs={{8,0},{10,2},{16,8},{18,10},{24,16},{26,18},{28,24},{30,26},{20,28... | collective-permute-start | bytes 786440 | tf_op jit(solution)/shard_map/ppermute | solution.py:333
  357.6 26.9 %collective-permute-start.78 = (bf16[256,512]{1,0:T(8,128)(2,1)}, bf16[256,512]{1,0:T(8,128)(2,1)S(1)}, u32[]{:S(2)}, u32[]{:S(2)}) collective-permute-start(bf16[256,512]{1,0:T(8,128)(2,1)} %get-tuple-element.300), channel_id=1, source_target_pairs={{0,8},{2,10},{8,16},{10,18},{16,24},{18,26},{24,28},{26,30},{28,20... | collective-permute-start | bytes 786440 | tf_op jit(solution)/shard_map/ppermute | solution.py:329
  358.3 26.1 %collective-permute-start.80 = (bf16[8,128,128]{2,1,0:T(8,128)(2,1)S(1)}, bf16[8,128,128]{2,1,0:T(8,128)(2,1)S(1)}, u32[]{:S(2)}, u32[]{:S(2)}) collective-permute-start(bf16[8,128,128]{2,1,0:T(8,128)(2,1)S(1)} %maximum_select_fusion.6), channel_id=1, source_target_pairs={{0,16},{2,18},{4,20},{6,22},{8,24},{10,26},{12,28},{14,30},{16,0},... | collective-permute-start | bytes 786440 | tf_op jit(solution)/shard_map/ppermute | solution.py:98
  366.6 33.5 %copy-start.86 = (s32[16]{0:T(128)S(1)}, s32[16]{0:T(128)}, u32[]{:S(2)}) copy-start(s32[16]{0:T(128)} %get-tuple-element.365.use_ref) | copy-start | bytes 196
  366.6 63.9 %collective-permute-start.86 = (bf16[256,1024]{1,0:T(8,128)(2,1)}, bf16[256,1024]{1,0:T(8,128)(2,1)}, u32[]{:S(2)}, u32[]{:S(2)}) collective-permute-start(bf16[256,1024]{1,0:T(8,128)(2,1)} %reduce-scatter.2.cloned.1.call-done), channel_id=1, source_target_pairs={{0,16},{2,18},{4,20},{6,22},{8,24},{10,26},{12,28},{14,30},{16,0},... | collective-permute-start | bytes 1572872 | tf_op jit(solution)/shard_map/ppermute | solution.py:223
  368.1 62.5 %collective-permute-start.85 = (bf16[256,1024]{1,0:T(8,128)(2,1)}, bf16[256,1024]{1,0:T(8,128)(2,1)}, u32[]{:S(2)}, u32[]{:S(2)}) collective-permute-start(bf16[256,1024]{1,0:T(8,128)(2,1)} %reduce-scatter.2.cloned.1.call-done), channel_id=1, source_target_pairs={{0,8},{2,10},{4,12},{6,14},{8,0},{10,2},{12,4},{14,6},{16,24},{18,... | collective-permute-start | bytes 1572872 | tf_op jit(solution)/shard_map/ppermute | solution.py:223
  368.6 31.3 %collective-permute-start.79 = (bf16[256,512]{1,0:T(8,128)(2,1)S(1)}, bf16[256,512]{1,0:T(8,128)(2,1)S(1)}, u32[]{:S(2)}, u32[]{:S(2)}) collective-permute-start(bf16[256,512]{1,0:T(8,128)(2,1)S(1)} %copy-done.108), channel_id=1, source_target_pairs={{8,0},{10,2},{16,8},{18,10},{24,16},{26,18},{28,24},{30,26},{20,28... | collective-permute-start | bytes 786440 | tf_op jit(solution)/shard_map/ppermute | solution.py:333
  399.8 19.1 %collective-permute-start.82 = (bf16[256,512]{1,0:T(8,128)(2,1)S(1)}, bf16[256,512]{1,0:T(8,128)(2,1)S(1)}, u32[]{:S(2)}, u32[]{:S(2)}) collective-permute-start(bf16[256,512]{1,0:T(8,128)(2,1)S(1)} %fusion.22), channel_id=1, source_target_pairs={{0,8},{2,10},{8,16},{10,18},{16,24},{18,26},{24,28},{26,30},{28,20... | collective-permute-start | bytes 786440 | tf_op jit(solution)/shard_map/ppermute | solution.py:329
  409.6 3.7 collective-permute-start.81
  411.0 2.3 collective-permute-start.83
  413.3 5.6 %collective-permute-start.84 = (f32[34,512]{1,0:T(8,128)S(1)}, f32[34,512]{1,0:T(8,128)S(1)}, u32[]{:S(2)}, u32[]{:S(2)}) collective-permute-start(f32[34,512]{1,0:T(8,128)S(1)} %fusion.48), channel_id=1, source_target_pairs={{0,4},{2,6},{4,0},{6,2},{8,12},{10,14},{12,8},{14,10},{16,20},{18,... | collective-permute-start | bytes 208904 | tf_op jit(solution)/shard_map/ppermute | solution.py:112
  421.0 9.3 %collective-permute-start.18 = (bf16[256,512]{1,0:T(8,128)(2,1)S(1)}, bf16[256,512]{1,0:T(8,128)(2,1)}, u32[]{:S(2)}, u32[]{:S(2)}) collective-permute-start(bf16[256,512]{1,0:T(8,128)(2,1)S(1)} %param.18), channel_id=1, source_target_pairs={{8,0},{10,2},{12,4},{14,6},{9,1},{11,3},{13,5},{15,7}} | collective-permute-start | bytes 786440 | tf_op jit(solution)/shard_map/cond/branch_0_fun/ppermute | solution.py:214
  431.7 9.3 %collective-permute-start.87 = (f32[34,512]{1,0:T(8,128)S(1)}, f32[34,512]{1,0:T(8,128)S(1)}, u32[]{:S(2)}, u32[]{:S(2)}) collective-permute-start(f32[34,512]{1,0:T(8,128)S(1)} %add.451), channel_id=1, source_target_pairs={{0,8},{2,10},{4,12},{6,14},{8,0},{10,2},{12,4},{14,6},{16,24},{18,... | collective-permute-start | bytes 208904 | tf_op jit(solution)/shard_map/ppermute | solution.py:112
  441.0 5.4 %collective-permute-start.88 = (f32[34,512]{1,0:T(8,128)S(1)}, f32[34,512]{1,0:T(8,128)S(1)}, u32[]{:S(2)}, u32[]{:S(2)}) collective-permute-start(f32[34,512]{1,0:T(8,128)S(1)} %add.457), channel_id=1, source_target_pairs={{0,16},{2,18},{4,20},{6,22},{8,24},{10,26},{12,28},{14,30},{16,0},... | collective-permute-start | bytes 208904 | tf_op jit(solution)/shard_map/ppermute | solution.py:112
  (118 other events, 718.8 us)
Sparse Core Ops, SparseCore 0:
  106.7 79.8 all-gather.1
  243.7 104.9 reduce-scatter.1
